TPU v7x, 512 devices: a whole 4x8x8 slice. The times are simulated.
512 devices in a mesh: group: 32 (over z_hi, x, core), loop: 16 (over y, z_lo).
Axes of the slice: x: 4, y: 8, z: 8 (z_hi: 4, z_lo: 2; z = z_hi * 2 + z_lo), core: 2. Of those that a mesh axis runs over, the one named last changes fastest.
Arguments:
- image_embed: bfloat16 [12288, 1152], P(('group', 'loop')), may hold values from -6 to 6
- text_embed: bfloat16 [12288, 1152], P(('group', 'loop')), may hold values from -6 to 6
- logit_scale: float32 [1], replicated, may hold values from 0.02 to 0.05
- logit_bias: float32 [1], replicated, may hold values from -4 to -1
Outputs:
- image_grad: float32 [12288, 1152], P(('group', 'loop'))
- text_grad: float32 [12288, 1152], P(('group', 'loop'))
All inputs are finite; a program needn't handle non-finite values.
Results may differ from a plain program's by a relative error of at most 0.0013.
Values may be sent and summed in bfloat16 or wider, within the bound.
No kernel may reach another device: no remote copies, remote signals or barrier semaphores. Data moves between devices by JAX's collectives and lax.ppermute only.
A program may use at most 64 MiB of HBM per device.

v0:
```python
import jax
import jax.numpy as jnp
from jax import lax
from jax.sharding import PartitionSpec as P


def from_behind(array, axis, by):
    length = lax.axis_size(axis)
    return lax.ppermute(array, axis, [(i, (i + by) % length) for i in range(length)])


def local(image_embed, text_embed, logit_scale, logit_bias):
    scale_value = logit_scale[0]
    bias_value = logit_bias[0]
    row_count = text_embed.shape[0]
    feature_count = text_embed.shape[1]
    loop_count = lax.axis_size("loop")
    group_index = lax.axis_index("group")
    loop_index = lax.axis_index("loop")
    gathered = lax.all_gather(image_embed, "group", axis=0, tiled=True)
    image_count = gathered.shape[0]
    positions = jnp.arange(image_count, dtype=jnp.int32)
    image_glob = (
        positions // row_count * loop_count + loop_index
    ) * row_count + positions % row_count

    def score_tile(text_block, text_glob):
        products = lax.dot_general(
            text_block, gathered, (((1,), (1,)), ((), ())), preferred_element_type=jnp.float32
        )
        logits = scale_value * products + bias_value
        labels = jnp.where(
            text_glob[:, None] == image_glob[None, :], jnp.float32(1.0), jnp.float32(-1.0)
        )
        weight = (-labels * scale_value * jax.nn.sigmoid(-labels * logits)).astype(jnp.bfloat16)
        return (weight, jnp.dot(weight, gathered, preferred_element_type=jnp.float32))

    def text_rows_of(source, offset, amount):
        return (
            (group_index * loop_count + source) * row_count
            + offset
            + jnp.arange(amount, dtype=jnp.int32)
        )

    weight_store = jnp.zeros((loop_count, row_count, image_count), jnp.bfloat16)
    text_store = jnp.zeros((loop_count, row_count, feature_count), jnp.bfloat16)

    def visit_block(step_index, cycle_state):
        text_block, accumulator, kept_weight, kept_text = cycle_state
        source = (loop_index - step_index) % loop_count
        weight, text_add = score_tile(text_block, text_rows_of(source, 0, row_count))
        kept_weight = lax.dynamic_update_slice_in_dim(kept_weight, weight[None], step_index, 0)
        kept_text = lax.dynamic_update_slice_in_dim(kept_text, text_block[None], step_index, 0)
        return (text_block, accumulator + text_add, kept_weight, kept_text)

    def travel_step(step_index, cycle_state):
        cycle_state = visit_block(step_index, cycle_state)
        text_block, accumulator = (
            from_behind(cycle_state[0].astype(jnp.float32), "loop", 1).astype(jnp.bfloat16),
            from_behind(cycle_state[1], "loop", 1),
        )
        return (text_block, accumulator, cycle_state[2], cycle_state[3])

    initial = (
        text_embed,
        jnp.zeros((row_count, feature_count), jnp.float32),
        weight_store,
        text_store,
    )
    cycle_state = lax.fori_loop(0, loop_count - 1, travel_step, initial)
    cycle_state = visit_block(loop_count - 1, cycle_state)
    text_out = from_behind(cycle_state[1], "loop", 1)
    kept_weight, kept_text = (cycle_state[2], cycle_state[3])
    kept_weight = kept_weight.reshape(loop_count * row_count, image_count)
    kept_text = kept_text.reshape(loop_count * row_count, feature_count)
    partial_value = lax.dot_general(
        kept_weight, kept_text, (((0,), (0,)), ((), ())), preferred_element_type=jnp.float32
    )
    image_out = lax.psum_scatter(partial_value, "group", scatter_dimension=0, tiled=True)
    return (image_out, text_out)


def solution(mesh):
    in_specs = (P(("group", "loop"), None), P(("group", "loop"), None), P(), P())
    out_specs = (P(("group", "loop"), None), P(("group", "loop"), None))
    return jax.shard_map(local, mesh=mesh, in_specs=in_specs, out_specs=out_specs, check_vma=False)
```

profile of v0, /device:TPU:1, one launch (start us, length us, event | category | flops | bytes accessed | tf_op | source)
XLA Modules:
  0.0 425.1 jit_solution(5147705579002334134)
XLA Ops:
  9.3 67.4 %all-gather.2.cloned.1.call-done = bf16[768,1152]{1,0:T(8,128)(2,1)} async-done(((bf16[24,1152]{1,0:T(8,128)(2,1)}), bf16[768,1152]{1,0:T(8,128)(2,1)}) %all-gather.2.cloned.1.call-update) | async-done | bytes 1769488 | tf_op jit(solution)/shard_map/all_gather | solution.py:20
  77.7 215.8 %while.23 = (s32[]{:T(128)}, bf16[24,1152]{1,0:T(8,128)(2,1)S(1)}, f32[24,1152]{1,0:T(8,128)S(1)}, bf16[16,24,768]{2,1,0:T(8,128)(2,1)}, bf16[16,24,1152]{2,1,0:...) while((s32[]{:T(128)}, bf16[24,1152]{1,0:T(8,128)(2,1)S(1)}, ...), condition=%wide.region_1.2_spmd.clone.clone, body=%wide.region_0.1_spmd.clone.clone.sunk | while | flops 85195816 | bytes 11896918 | solution.py:70
  79.8 4.1 bitcast_dynamic-update-slice_fusion.6
  84.2 4.3 %collective-permute-start.1 = (f32[24,1152]{1,0:T(8,128)S(1)}, f32[24,1152]{1,0:T(8,128)S(1)}, u32[]{:S(2)}, u32[]{:S(2)}) collective-permute-start(f32[24,1152]{1,0:T(8,128)S(1)} %convolution_add_fusion.3), channel_id=1, source_target_pairs={{0,1},{1,2},{2,3},{3,4},{4,5},{5,6},{6,7},{7,8},{8,9},{9,10},{10,1... | collective-permute-start | bytes 331784 | tf_op jit(solution)/shard_map/while/body/eval_jaxpr/ppermute | solution.py:9
  94.7 4.1 bitcast_dynamic-update-slice_fusion.6
  102.3 4.4 %collective-permute-done.1 = f32[24,1152]{1,0:T(8,128)S(1)} collective-permute-done((f32[24,1152]{1,0:T(8,128)S(1)}, f32[24,1152]{1,0:T(8,128)S(1)}, u32[]{:S(2)}, u32[]{:S(2)}) %collective-permute-start.1) | collective-permute-done | bytes 110624 | tf_op jit(solution)/shard_map/while/body/eval_jaxpr/ppermute | solution.py:9
  116.4 4.5 %collective-permute-done.1 = f32[24,1152]{1,0:T(8,128)S(1)} collective-permute-done((f32[24,1152]{1,0:T(8,128)S(1)}, f32[24,1152]{1,0:T(8,128)S(1)}, u32[]{:S(2)}, u32[]{:S(2)}) %collective-permute-start.1) | collective-permute-done | bytes 110624 | tf_op jit(solution)/shard_map/while/body/eval_jaxpr/ppermute | solution.py:9
  123.0 4.1 bitcast_dynamic-update-slice_fusion.6
  129.7 5.4 %collective-permute-done.1 = f32[24,1152]{1,0:T(8,128)S(1)} collective-permute-done((f32[24,1152]{1,0:T(8,128)S(1)}, f32[24,1152]{1,0:T(8,128)S(1)}, u32[]{:S(2)}, u32[]{:S(2)}) %collective-permute-start.1) | collective-permute-done | bytes 110624 | tf_op jit(solution)/shard_map/while/body/eval_jaxpr/ppermute | solution.py:9
  137.2 4.1 bitcast_dynamic-update-slice_fusion.6
  143.8 5.4 %collective-permute-done.1 = f32[24,1152]{1,0:T(8,128)S(1)} collective-permute-done((f32[24,1152]{1,0:T(8,128)S(1)}, f32[24,1152]{1,0:T(8,128)S(1)}, u32[]{:S(2)}, u32[]{:S(2)}) %collective-permute-start.1) | collective-permute-done | bytes 110624 | tf_op jit(solution)/shard_map/while/body/eval_jaxpr/ppermute | solution.py:9
  151.3 4.1 bitcast_dynamic-update-slice_fusion.6
  157.7 6.2 %collective-permute-done.1 = f32[24,1152]{1,0:T(8,128)S(1)} collective-permute-done((f32[24,1152]{1,0:T(8,128)S(1)}, f32[24,1152]{1,0:T(8,128)S(1)}, u32[]{:S(2)}, u32[]{:S(2)}) %collective-permute-start.1) | collective-permute-done | bytes 110624 | tf_op jit(solution)/shard_map/while/body/eval_jaxpr/ppermute | solution.py:9
  172.8 6.0 %collective-permute-done.1 = f32[24,1152]{1,0:T(8,128)S(1)} collective-permute-done((f32[24,1152]{1,0:T(8,128)S(1)}, f32[24,1152]{1,0:T(8,128)S(1)}, u32[]{:S(2)}, u32[]{:S(2)}) %collective-permute-start.1) | collective-permute-done | bytes 110624 | tf_op jit(solution)/shard_map/while/body/eval_jaxpr/ppermute | solution.py:9
  180.9 4.1 bitcast_dynamic-update-slice_fusion.6
  187.3 5.6 %collective-permute-done.1 = f32[24,1152]{1,0:T(8,128)S(1)} collective-permute-done((f32[24,1152]{1,0:T(8,128)S(1)}, f32[24,1152]{1,0:T(8,128)S(1)}, u32[]{:S(2)}, u32[]{:S(2)}) %collective-permute-start.1) | collective-permute-done | bytes 110624 | tf_op jit(solution)/shard_map/while/body/eval_jaxpr/ppermute | solution.py:9
  195.0 4.1 bitcast_dynamic-update-slice_fusion.6
  202.2 4.8 %collective-permute-done.1 = f32[24,1152]{1,0:T(8,128)S(1)} collective-permute-done((f32[24,1152]{1,0:T(8,128)S(1)}, f32[24,1152]{1,0:T(8,128)S(1)}, u32[]{:S(2)}, u32[]{:S(2)}) %collective-permute-start.1) | collective-permute-done | bytes 110624 | tf_op jit(solution)/shard_map/while/body/eval_jaxpr/ppermute | solution.py:9
  209.2 4.1 bitcast_dynamic-update-slice_fusion.6
  215.5 5.6 %collective-permute-done.1 = f32[24,1152]{1,0:T(8,128)S(1)} collective-permute-done((f32[24,1152]{1,0:T(8,128)S(1)}, f32[24,1152]{1,0:T(8,128)S(1)}, u32[]{:S(2)}, u32[]{:S(2)}) %collective-permute-start.1) | collective-permute-done | bytes 110624 | tf_op jit(solution)/shard_map/while/body/eval_jaxpr/ppermute | solution.py:9
  223.3 4.1 bitcast_dynamic-update-slice_fusion.6
  230.1 5.2 %collective-permute-done.1 = f32[24,1152]{1,0:T(8,128)S(1)} collective-permute-done((f32[24,1152]{1,0:T(8,128)S(1)}, f32[24,1152]{1,0:T(8,128)S(1)}, u32[]{:S(2)}, u32[]{:S(2)}) %collective-permute-start.1) | collective-permute-done | bytes 110624 | tf_op jit(solution)/shard_map/while/body/eval_jaxpr/ppermute | solution.py:9
  237.5 4.1 bitcast_dynamic-update-slice_fusion.6
  244.9 4.6 %collective-permute-done.1 = f32[24,1152]{1,0:T(8,128)S(1)} collective-permute-done((f32[24,1152]{1,0:T(8,128)S(1)}, f32[24,1152]{1,0:T(8,128)S(1)}, u32[]{:S(2)}, u32[]{:S(2)}) %collective-permute-start.1) | collective-permute-done | bytes 110624 | tf_op jit(solution)/shard_map/while/body/eval_jaxpr/ppermute | solution.py:9
  251.6 4.1 bitcast_dynamic-update-slice_fusion.6
  258.2 5.9 %collective-permute-done.1 = f32[24,1152]{1,0:T(8,128)S(1)} collective-permute-done((f32[24,1152]{1,0:T(8,128)S(1)}, f32[24,1152]{1,0:T(8,128)S(1)}, u32[]{:S(2)}, u32[]{:S(2)}) %collective-permute-start.1) | collective-permute-done | bytes 110624 | tf_op jit(solution)/shard_map/while/body/eval_jaxpr/ppermute | solution.py:9
  266.3 4.1 bitcast_dynamic-update-slice_fusion.6
  273.4 5.9 %collective-permute-done.1 = f32[24,1152]{1,0:T(8,128)S(1)} collective-permute-done((f32[24,1152]{1,0:T(8,128)S(1)}, f32[24,1152]{1,0:T(8,128)S(1)}, u32[]{:S(2)}, u32[]{:S(2)}) %collective-permute-start.1) | collective-permute-done | bytes 110624 | tf_op jit(solution)/shard_map/while/body/eval_jaxpr/ppermute | solution.py:9
  281.4 4.1 bitcast_dynamic-update-slice_fusion.6
  288.8 4.7 %collective-permute-done.1 = f32[24,1152]{1,0:T(8,128)S(1)} collective-permute-done((f32[24,1152]{1,0:T(8,128)S(1)}, f32[24,1152]{1,0:T(8,128)S(1)}, u32[]{:S(2)}, u32[]{:S(2)}) %collective-permute-start.1) | collective-permute-done | bytes 110624 | tf_op jit(solution)/shard_map/while/body/eval_jaxpr/ppermute | solution.py:9
  304.0 6.8 %collective-permute-done.2 = f32[24,1152]{1,0:T(8,128)S(1)} collective-permute-done((f32[24,1152]{1,0:T(8,128)S(1)}, f32[24,1152]{1,0:T(8,128)S(1)}, u32[]{:S(2)}, u32[]{:S(2)}) %collective-permute-start.2) | collective-permute-done | bytes 110624 | tf_op jit(solution)/shard_map/ppermute | solution.py:9
  310.8 106.8 %reduce-scatter.4.cloned.1.call-done = f32[24,1152]{1,0:T(8,128)} async-done(((f32[768,1152]{1,0:T(8,128)}), f32[24,1152]{1,0:T(8,128)}) %reduce-scatter.4.cloned.1.call-update) | async-done | bytes 110608
  (171 shorter events, 96.1 us)
Async XLA Ops:
  7.2 69.5 %all-gather.2.cloned.1.call-start = ((), (), s32[]{:S(2)}) async-start(), calls=%async_computation.1 | async-start | bytes 1824768 | tf_op jit(solution)/shard_map/all_gather | solution.py:20
  7.9 409.7 %reduce-scatter.4.cloned.1.call-start = ((), (), s32[]{:S(2)}) async-start(), calls=%async_computation.2 | async-start | bytes 3649536
  77.7 10.9 %collective-permute-start = (bf16[24,1152]{1,0:T(8,128)(2,1)S(1)}, bf16[24,1152]{1,0:T(8,128)(2,1)S(1)}, u32[]{:S(2)}, u32[]{:S(2)}) collective-permute-start(bf16[24,1152]{1,0:T(8,128)(2,1)S(1)} %copy.14), channel_id=1, source_target_pairs={{0,1},{1,2},{2,3},{3,4},{4,5},{5,6},{6,7},{7,8},{8,9},{9,10},{10,1... | collective-permute-start | bytes 165896 | tf_op jit(solution)/shard_map/while/body/eval_jaxpr/ppermute | solution.py:9
  84.2 8.2 %collective-permute-start.1 = (f32[24,1152]{1,0:T(8,128)S(1)}, f32[24,1152]{1,0:T(8,128)S(1)}, u32[]{:S(2)}, u32[]{:S(2)}) collective-permute-start(f32[24,1152]{1,0:T(8,128)S(1)} %convolution_add_fusion.3), channel_id=1, source_target_pairs={{0,1},{1,2},{2,3},{3,4},{4,5},{5,6},{6,7},{7,8},{8,9},{9,10},{10,1... | collective-permute-start | bytes 331784 | tf_op jit(solution)/shard_map/while/body/eval_jaxpr/ppermute | solution.py:9
  92.5 9.9 %collective-permute-start = (bf16[24,1152]{1,0:T(8,128)(2,1)S(1)}, bf16[24,1152]{1,0:T(8,128)(2,1)S(1)}, u32[]{:S(2)}, u32[]{:S(2)}) collective-permute-start(bf16[24,1152]{1,0:T(8,128)(2,1)S(1)} %copy.14), channel_id=1, source_target_pairs={{0,1},{1,2},{2,3},{3,4},{4,5},{5,6},{6,7},{7,8},{8,9},{9,10},{10,1... | collective-permute-start | bytes 165896 | tf_op jit(solution)/shard_map/while/body/eval_jaxpr/ppermute | solution.py:9
  99.2 7.6 %collective-permute-start.1 = (f32[24,1152]{1,0:T(8,128)S(1)}, f32[24,1152]{1,0:T(8,128)S(1)}, u32[]{:S(2)}, u32[]{:S(2)}) collective-permute-start(f32[24,1152]{1,0:T(8,128)S(1)} %convolution_add_fusion.3), channel_id=1, source_target_pairs={{0,1},{1,2},{2,3},{3,4},{4,5},{5,6},{6,7},{7,8},{8,9},{9,10},{10,1... | collective-permute-start | bytes 331784 | tf_op jit(solution)/shard_map/while/body/eval_jaxpr/ppermute | solution.py:9
  106.8 9.6 %collective-permute-start = (bf16[24,1152]{1,0:T(8,128)(2,1)S(1)}, bf16[24,1152]{1,0:T(8,128)(2,1)S(1)}, u32[]{:S(2)}, u32[]{:S(2)}) collective-permute-start(bf16[24,1152]{1,0:T(8,128)(2,1)S(1)} %copy.14), channel_id=1, source_target_pairs={{0,1},{1,2},{2,3},{3,4},{4,5},{5,6},{6,7},{7,8},{8,9},{9,10},{10,1... | collective-permute-start | bytes 165896 | tf_op jit(solution)/shard_map/while/body/eval_jaxpr/ppermute | solution.py:9
  113.3 7.6 %collective-permute-start.1 = (f32[24,1152]{1,0:T(8,128)S(1)}, f32[24,1152]{1,0:T(8,128)S(1)}, u32[]{:S(2)}, u32[]{:S(2)}) collective-permute-start(f32[24,1152]{1,0:T(8,128)S(1)} %convolution_add_fusion.3), channel_id=1, source_target_pairs={{0,1},{1,2},{2,3},{3,4},{4,5},{5,6},{6,7},{7,8},{8,9},{9,10},{10,1... | collective-permute-start | bytes 331784 | tf_op jit(solution)/shard_map/while/body/eval_jaxpr/ppermute | solution.py:9
  120.9 8.8 %collective-permute-start = (bf16[24,1152]{1,0:T(8,128)(2,1)S(1)}, bf16[24,1152]{1,0:T(8,128)(2,1)S(1)}, u32[]{:S(2)}, u32[]{:S(2)}) collective-permute-start(bf16[24,1152]{1,0:T(8,128)(2,1)S(1)} %copy.14), channel_id=1, source_target_pairs={{0,1},{1,2},{2,3},{3,4},{4,5},{5,6},{6,7},{7,8},{8,9},{9,10},{10,1... | collective-permute-start | bytes 165896 | tf_op jit(solution)/shard_map/while/body/eval_jaxpr/ppermute | solution.py:9
  127.4 7.6 %collective-permute-start.1 = (f32[24,1152]{1,0:T(8,128)S(1)}, f32[24,1152]{1,0:T(8,128)S(1)}, u32[]{:S(2)}, u32[]{:S(2)}) collective-permute-start(f32[24,1152]{1,0:T(8,128)S(1)} %convolution_add_fusion.3), channel_id=1, source_target_pairs={{0,1},{1,2},{2,3},{3,4},{4,5},{5,6},{6,7},{7,8},{8,9},{9,10},{10,1... | collective-permute-start | bytes 331784 | tf_op jit(solution)/shard_map/while/body/eval_jaxpr/ppermute | solution.py:9
  135.1 8.7 %collective-permute-start = (bf16[24,1152]{1,0:T(8,128)(2,1)S(1)}, bf16[24,1152]{1,0:T(8,128)(2,1)S(1)}, u32[]{:S(2)}, u32[]{:S(2)}) collective-permute-start(bf16[24,1152]{1,0:T(8,128)(2,1)S(1)} %copy.14), channel_id=1, source_target_pairs={{0,1},{1,2},{2,3},{3,4},{4,5},{5,6},{6,7},{7,8},{8,9},{9,10},{10,1... | collective-permute-start | bytes 165896 | tf_op jit(solution)/shard_map/while/body/eval_jaxpr/ppermute | solution.py:9
  141.6 7.6 %collective-permute-start.1 = (f32[24,1152]{1,0:T(8,128)S(1)}, f32[24,1152]{1,0:T(8,128)S(1)}, u32[]{:S(2)}, u32[]{:S(2)}) collective-permute-start(f32[24,1152]{1,0:T(8,128)S(1)} %convolution_add_fusion.3), channel_id=1, source_target_pairs={{0,1},{1,2},{2,3},{3,4},{4,5},{5,6},{6,7},{7,8},{8,9},{9,10},{10,1... | collective-permute-start | bytes 331784 | tf_op jit(solution)/shard_map/while/body/eval_jaxpr/ppermute | solution.py:9
  149.2 8.5 %collective-permute-start = (bf16[24,1152]{1,0:T(8,128)(2,1)S(1)}, bf16[24,1152]{1,0:T(8,128)(2,1)S(1)}, u32[]{:S(2)}, u32[]{:S(2)}) collective-permute-start(bf16[24,1152]{1,0:T(8,128)(2,1)S(1)} %copy.14), channel_id=1, source_target_pairs={{0,1},{1,2},{2,3},{3,4},{4,5},{5,6},{6,7},{7,8},{8,9},{9,10},{10,1... | collective-permute-start | bytes 165896 | tf_op jit(solution)/shard_map/while/body/eval_jaxpr/ppermute | solution.py:9
  155.7 8.2 %collective-permute-start.1 = (f32[24,1152]{1,0:T(8,128)S(1)}, f32[24,1152]{1,0:T(8,128)S(1)}, u32[]{:S(2)}, u32[]{:S(2)}) collective-permute-start(f32[24,1152]{1,0:T(8,128)S(1)} %convolution_add_fusion.3), channel_id=1, source_target_pairs={{0,1},{1,2},{2,3},{3,4},{4,5},{5,6},{6,7},{7,8},{8,9},{9,10},{10,1... | collective-permute-start | bytes 331784 | tf_op jit(solution)/shard_map/while/body/eval_jaxpr/ppermute | solution.py:9
  164.0 8.8 %collective-permute-start = (bf16[24,1152]{1,0:T(8,128)(2,1)S(1)}, bf16[24,1152]{1,0:T(8,128)(2,1)S(1)}, u32[]{:S(2)}, u32[]{:S(2)}) collective-permute-start(bf16[24,1152]{1,0:T(8,128)(2,1)S(1)} %copy.14), channel_id=1, source_target_pairs={{0,1},{1,2},{2,3},{3,4},{4,5},{5,6},{6,7},{7,8},{8,9},{9,10},{10,1... | collective-permute-start | bytes 165896 | tf_op jit(solution)/shard_map/while/body/eval_jaxpr/ppermute | solution.py:9
  170.5 8.2 %collective-permute-start.1 = (f32[24,1152]{1,0:T(8,128)S(1)}, f32[24,1152]{1,0:T(8,128)S(1)}, u32[]{:S(2)}, u32[]{:S(2)}) collective-permute-start(f32[24,1152]{1,0:T(8,128)S(1)} %convolution_add_fusion.3), channel_id=1, source_target_pairs={{0,1},{1,2},{2,3},{3,4},{4,5},{5,6},{6,7},{7,8},{8,9},{9,10},{10,1... | collective-permute-start | bytes 331784 | tf_op jit(solution)/shard_map/while/body/eval_jaxpr/ppermute | solution.py:9
  178.7 8.6 %collective-permute-start = (bf16[24,1152]{1,0:T(8,128)(2,1)S(1)}, bf16[24,1152]{1,0:T(8,128)(2,1)S(1)}, u32[]{:S(2)}, u32[]{:S(2)}) collective-permute-start(bf16[24,1152]{1,0:T(8,128)(2,1)S(1)} %copy.14), channel_id=1, source_target_pairs={{0,1},{1,2},{2,3},{3,4},{4,5},{5,6},{6,7},{7,8},{8,9},{9,10},{10,1... | collective-permute-start | bytes 165896 | tf_op jit(solution)/shard_map/while/body/eval_jaxpr/ppermute | solution.py:9
  185.3 7.6 %collective-permute-start.1 = (f32[24,1152]{1,0:T(8,128)S(1)}, f32[24,1152]{1,0:T(8,128)S(1)}, u32[]{:S(2)}, u32[]{:S(2)}) collective-permute-start(f32[24,1152]{1,0:T(8,128)S(1)} %convolution_add_fusion.3), channel_id=1, source_target_pairs={{0,1},{1,2},{2,3},{3,4},{4,5},{5,6},{6,7},{7,8},{8,9},{9,10},{10,1... | collective-permute-start | bytes 331784 | tf_op jit(solution)/shard_map/while/body/eval_jaxpr/ppermute | solution.py:9
  192.9 9.3 %collective-permute-start = (bf16[24,1152]{1,0:T(8,128)(2,1)S(1)}, bf16[24,1152]{1,0:T(8,128)(2,1)S(1)}, u32[]{:S(2)}, u32[]{:S(2)}) collective-permute-start(bf16[24,1152]{1,0:T(8,128)(2,1)S(1)} %copy.14), channel_id=1, source_target_pairs={{0,1},{1,2},{2,3},{3,4},{4,5},{5,6},{6,7},{7,8},{8,9},{9,10},{10,1... | collective-permute-start | bytes 165896 | tf_op jit(solution)/shard_map/while/body/eval_jaxpr/ppermute | solution.py:9
  199.4 7.6 %collective-permute-start.1 = (f32[24,1152]{1,0:T(8,128)S(1)}, f32[24,1152]{1,0:T(8,128)S(1)}, u32[]{:S(2)}, u32[]{:S(2)}) collective-permute-start(f32[24,1152]{1,0:T(8,128)S(1)} %convolution_add_fusion.3), channel_id=1, source_target_pairs={{0,1},{1,2},{2,3},{3,4},{4,5},{5,6},{6,7},{7,8},{8,9},{9,10},{10,1... | collective-permute-start | bytes 331784 | tf_op jit(solution)/shard_map/while/body/eval_jaxpr/ppermute | solution.py:9
  207.0 8.5 %collective-permute-start = (bf16[24,1152]{1,0:T(8,128)(2,1)S(1)}, bf16[24,1152]{1,0:T(8,128)(2,1)S(1)}, u32[]{:S(2)}, u32[]{:S(2)}) collective-permute-start(bf16[24,1152]{1,0:T(8,128)(2,1)S(1)} %copy.14), channel_id=1, source_target_pairs={{0,1},{1,2},{2,3},{3,4},{4,5},{5,6},{6,7},{7,8},{8,9},{9,10},{10,1... | collective-permute-start | bytes 165896 | tf_op jit(solution)/shard_map/while/body/eval_jaxpr/ppermute | solution.py:9
  213.6 7.6 %collective-permute-start.1 = (f32[24,1152]{1,0:T(8,128)S(1)}, f32[24,1152]{1,0:T(8,128)S(1)}, u32[]{:S(2)}, u32[]{:S(2)}) collective-permute-start(f32[24,1152]{1,0:T(8,128)S(1)} %convolution_add_fusion.3), channel_id=1, source_target_pairs={{0,1},{1,2},{2,3},{3,4},{4,5},{5,6},{6,7},{7,8},{8,9},{9,10},{10,1... | collective-permute-start | bytes 331784 | tf_op jit(solution)/shard_map/while/body/eval_jaxpr/ppermute | solution.py:9
  221.2 8.9 %collective-permute-start = (bf16[24,1152]{1,0:T(8,128)(2,1)S(1)}, bf16[24,1152]{1,0:T(8,128)(2,1)S(1)}, u32[]{:S(2)}, u32[]{:S(2)}) collective-permute-start(bf16[24,1152]{1,0:T(8,128)(2,1)S(1)} %copy.14), channel_id=1, source_target_pairs={{0,1},{1,2},{2,3},{3,4},{4,5},{5,6},{6,7},{7,8},{8,9},{9,10},{10,1... | collective-permute-start | bytes 165896 | tf_op jit(solution)/shard_map/while/body/eval_jaxpr/ppermute | solution.py:9
  227.7 7.6 %collective-permute-start.1 = (f32[24,1152]{1,0:T(8,128)S(1)}, f32[24,1152]{1,0:T(8,128)S(1)}, u32[]{:S(2)}, u32[]{:S(2)}) collective-permute-start(f32[24,1152]{1,0:T(8,128)S(1)} %convolution_add_fusion.3), channel_id=1, source_target_pairs={{0,1},{1,2},{2,3},{3,4},{4,5},{5,6},{6,7},{7,8},{8,9},{9,10},{10,1... | collective-permute-start | bytes 331784 | tf_op jit(solution)/shard_map/while/body/eval_jaxpr/ppermute | solution.py:9
  235.3 9.6 %collective-permute-start = (bf16[24,1152]{1,0:T(8,128)(2,1)S(1)}, bf16[24,1152]{1,0:T(8,128)(2,1)S(1)}, u32[]{:S(2)}, u32[]{:S(2)}) collective-permute-start(bf16[24,1152]{1,0:T(8,128)(2,1)S(1)} %copy.14), channel_id=1, source_target_pairs={{0,1},{1,2},{2,3},{3,4},{4,5},{5,6},{6,7},{7,8},{8,9},{9,10},{10,1... | collective-permute-start | bytes 165896 | tf_op jit(solution)/shard_map/while/body/eval_jaxpr/ppermute | solution.py:9
  241.9 7.6 %collective-permute-start.1 = (f32[24,1152]{1,0:T(8,128)S(1)}, f32[24,1152]{1,0:T(8,128)S(1)}, u32[]{:S(2)}, u32[]{:S(2)}) collective-permute-start(f32[24,1152]{1,0:T(8,128)S(1)} %convolution_add_fusion.3), channel_id=1, source_target_pairs={{0,1},{1,2},{2,3},{3,4},{4,5},{5,6},{6,7},{7,8},{8,9},{9,10},{10,1... | collective-permute-start | bytes 331784 | tf_op jit(solution)/shard_map/while/body/eval_jaxpr/ppermute | solution.py:9
  249.5 8.7 %collective-permute-start = (bf16[24,1152]{1,0:T(8,128)(2,1)S(1)}, bf16[24,1152]{1,0:T(8,128)(2,1)S(1)}, u32[]{:S(2)}, u32[]{:S(2)}) collective-permute-start(bf16[24,1152]{1,0:T(8,128)(2,1)S(1)} %copy.14), channel_id=1, source_target_pairs={{0,1},{1,2},{2,3},{3,4},{4,5},{5,6},{6,7},{7,8},{8,9},{9,10},{10,1... | collective-permute-start | bytes 165896 | tf_op jit(solution)/shard_map/while/body/eval_jaxpr/ppermute | solution.py:9
  256.0 8.1 %collective-permute-start.1 = (f32[24,1152]{1,0:T(8,128)S(1)}, f32[24,1152]{1,0:T(8,128)S(1)}, u32[]{:S(2)}, u32[]{:S(2)}) collective-permute-start(f32[24,1152]{1,0:T(8,128)S(1)} %convolution_add_fusion.3), channel_id=1, source_target_pairs={{0,1},{1,2},{2,3},{3,4},{4,5},{5,6},{6,7},{7,8},{8,9},{9,10},{10,1... | collective-permute-start | bytes 331784 | tf_op jit(solution)/shard_map/while/body/eval_jaxpr/ppermute | solution.py:9
  264.1 9.2 %collective-permute-start = (bf16[24,1152]{1,0:T(8,128)(2,1)S(1)}, bf16[24,1152]{1,0:T(8,128)(2,1)S(1)}, u32[]{:S(2)}, u32[]{:S(2)}) collective-permute-start(bf16[24,1152]{1,0:T(8,128)(2,1)S(1)} %copy.14), channel_id=1, source_target_pairs={{0,1},{1,2},{2,3},{3,4},{4,5},{5,6},{6,7},{7,8},{8,9},{9,10},{10,1... | collective-permute-start | bytes 165896 | tf_op jit(solution)/shard_map/while/body/eval_jaxpr/ppermute | solution.py:9
  270.7 8.6 %collective-permute-start.1 = (f32[24,1152]{1,0:T(8,128)S(1)}, f32[24,1152]{1,0:T(8,128)S(1)}, u32[]{:S(2)}, u32[]{:S(2)}) collective-permute-start(f32[24,1152]{1,0:T(8,128)S(1)} %convolution_add_fusion.3), channel_id=1, source_target_pairs={{0,1},{1,2},{2,3},{3,4},{4,5},{5,6},{6,7},{7,8},{8,9},{9,10},{10,1... | collective-permute-start | bytes 331784 | tf_op jit(solution)/shard_map/while/body/eval_jaxpr/ppermute | solution.py:9
  279.3 9.4 %collective-permute-start = (bf16[24,1152]{1,0:T(8,128)(2,1)S(1)}, bf16[24,1152]{1,0:T(8,128)(2,1)S(1)}, u32[]{:S(2)}, u32[]{:S(2)}) collective-permute-start(bf16[24,1152]{1,0:T(8,128)(2,1)S(1)} %copy.14), channel_id=1, source_target_pairs={{0,1},{1,2},{2,3},{3,4},{4,5},{5,6},{6,7},{7,8},{8,9},{9,10},{10,1... | collective-permute-start | bytes 165896 | tf_op jit(solution)/shard_map/while/body/eval_jaxpr/ppermute | solution.py:9
  302.1 8.8 %collective-permute-start.2 = (f32[24,1152]{1,0:T(8,128)S(1)}, f32[24,1152]{1,0:T(8,128)S(1)}, u32[]{:S(2)}, u32[]{:S(2)}) collective-permute-start(f32[24,1152]{1,0:T(8,128)S(1)} %convolution_add_fusion.1), channel_id=1, source_target_pairs={{0,1},{1,2},{2,3},{3,4},{4,5},{5,6},{6,7},{7,8},{8,9},{9,10},{10,1... | collective-permute-start | bytes 331784 | tf_op jit(solution)/shard_map/ppermute | solution.py:9
  (18 other events, 172.7 us)
Sparse Core Ops, SparseCore 0:
  11.1 65.5 all-gather.1
  300.4 117.1 reduce-scatter.3
where the time goes:
time: 427 us; the launch traced here: 425 us
  waiting for transfers between devices  260 us (61%)
  matrix products  73.3 us (17%)
  starting transfers between devices  71.6 us (17%)
  between operations  15.4 us (4%)
    unnamed x3, waiting for transfers between devices  107 us
    ppermute x31, waiting for transfers between devices, from_behind(): lax.ppermute(array, axis, [(i, (i + by) % length) for i in range(length)])  85 us
    ppermute x31, starting transfers between devices, from_behind(): lax.ppermute(array, axis, [(i, (i + by) % length) for i in range(length)])  71.5 us
    all_gather x1, waiting for transfers between devices, local(): gathered = lax.all_gather(image_embed, 'group', axis=0, tiled=True)  67.4 us
    dot_general x16, matrix products, score_tile(): lax.dot_general(text_block, gathered, (((1,), (1,)), ((), ())), preferred...  63.7 us
  transfers between devices with their start and end apart: 33, of which 18 were waited for; matrix products, arithmetic and copies ran while one was open for 16% of the time, Pallas kernels for 0%

commit v1 on v0

v1 whole, which is shorter than its diff:
```python
import jax
import jax.numpy as jnp
from jax import lax
from jax.experimental import pallas as pl
from jax.experimental.pallas import tpu as pltpu
from jax.sharding import Mesh, PartitionSpec as P

ROW_AXES = ("z_hi", "x")
LOOP_AXES = ("y", "z_lo")
LANES = 128


def finer_mesh(mesh):
    devices = mesh.devices.reshape(4, 4, 2, 8, 2)
    return Mesh(devices, ("z_hi", "x", "core", "y", "z_lo"))


def weights_of(text, image, scale_value, bias_value, same):
    products = lax.dot_general(
        text, image, (((1,), (1,)), ((), ())), preferred_element_type=jnp.float32
    )
    logits = scale_value * products + bias_value
    if same is None:
        return (scale_value / (1.0 + jnp.exp(-logits))).astype(jnp.bfloat16)
    magnitude = scale_value / (1.0 + jnp.exp(jnp.where(same, logits, -logits)))
    return jnp.where(same, -magnitude, magnitude).astype(jnp.bfloat16)


def pack_into(packed_ref, block, values):
    largest = jnp.max(jnp.abs(values), axis=-1, keepdims=True)
    power = jnp.floor(jnp.log2(jnp.maximum(largest, 2.0**-100)))
    width = values.shape[-1]
    packed_ref[block, :, :width] = values * jnp.exp2(13.0 - power)
    packed_ref[block, :, width:] = jnp.broadcast_to(power, (values.shape[0], LANES))


def own_kernel(place_ref, numbers_ref, text_ref, image_ref, text_part_ref, image_part_ref):
    rows = text_ref.shape[0]
    count = image_ref.shape[0]
    text_at = lax.broadcasted_iota(jnp.int32, (rows, count), 0) - place_ref[0]
    image_at = lax.broadcasted_iota(jnp.int32, (rows, count), 1) - place_ref[1]
    same = (text_at == image_at) & (text_at >= 0) & (text_at < place_ref[2])
    text = text_ref[...]
    image = image_ref[...]
    weight = weights_of(text, image, numbers_ref[0], numbers_ref[1], same)
    text_part_ref[...] = jnp.dot(weight, image, preferred_element_type=jnp.float32)
    image_part_ref[...] = lax.dot_general(
        weight, text, (((0,), (0,)), ((), ())), preferred_element_type=jnp.float32
    )


def other_kernel(
    numbers_ref, text_ref, image_ref, text_before_ref, packed_ref, image_part_ref, total_ref
):
    text = text_ref[...]
    image = image_ref[...]
    weight = weights_of(text, image, numbers_ref[0], numbers_ref[1], None)
    image_part_ref[...] = lax.dot_general(
        weight, text, (((0,), (0,)), ((), ())), preferred_element_type=jnp.float32
    )
    total_ref[...] = text_before_ref[...] + jnp.dot(
        weight, image, preferred_element_type=jnp.float32
    )
    blocks, rows, _ = packed_ref.shape
    for block in range(blocks):
        pack_into(packed_ref, block, total_ref[pl.ds(block * rows, rows), :])


def add_kernel(own_ref, arrived_ref, packed_ref):
    blocks, rows, _ = packed_ref.shape
    for block in range(blocks):
        part = pl.ds(block * rows, rows)
        pack_into(packed_ref, block, own_ref[part, :] + arrived_ref[part, :])


def sum_kernel(packed_ref, out_ref):
    width = out_ref.shape[-1]
    total = jnp.zeros(out_ref.shape, jnp.float32)
    for block in range(packed_ref.shape[0]):
        factor = jnp.exp2(packed_ref[block, :, width:] - 13.0)[:, :1]
        total = total + packed_ref[block, :, :width] * factor
    out_ref[...] = total


def spread(array, axes, count):
    return lax.all_to_all(
        jnp.broadcast_to(array[None], (count, *array.shape)), axes, 0, 0, tiled=True
    )


def exchange(packed, axes):
    arrived = lax.all_to_all(packed.astype(jnp.float16), axes, 0, 0, tiled=True)
    return arrived.astype(jnp.float32)


def local(image_embed, text_embed, logit_scale, logit_bias):
    row_count, feature_count = text_embed.shape
    row_places = lax.axis_size(ROW_AXES)
    loop_count = lax.axis_size(LOOP_AXES)
    row_place = lax.axis_index(ROW_AXES)
    loop_place = lax.axis_index(LOOP_AXES)
    swap = [(0, 1), (1, 0)]

    texts = spread(text_embed, LOOP_AXES, loop_count).reshape(-1, feature_count)
    images = spread(image_embed, ROW_AXES, row_places).reshape(-1, feature_count)
    other_images = lax.ppermute(images, "core", swap)
    numbers = jnp.concatenate([logit_scale, logit_bias])
    place = jnp.stack([loop_place * row_count, row_place * row_count, jnp.int32(row_count)])
    smem = pl.BlockSpec(memory_space=pltpu.SMEM)
    vmem = pl.BlockSpec(memory_space=pltpu.VMEM)
    text_rows, image_rows = texts.shape[0], images.shape[0]

    def call(kernel, name, in_specs, out_shape, *arguments, work=0, scratch=()):
        return pl.pallas_call(
            kernel,
            out_shape=out_shape,
            in_specs=in_specs,
            out_specs=jax.tree.map(lambda _: vmem, out_shape),
            scratch_shapes=scratch,
            compiler_params=pltpu.CompilerParams(vmem_limit_bytes=32 * 2**20),
            cost_estimate=pl.CostEstimate(
                flops=work * feature_count,
                bytes_accessed=4 * (text_rows + image_rows) * feature_count,
                transcendentals=work // 6,
            ),
            name=name,
        )(*arguments)

    def wide(*shape):
        return jax.ShapeDtypeStruct(shape, jnp.float32)

    text_shape = wide(text_rows, feature_count)
    image_shape = wide(image_rows, feature_count)
    result = wide(row_count, feature_count)
    work = 6 * text_rows * image_rows
    text_part, own_part = call(
        own_kernel, "own_block", [smem, smem, vmem, vmem], (text_shape, image_shape),
        place, numbers, texts, images, work=work,
    )
    text_packed, other_part = call(
        other_kernel, "other_block", [smem, vmem, vmem, vmem], (wide(loop_count, row_count, feature_count + LANES), image_shape),
        numbers, texts, other_images, text_part, work=work,
        scratch=[pltpu.VMEM(text_shape.shape, jnp.float32)],
    )
    arrived = lax.ppermute(other_part, "core", swap)
    text_arrived = exchange(text_packed, LOOP_AXES)
    text_out = call(sum_kernel, "text_sum", [vmem], result, text_arrived)
    image_packed = call(
        add_kernel, "image_pack", [vmem, vmem],
        wide(row_places, row_count, feature_count + LANES), own_part, arrived,
    )
    image_arrived = exchange(image_packed, ROW_AXES)
    image_out = call(sum_kernel, "image_sum", [vmem], result, image_arrived)
    return (image_out, text_out)


def solution(mesh):
    fine = finer_mesh(mesh)
    rows = P(("z_hi", "x", "core", "y", "z_lo"), None)
    return jax.shard_map(
        local, mesh=fine, in_specs=(rows, rows, P(), P()), out_specs=(rows, rows), check_vma=False
    )
```

time: 427 us -> 144 us (0.34)
  the two profiles are of different devices: /device:TPU:1 before, /device:TPU:24 now
where the time goes in v1:
time: 144 us
  waiting for transfers between devices  66.5 us (46%)
  blocking collectives  34.9 us (24%)
  starting transfers between devices  25.9 us (18%)
  Pallas kernels  7.71 us (5%)
  other arithmetic  3.71 us (3%)
  local copies, waits for them, and re-layouts  3.1 us (2%)
  between operations  2.03 us (1%)
    all_to_all x2, waiting for transfers between devices, exchange(): arrived = lax.all_to_all(packed.astype(jnp.float16), axes, 0, 0, tiled=True)  43.3 us
    all_to_all x1, blocking collectives, spread(): lax.all_to_all(jnp.broadcast_to(array[None], (count, *array.shape)), axes...  34.9 us
    all_to_all x1, waiting for transfers between devices, spread(): lax.all_to_all(jnp.broadcast_to(array[None], (count, *array.shape)), axes...  19.5 us
    all_to_all x1, starting transfers between devices, spread(): lax.all_to_all(jnp.broadcast_to(array[None], (count, *array.shape)), axes...  11.9 us
    all_to_all x2, starting transfers between devices, exchange(): arrived = lax.all_to_all(packed.astype(jnp.float16), axes, 0, 0, tiled=True)  10.2 us
    pallas_call x5, Pallas kernels, call(): pl.pallas_call(kernel, out_shape=out_shape, in_specs=in_specs, out_specs=...  7.71 us
    ppermute x1, waiting for transfers between devices, local(): arrived = lax.ppermute(other_part, 'core', swap)  3.66 us
  transfers between devices with their start and end apart: 5, of which 4 were waited for; matrix products, arithmetic and copies ran while one was open for 2% of the time, Pallas kernels for 3%

profile of v1, /device:TPU:24, one launch (start us, length us, event | category | flops | bytes accessed | tf_op | source)
XLA Modules:
  0.0 143.8 jit_solution(9039255480508549786)
XLA Ops:
  0.6 0.0 copy-start.2
  0.6 0.9 broadcast_in_dim.5
  1.5 34.9 %all_to_all.20 = bf16[16,24,1152]{2,1,0:T(8,128)(2,1)S(1)} all-to-all(bf16[16,24,1152]{2,1,0:T(8,128)(2,1)S(1)} %broadcast_in_dim.5), channel_id=1, replica_groups=mesh['z_hi'=4,'x'=4,'core'=2,'y'=8,'z_lo'=2] {'z_hi','x'}, dimensions={0} | all-to-all | bytes 1769472 | tf_op jit(solution)/shard_map/all_to_all | solution.py:86
  36.4 0.0 copy-done.2
  36.4 1.0 broadcast_in_dim.4
  37.4 11.9 %all-to-all-start = ((bf16[16,24,1152]{2,1,0:T(8,128)(2,1)}), bf16[16,24,1152]{2,1,0:T(8,128)(2,1)S(1)}, u32[]{:S(2)}, u32[]{:S(2)}) async-start(bf16[16,24,1152]{2,1,0:T(8,128)(2,1)} %broadcast_in_dim.4), calls=%async_computation | async-start | bytes 1769472 | tf_op jit(solution)/shard_map/all_to_all | solution.py:86
  49.3 1.9 %collective-permute-start = (bf16[384,1152]{1,0:T(8,128)(2,1)S(1)}, bf16[384,1152]{1,0:T(8,128)(2,1)}, u32[]{:S(2)}, u32[]{:S(2)}) collective-permute-start(bf16[384,1152]{1,0:T(8,128)(2,1)S(1)} %bitcast.6), channel_id=1, source_target_pairs={{0,16},{16,0},{1,17},{17,1},{2,18},{18,2},{3,19},{19,3},{4,20},{20... | collective-permute-start | bytes 2654216 | tf_op jit(solution)/shard_map/ppermute | solution.py:106
  52.5 0.1 pad_maximum_fusion.numbers_ref
  52.6 0.1 pad_add_fusion.place_ref
  52.7 19.5 %all-to-all-done = bf16[16,24,1152]{2,1,0:T(8,128)(2,1)S(1)} async-done(((bf16[16,24,1152]{2,1,0:T(8,128)(2,1)}), bf16[16,24,1152]{2,1,0:T(8,128)(2,1)S(1)}, u32[]{:S(2)}, u32[]{:S(2)}) %all-to-all-start) | async-done | bytes 884768 | tf_op jit(solution)/shard_map/all_to_all | solution.py:86
  72.2 2.4 %own_block.1 = (f32[384,1152]{1,0:T(8,128)S(1)}, f32[384,1152]{1,0:T(8,128)S(1)}) custom-call(s32[3]{0:T(128)S(1)} %pad_add_fusion.place_ref, f32[2]{0:T(128)S(1)} %pad_maximum_fusion.numbers_ref, bf16[384,1152]{1,0:T(8,128)(2,1)S(1)} %bitcast.4, bf16[384,1152]{1,0:T(8,128)(2,1)S(1)} %bitcast.7), custom_call_target="tpu_custom_call" | custom-call | flops 1019215872 | bytes 3538944 | tf_op jit(solution)/shard_map/own_block/pallas_call | solution.py:114
  74.7 0.0 collective-permute-done.image_ref
  74.7 3.3 %other_block.1 = (f32[16,24,1280]{2,1,0:T(8,128)S(1)}, f32[384,1152]{1,0:T(8,128)S(1)}) custom-call(f32[2]{0:T(128)S(1)} %pad_maximum_fusion.numbers_ref, bf16[384,1152]{1,0:T(8,128)(2,1)S(1)} %bitcast.5, bf16[384,1152]{1,0:T(8,128)(2,1)} %collective-permute-done.image_ref, f32[384,1152]{1,0:T(8,128)S(1)} %get-tuple-element.7.text_before_ref), custom_call_target="tpu_custom_call" | custom-call | flops 1019215872 | bytes 3538944 | tf_op jit(solution)/shard_map/other_block/pallas_call | solution.py:114
  77.9 0.0 copy-start
  78.0 1.2 copy-done
  79.2 0.0 copy-start.1
  79.2 1.1 convert_element_type.14
  80.2 6.3 %all-to-all-start.3 = ((f16[16,24,1280]{2,1,0:T(8,128)(2,1)}), f16[16,24,1280]{2,1,0:T(8,128)(2,1)}, u32[]{:S(2)}, u32[]{:S(2)}) async-start(f16[16,24,1280]{2,1,0:T(8,128)(2,1)} %convert_element_type.14), calls=%async_computation.3 | async-start | bytes 1966080 | tf_op jit(solution)/shard_map/all_to_all | solution.py:92
  86.5 0.0 copy-done.1
  86.5 1.9 %collective-permute-start.1 = (f32[384,1152]{1,0:T(8,128)S(1)}, f32[384,1152]{1,0:T(8,128)S(1)}, u32[]{:S(2)}, u32[]{:S(2)}) collective-permute-start(f32[384,1152]{1,0:T(8,128)S(1)} %copy-done.1), channel_id=1, source_target_pairs={{0,16},{16,0},{1,17},{17,1},{2,18},{18,2},{3,19},{19,3},{4,20},{20... | collective-permute-start | bytes 5308424 | tf_op jit(solution)/shard_map/ppermute | solution.py:145
  88.5 3.7 %collective-permute-done.1.arrived_ref = f32[384,1152]{1,0:T(8,128)S(1)} collective-permute-done((f32[384,1152]{1,0:T(8,128)S(1)}, f32[384,1152]{1,0:T(8,128)S(1)}, u32[]{:S(2)}, u32[]{:S(2)}) %collective-permute-start.1) | collective-permute-done | bytes 1769504 | tf_op jit(solution)/shard_map/ppermute | solution.py:145
  92.1 0.3 image_pack.1
  92.5 1.0 convert_element_type.12
  93.5 17.1 %all-to-all-done.3 = f16[16,24,1280]{2,1,0:T(8,128)(2,1)} async-done(((f16[16,24,1280]{2,1,0:T(8,128)(2,1)}), f16[16,24,1280]{2,1,0:T(8,128)(2,1)}, u32[]{:S(2)}, u32[]{:S(2)}) %all-to-all-start.3) | async-done | bytes 983072 | tf_op jit(solution)/shard_map/all_to_all | solution.py:92
  110.6 3.9 %all-to-all-start.2 = ((f16[16,24,1280]{2,1,0:T(8,128)(2,1)}), f16[16,24,1280]{2,1,0:T(8,128)(2,1)S(1)}, u32[]{:S(2)}, u32[]{:S(2)}) async-start(f16[16,24,1280]{2,1,0:T(8,128)(2,1)} %convert_element_type.12), calls=%async_computation.2 | async-start | bytes 1966080 | tf_op jit(solution)/shard_map/all_to_all | solution.py:92
  114.5 1.3 convert_element_type.15.packed_ref
  115.8 0.8 text_sum.1
  116.6 26.2 %all-to-all-done.2 = f16[16,24,1280]{2,1,0:T(8,128)(2,1)S(1)} async-done(((f16[16,24,1280]{2,1,0:T(8,128)(2,1)}), f16[16,24,1280]{2,1,0:T(8,128)(2,1)S(1)}, u32[]{:S(2)}, u32[]{:S(2)}) %all-to-all-start.2) | async-done | bytes 983072 | tf_op jit(solution)/shard_map/all_to_all | solution.py:92
  142.8 0.1 convert_element_type.13.packed_ref
  143.0 0.8 image_sum.1
Async XLA Ops:
  0.6 35.8 %copy-start.2 = (bf16[24,1152]{1,0:T(8,128)(2,1)S(1)}, bf16[24,1152]{1,0:T(8,128)(2,1)}, u32[]{:S(2)}) copy-start(bf16[24,1152]{1,0:T(8,128)(2,1)} %param.5) | copy-start | bytes 165892
  37.4 34.8 %all-to-all-start = ((bf16[16,24,1152]{2,1,0:T(8,128)(2,1)}), bf16[16,24,1152]{2,1,0:T(8,128)(2,1)S(1)}, u32[]{:S(2)}, u32[]{:S(2)}) async-start(bf16[16,24,1152]{2,1,0:T(8,128)(2,1)} %broadcast_in_dim.4), calls=%async_computation | async-start | bytes 1769472 | tf_op jit(solution)/shard_map/all_to_all | solution.py:86
  49.3 25.3 %collective-permute-start = (bf16[384,1152]{1,0:T(8,128)(2,1)S(1)}, bf16[384,1152]{1,0:T(8,128)(2,1)}, u32[]{:S(2)}, u32[]{:S(2)}) collective-permute-start(bf16[384,1152]{1,0:T(8,128)(2,1)S(1)} %bitcast.6), channel_id=1, source_target_pairs={{0,16},{16,0},{1,17},{17,1},{2,18},{18,2},{3,19},{19,3},{4,20},{20... | collective-permute-start | bytes 2654216 | tf_op jit(solution)/shard_map/ppermute | solution.py:106
  77.9 1.2 copy-start
  79.2 7.4 %copy-start.1 = (f32[384,1152]{1,0:T(8,128)S(1)}, f32[384,1152]{1,0:T(8,128)}, u32[]{:S(2)}) copy-start(f32[384,1152]{1,0:T(8,128)} %copy-done) | copy-start | bytes 5308420
  80.2 30.4 %all-to-all-start.3 = ((f16[16,24,1280]{2,1,0:T(8,128)(2,1)}), f16[16,24,1280]{2,1,0:T(8,128)(2,1)}, u32[]{:S(2)}, u32[]{:S(2)}) async-start(f16[16,24,1280]{2,1,0:T(8,128)(2,1)} %convert_element_type.14), calls=%async_computation.3 | async-start | bytes 1966080 | tf_op jit(solution)/shard_map/all_to_all | solution.py:92
  86.5 5.6 %collective-permute-start.1 = (f32[384,1152]{1,0:T(8,128)S(1)}, f32[384,1152]{1,0:T(8,128)S(1)}, u32[]{:S(2)}, u32[]{:S(2)}) collective-permute-start(f32[384,1152]{1,0:T(8,128)S(1)} %copy-done.1), channel_id=1, source_target_pairs={{0,16},{16,0},{1,17},{17,1},{2,18},{18,2},{3,19},{19,3},{4,20},{20... | collective-permute-start | bytes 5308424 | tf_op jit(solution)/shard_map/ppermute | solution.py:145
  110.6 32.3 %all-to-all-start.2 = ((f16[16,24,1280]{2,1,0:T(8,128)(2,1)}), f16[16,24,1280]{2,1,0:T(8,128)(2,1)S(1)}, u32[]{:S(2)}, u32[]{:S(2)}) async-start(f16[16,24,1280]{2,1,0:T(8,128)(2,1)} %convert_element_type.12), calls=%async_computation.2 | async-start | bytes 1966080 | tf_op jit(solution)/shard_map/all_to_all | solution.py:92

commit v2 on v1

v2 whole, which is shorter than its diff:
```python
import functools

import jax
import jax.numpy as jnp
from jax import lax
from jax.experimental import pallas as pl
from jax.experimental.pallas import tpu as pltpu
from jax.sharding import Mesh, PartitionSpec as P

MESH_AXES = ("z_hi", "x", "core", "y", "z_lo")
TEXT_AXES = ("y", "z_lo")
LANES = 128
FOLD = 8


def finer_mesh(mesh):
    devices = mesh.devices.reshape(4, 4, 2, 8, 2)
    return Mesh(devices, MESH_AXES)


def weights_of(text, image, scale_value, bias_value, same):
    products = lax.dot_general(
        text, image, (((1,), (1,)), ((), ())), preferred_element_type=jnp.float32
    )
    logits = scale_value * products + bias_value
    if same is None:
        return (scale_value / (1.0 + jnp.exp(-logits))).astype(jnp.bfloat16)
    magnitude = scale_value / (1.0 + jnp.exp(jnp.where(same, logits, -logits)))
    return jnp.where(same, -magnitude, magnitude).astype(jnp.bfloat16)


def pack_into(packed_ref, block, values):
    rows, width = values.shape
    largest = jnp.max(jnp.abs(values), axis=-1, keepdims=True)
    power = jnp.floor(jnp.log2(jnp.maximum(largest, 2.0**-100)))
    scaled = values * jnp.exp2(13.0 - power)
    lane = lax.broadcasted_iota(jnp.int32, (FOLD, LANES), 1)
    tail = jnp.zeros((FOLD, LANES), jnp.float32)
    for k in range(rows // FOLD):
        part = slice(k * FOLD, (k + 1) * FOLD)
        packed_ref[block, :, k * width : (k + 1) * width] = scaled[part, :]
        tail = jnp.where(lane == k, power[part, :], tail)
    packed_ref[block, :, rows // FOLD * width :] = tail


def first_kernel(numbers_ref, text_ref, image_ref, text_part_ref, image_part_ref):
    text = text_ref[...]
    image = image_ref[...]
    weight = weights_of(text, image, numbers_ref[0], numbers_ref[1], None)
    image_part_ref[...] = lax.dot_general(
        weight, text, (((0,), (0,)), ((), ())), preferred_element_type=jnp.float32
    )
    text_part_ref[...] = jnp.dot(weight, image, preferred_element_type=jnp.float32)


def second_kernel(
    place_ref,
    numbers_ref,
    text_ref,
    image_ref,
    text_before_ref,
    packed_ref,
    image_part_ref,
    total_ref,
):
    rows = text_ref.shape[0]
    count = image_ref.shape[0]
    text_at = lax.broadcasted_iota(jnp.int32, (rows, count), 0) - place_ref[0]
    image_at = lax.broadcasted_iota(jnp.int32, (rows, count), 1)
    same = (text_at == image_at) & (text_at < place_ref[1])
    text = text_ref[...]
    image = image_ref[...]
    weight = weights_of(text, image, numbers_ref[0], numbers_ref[1], same)
    total_ref[...] = text_before_ref[...] + jnp.dot(
        weight, image, preferred_element_type=jnp.float32
    )
    blocks = packed_ref.shape[0]
    block_rows = rows // blocks
    for block in range(blocks):
        pack_into(packed_ref, block, total_ref[pl.ds(block * block_rows, block_rows), :])
    image_part_ref[...] = lax.dot_general(
        weight, text, (((0,), (0,)), ((), ())), preferred_element_type=jnp.float32
    )


def unpacked(packed_ref, block, width, k):
    folds = (packed_ref.shape[-1] - LANES) // width
    factor = jnp.exp2(packed_ref[block, :, folds * width :] - 13.0)[:, k : k + 1]
    return packed_ref[block, :, k * width : (k + 1) * width] * factor


def add_kernel(own_ref, arrived_ref, kept_ref, *packed_refs):
    kept_rows = kept_ref.shape[0]
    kept = pl.ds(0, kept_rows)
    kept_ref[...] = own_ref[kept, :] + arrived_ref[kept, :]
    blocks = packed_refs[0].shape[0]
    block_rows = kept_rows // blocks
    for place, packed_ref in enumerate(packed_refs):
        for block in range(blocks):
            part = pl.ds((place + 1) * kept_rows + block * block_rows, block_rows)
            pack_into(packed_ref, block, own_ref[part, :] + arrived_ref[part, :])


def middle_kernel(places, *refs):
    before_ref, arrived_refs = refs[0], refs[1:places]
    kept_ref, packed_refs = refs[places], refs[places + 1 :]
    width = before_ref.shape[-1]
    block_rows = kept_ref.shape[0]
    for block in range(len(packed_refs) + 1):
        stretches = []
        for k in range(block_rows // FOLD):
            total = before_ref[pl.ds(block * block_rows + k * FOLD, FOLD), :]
            for arrived_ref in arrived_refs:
                total = total + unpacked(arrived_ref, block, width, k)
            stretches.append(total)
        total = jnp.concatenate(stretches, axis=0)
        if block == 0:
            kept_ref[...] = total
        else:
            pack_into(packed_refs[block - 1], 0, total)


def last_kernel(*refs):
    before_ref, arrived_refs, out_ref = refs[0], refs[1:-1], refs[-1]
    rows, width = out_ref.shape
    for k in range(rows // FOLD):
        part = pl.ds(k * FOLD, FOLD)
        total = before_ref[part, :]
        for arrived_ref in arrived_refs:
            total = total + unpacked(arrived_ref, 0, width, k)
        out_ref[part, :] = total


def sum_kernel(packed_ref, out_ref):
    rows, width = out_ref.shape
    for k in range(rows // FOLD):
        total = unpacked(packed_ref, 0, width, k)
        for block in range(1, packed_ref.shape[0]):
            total = total + unpacked(packed_ref, block, width, k)
        out_ref[pl.ds(k * FOLD, FOLD), :] = total


def spread(array, axes, count):
    return lax.all_to_all(
        jnp.broadcast_to(array[None], (count, *array.shape)), axes, 0, 0, tiled=True
    )


def exchange(packed, axes):
    arrived = lax.all_to_all(packed.astype(jnp.float16), axes, 0, 0, tiled=True)
    return arrived.astype(jnp.float32)


def gather_ring(array, axis):
    size = lax.axis_size(axis)
    others = [
        lax.ppermute(array, axis, [((i + k) % size, i) for i in range(size)])
        for k in range(1, size)
    ]
    return jnp.concatenate([array, *others], axis=0)


def send_ring(packed, axis):
    size = lax.axis_size(axis)
    return [
        lax.ppermute(
            array.astype(jnp.float16), axis, [(i, (i + k) % size) for i in range(size)]
        ).astype(jnp.float32)
        for k, array in enumerate(packed, 1)
    ]


def local(image_embed, text_embed, logit_scale, logit_bias):
    row_count, feature_count = text_embed.shape
    text_places = lax.axis_size(TEXT_AXES)
    x_places, z_places = lax.axis_size("x"), lax.axis_size("z_hi")
    text_place = lax.axis_index(TEXT_AXES)
    swap = [(0, 1), (1, 0)]

    texts = spread(text_embed, TEXT_AXES, text_places).reshape(-1, feature_count)
    images = gather_ring(gather_ring(image_embed, "z_hi"), "x")
    other_images = lax.ppermute(images, "core", swap)
    numbers = jnp.concatenate([logit_scale, logit_bias])
    place = jnp.stack([text_place * row_count, jnp.int32(row_count)])
    smem = pl.BlockSpec(memory_space=pltpu.SMEM)
    vmem = pl.BlockSpec(memory_space=pltpu.VMEM)
    text_rows, image_rows = texts.shape[0], images.shape[0]

    def call(kernel, name, in_specs, out_shape, *arguments, work=0, scratch=()):
        return pl.pallas_call(
            kernel,
            out_shape=out_shape,
            in_specs=in_specs,
            out_specs=jax.tree.map(lambda _: vmem, out_shape),
            scratch_shapes=scratch,
            compiler_params=pltpu.CompilerParams(vmem_limit_bytes=32 * 2**20),
            cost_estimate=pl.CostEstimate(
                flops=work * feature_count,
                bytes_accessed=4 * (text_rows + image_rows) * feature_count,
                transcendentals=work // 6,
            ),
            name=name,
        )(*arguments)

    def wide(*shape):
        return jax.ShapeDtypeStruct(shape, jnp.float32)

    def packed(places):
        return wide(places, FOLD, row_count // FOLD * feature_count + LANES)

    text_shape = wide(text_rows, feature_count)
    image_shape = wide(image_rows, feature_count)
    result = wide(row_count, feature_count)
    work = 6 * text_rows * image_rows
    text_part, other_part = call(
        first_kernel, "other_block", [smem, vmem, vmem], (text_shape, image_shape),
        numbers, texts, other_images, work=work,
    )
    arrived = lax.ppermute(other_part, "core", swap)
    text_packed, own_part = call(
        second_kernel, "own_block", [smem, smem, vmem, vmem, vmem],
        (packed(text_places), image_shape), place, numbers, texts, images, text_part,
        work=work, scratch=[pltpu.VMEM(text_shape.shape, jnp.float32)],
    )
    text_arrived = exchange(text_packed, TEXT_AXES)
    text_out = call(sum_kernel, "text_sum", [vmem], result, text_arrived)
    kept, *packed_x = call(
        add_kernel, "image_x", [vmem, vmem],
        (wide(z_places * row_count, feature_count), *[packed(z_places)] * (x_places - 1)),
        own_part, arrived,
    )
    kept, *packed_z = call(
        functools.partial(middle_kernel, x_places), "image_z", [vmem] * x_places, (result, *[packed(1)] * (z_places - 1)),
        kept, *send_ring(packed_x, "x"),
    )
    image_out = call(
        last_kernel, "image_sum", [vmem] * z_places, result, kept, *send_ring(packed_z, "z_hi")
    )
    return (image_out, text_out)


def solution(mesh):
    fine = finer_mesh(mesh)
    rows = P(MESH_AXES, None)
    return jax.shard_map(
        local, mesh=fine, in_specs=(rows, rows, P(), P()), out_specs=(rows, rows), check_vma=False
    )
```

time: 144 us -> 118 us (0.82)
  the two profiles are of different devices: /device:TPU:24 before, /device:TPU:1 now
where the time goes in v2:
time: 118 us; the launch traced here: 116 us
  starting transfers between devices  72.3 us (61%)
  waiting for transfers between devices  22.9 us (19%)
  Pallas kernels  8.01 us (7%)
  local copies, waits for them, and re-layouts  7.78 us (7%)
  other arithmetic  2.77 us (2%)
  between operations  2.24 us (2%)
    ppermute x6, starting transfers between devices, gather_ring(): lax.ppermute(array, axis, [((i + k) % size, i) for i in range(size)])  27.6 us
    ppermute x6, starting transfers between devices, send_ring(): lax.ppermute(array.astype(jnp.float16), axis, [(i, (i + k) % size) for i...  20.8 us
    ppermute x6, waiting for transfers between devices, send_ring(): lax.ppermute(array.astype(jnp.float16), axis, [(i, (i + k) % size) for i...  11.7 us
    ppermute x6, waiting for transfers between devices, gather_ring(): lax.ppermute(array, axis, [((i + k) % size, i) for i in range(size)])  9.32 us
    all_to_all x1, starting transfers between devices, spread(): lax.all_to_all(jnp.broadcast_to(array[None], (count, *array.shape)), axes...  8.4 us
    pallas_call x6, Pallas kernels, call(): pl.pallas_call(kernel, out_shape=out_shape, in_specs=in_specs, out_specs=...  8.01 us
    ppermute x1, starting transfers between devices, local(): arrived = lax.ppermute(other_part, 'core', swap)  6.15 us
    unnamed x17, local copies, waits for them, and re-layouts  5.94 us
  transfers between devices with their start and end apart: 16, of which 9 were waited for; matrix products, arithmetic and copies ran while one was open for 5% of the time, Pallas kernels for 4%

profile of v2, /device:TPU:1, one launch (start us, length us, event | category | flops | bytes accessed | tf_op | source)
XLA Modules:
  0.0 116.0 jit_solution(18384156274660235116)
XLA Ops:
  0.6 11.5 %collective-permute-start.1 = (bf16[24,1152]{1,0:T(8,128)(2,1)}, bf16[24,1152]{1,0:T(8,128)(2,1)S(1)}, u32[]{:S(2)}, u32[]{:S(2)}) collective-permute-start(bf16[24,1152]{1,0:T(8,128)(2,1)} %param.4), channel_id=1, source_target_pairs={{256,0},{384,128},{0,256},{128,384},{257,1},{385,129},{1,257},{129... | collective-permute-start | bytes 165896 | tf_op jit(solution)/shard_map/ppermute | solution.py:157
  12.1 1.9 %collective-permute-start = (bf16[24,1152]{1,0:T(8,128)(2,1)}, bf16[24,1152]{1,0:T(8,128)(2,1)S(1)}, u32[]{:S(2)}, u32[]{:S(2)}) collective-permute-start(bf16[24,1152]{1,0:T(8,128)(2,1)} %param.4), channel_id=1, source_target_pairs={{128,0},{256,128},{384,256},{0,384},{129,1},{257,129},{385,257},{1... | collective-permute-start | bytes 165896 | tf_op jit(solution)/shard_map/ppermute | solution.py:157
  14.1 4.2 %collective-permute-start.2 = (bf16[24,1152]{1,0:T(8,128)(2,1)}, bf16[24,1152]{1,0:T(8,128)(2,1)S(1)}, u32[]{:S(2)}, u32[]{:S(2)}) collective-permute-start(bf16[24,1152]{1,0:T(8,128)(2,1)} %param.4), channel_id=1, source_target_pairs={{384,0},{0,128},{128,256},{256,384},{385,1},{1,129},{129,257},{257... | collective-permute-start | bytes 165896 | tf_op jit(solution)/shard_map/ppermute | solution.py:157
  19.6 1.7 %collective-permute-done.2 = bf16[24,1152]{1,0:T(8,128)(2,1)S(1)} collective-permute-done((bf16[24,1152]{1,0:T(8,128)(2,1)}, bf16[24,1152]{1,0:T(8,128)(2,1)S(1)}, u32[]{:S(2)}, u32[]{:S(2)}) %collective-permute-start.2) | collective-permute-done | bytes 55328 | tf_op jit(solution)/shard_map/ppermute | solution.py:157
  21.3 4.4 %collective-permute-start.3 = (bf16[96,1152]{1,0:T(8,128)(2,1)S(1)}, bf16[96,1152]{1,0:T(8,128)(2,1)S(1)}, u32[]{:S(2)}, u32[]{:S(2)}) collective-permute-start(bf16[96,1152]{1,0:T(8,128)(2,1)S(1)} %get-tuple-element.26), channel_id=1, source_target_pairs={{32,0},{64,32},{96,64},{0,96},{33,1},{65,33},{97,65},{1,97},{34,2}... | collective-permute-start | bytes 663560 | tf_op jit(solution)/shard_map/ppermute | solution.py:157
  25.7 1.8 %broadcast_in_dim.2 = bf16[16,24,1152]{2,1,0:T(8,128)(2,1)} broadcast(bf16[24,1152]{1,0:T(8,128)(2,1)} %param.5), dimensions={1,2} | broadcast | bytes 940032 | tf_op jit(solution)/shard_map/broadcast_in_dim | solution.py:145
  27.5 8.4 %all-to-all-start = ((bf16[16,24,1152]{2,1,0:T(8,128)(2,1)}), bf16[16,24,1152]{2,1,0:T(8,128)(2,1)S(1)}, u32[]{:S(2)}, u32[]{:S(2)}) async-start(bf16[16,24,1152]{2,1,0:T(8,128)(2,1)} %broadcast_in_dim.2), calls=%async_computation | async-start | bytes 1769472 | tf_op jit(solution)/shard_map/all_to_all | solution.py:144
  35.9 1.9 %collective-permute-start.5 = (bf16[96,1152]{1,0:T(8,128)(2,1)S(1)}, bf16[96,1152]{1,0:T(8,128)(2,1)S(1)}, u32[]{:S(2)}, u32[]{:S(2)}) collective-permute-start(bf16[96,1152]{1,0:T(8,128)(2,1)S(1)} %get-tuple-element.26), channel_id=1, source_target_pairs={{96,0},{0,32},{32,64},{64,96},{97,1},{1,33},{33,65},{65,97},{98,2}... | collective-permute-start | bytes 663560 | tf_op jit(solution)/shard_map/ppermute | solution.py:157
  37.9 3.6 %collective-permute-start.4 = (bf16[96,1152]{1,0:T(8,128)(2,1)S(1)}, bf16[96,1152]{1,0:T(8,128)(2,1)S(1)}, u32[]{:S(2)}, u32[]{:S(2)}) collective-permute-start(bf16[96,1152]{1,0:T(8,128)(2,1)S(1)} %get-tuple-element.26), channel_id=1, source_target_pairs={{64,0},{96,32},{0,64},{32,96},{65,1},{97,33},{1,65},{33,97},{66,2}... | collective-permute-start | bytes 663560 | tf_op jit(solution)/shard_map/ppermute | solution.py:157
  41.6 7.2 %collective-permute-done.4 = bf16[96,1152]{1,0:T(8,128)(2,1)S(1)} collective-permute-done((bf16[96,1152]{1,0:T(8,128)(2,1)S(1)}, bf16[96,1152]{1,0:T(8,128)(2,1)S(1)}, u32[]{:S(2)}, u32[]{:S(2)}) %collective-permute-start.4) | collective-permute-done | bytes 221216 | tf_op jit(solution)/shard_map/ppermute | solution.py:157
  48.8 5.1 %collective-permute-start.6 = (bf16[384,1152]{1,0:T(8,128)(2,1)S(1)}, bf16[384,1152]{1,0:T(8,128)(2,1)S(1)}, u32[]{:S(2)}, u32[]{:S(2)}) collective-permute-start(bf16[384,1152]{1,0:T(8,128)(2,1)S(1)} %constant_dynamic-update-slice_fusion.4.image_ref), channel_id=1, source_target_pairs={{0,16},{16,0},{1,17},{17,1},{2,18},{18,2},{3,19},{19,3},{4,20},{20... | collective-permute-start | bytes 2654216 | tf_op jit(solution)/shard_map/ppermute | solution.py:182
  55.9 1.2 %all-to-all-done = bf16[16,24,1152]{2,1,0:T(8,128)(2,1)S(1)} async-done(((bf16[16,24,1152]{2,1,0:T(8,128)(2,1)}), bf16[16,24,1152]{2,1,0:T(8,128)(2,1)S(1)}, u32[]{:S(2)}, u32[]{:S(2)}) %all-to-all-start) | async-done | bytes 884768 | tf_op jit(solution)/shard_map/all_to_all | solution.py:144
  57.1 3.2 %other_block.1 = (f32[384,1152]{1,0:T(8,128)S(1)}, f32[384,1152]{1,0:T(8,128)}) custom-call(f32[2]{0:T(128)S(1)} %pad_maximum_fusion.numbers_ref, bf16[384,1152]{1,0:T(8,128)(2,1)S(1)} %bitcast.2, bf16[384,1152]{1,0:T(8,128)(2,1)S(1)} %collective-permute-done.6.image_ref), custom_call_target="tpu_custom_call" | custom-call | flops 1019215872 | bytes 3538944 | tf_op jit(solution)/shard_map/other_block/pallas_call | solution.py:190
  60.3 1.2 %copy-done.4 = f32[384,1152]{1,0:T(8,128)} copy-done((f32[384,1152]{1,0:T(8,128)}, f32[384,1152]{1,0:T(8,128)S(1)}, u32[]{:S(2)}) %copy-start.4) | copy-done | bytes 1769496
  61.5 6.1 %collective-permute-start.7 = (f32[384,1152]{1,0:T(8,128)}, f32[384,1152]{1,0:T(8,128)S(1)}, u32[]{:S(2)}, u32[]{:S(2)}) collective-permute-start(f32[384,1152]{1,0:T(8,128)} %get-tuple-element.16), channel_id=1, source_target_pairs={{0,16},{16,0},{1,17},{17,1},{2,18},{18,2},{3,19},{19,3},{4,20},{20... | collective-permute-start | bytes 5308424 | tf_op jit(solution)/shard_map/ppermute | solution.py:219
  67.7 1.2 %copy-done.1 = bf16[16,24,1152]{2,1,0:T(8,128)(2,1)S(1)} copy-done((bf16[16,24,1152]{2,1,0:T(8,128)(2,1)S(1)}, bf16[16,24,1152]{2,1,0:T(8,128)(2,1)}, u32[]{:S(2)}) %copy-start.1) | copy-done | bytes 884760
  68.9 1.2 %copy-done.3 = bf16[384,1152]{1,0:T(8,128)(2,1)S(1)} copy-done((bf16[384,1152]{1,0:T(8,128)(2,1)S(1)}, bf16[384,1152]{1,0:T(8,128)(2,1)}, u32[]{:S(2)}) %copy-start.3) | copy-done | bytes 884760
  70.0 1.5 %copy-done.5 = f32[384,1152]{1,0:T(8,128)S(1)} copy-done((f32[384,1152]{1,0:T(8,128)S(1)}, f32[384,1152]{1,0:T(8,128)}, u32[]{:S(2)}) %copy-start.5) | copy-done | bytes 1769496
  71.5 2.7 %own_block.1 = (f32[16,8,3584]{2,1,0:T(8,128)S(1)}, f32[384,1152]{1,0:T(8,128)S(1)}) custom-call(s32[2]{0:T(128)S(1)} %pad_add_fusion.place_ref, f32[2]{0:T(128)S(1)} %pad_maximum_fusion.numbers_ref, bf16[384,1152]{1,0:T(8,128)(2,1)S(1)} %bitcast.3, bf16[384,1152]{1,0:T(8,128)(2,1)S(1)} %copy-done.3, f32[384,1152]{1,0:T(8,128)S(1)} %copy-done.5), custom_call_target="tpu_custom_call" | custom-call | flops 1019215872 | bytes 3538944 | tf_op jit(solution)/shard_map/own_block/pallas_call | solution.py:190
  74.2 1.0 convert_element_type.54
  75.2 4.3 %all-to-all-start.1 = ((f16[16,8,3584]{2,1,0:T(8,128)(2,1)}), f16[16,8,3584]{2,1,0:T(8,128)(2,1)}, u32[]{:S(2)}, u32[]{:S(2)}) async-start(f16[16,8,3584]{2,1,0:T(8,128)(2,1)} %convert_element_type.54), calls=%async_computation.1 | async-start | bytes 1835008 | tf_op jit(solution)/shard_map/all_to_all | solution.py:150
  79.9 2.5 %collective-permute-start.10 = (f16[4,8,3584]{2,1,0:T(8,128)(2,1)S(1)}, f16[4,8,3584]{2,1,0:T(8,128)(2,1)S(1)}, u32[]{:S(2)}, u32[]{:S(2)}) collective-permute-start(f16[4,8,3584]{2,1,0:T(8,128)(2,1)S(1)} %convert_element_type.46), channel_id=1, source_target_pairs={{0,96},{32,0},{64,32},{96,64},{1,97},{33,1},{65,33},{97,65},{2,98}... | collective-permute-start | bytes 688136 | tf_op jit(solution)/shard_map/ppermute | solution.py:166
  82.4 2.1 %collective-permute-start.9 = (f16[4,8,3584]{2,1,0:T(8,128)(2,1)S(1)}, f16[4,8,3584]{2,1,0:T(8,128)(2,1)S(1)}, u32[]{:S(2)}, u32[]{:S(2)}) collective-permute-start(f16[4,8,3584]{2,1,0:T(8,128)(2,1)S(1)} %convert_element_type.44), channel_id=1, source_target_pairs={{0,64},{32,96},{64,0},{96,32},{1,65},{33,97},{65,1},{97,33},{2,66}... | collective-permute-start | bytes 688136 | tf_op jit(solution)/shard_map/ppermute | solution.py:166
  84.6 2.6 %collective-permute-start.8 = (f16[4,8,3584]{2,1,0:T(8,128)(2,1)S(1)}, f16[4,8,3584]{2,1,0:T(8,128)(2,1)S(1)}, u32[]{:S(2)}, u32[]{:S(2)}) collective-permute-start(f16[4,8,3584]{2,1,0:T(8,128)(2,1)S(1)} %convert_element_type.42), channel_id=1, source_target_pairs={{0,32},{32,64},{64,96},{96,0},{1,33},{33,65},{65,97},{97,1},{2,34}... | collective-permute-start | bytes 688136 | tf_op jit(solution)/shard_map/ppermute | solution.py:166
  87.2 2.0 %collective-permute-done.10 = f16[4,8,3584]{2,1,0:T(8,128)(2,1)S(1)} collective-permute-done((f16[4,8,3584]{2,1,0:T(8,128)(2,1)S(1)}, f16[4,8,3584]{2,1,0:T(8,128)(2,1)S(1)}, u32[]{:S(2)}, u32[]{:S(2)}) %collective-permute-start.10) | collective-permute-done | bytes 229408 | tf_op jit(solution)/shard_map/ppermute | solution.py:166
  89.2 3.7 %collective-permute-done.9 = f16[4,8,3584]{2,1,0:T(8,128)(2,1)S(1)} collective-permute-done((f16[4,8,3584]{2,1,0:T(8,128)(2,1)S(1)}, f16[4,8,3584]{2,1,0:T(8,128)(2,1)S(1)}, u32[]{:S(2)}, u32[]{:S(2)}) %collective-permute-start.9) | collective-permute-done | bytes 229408 | tf_op jit(solution)/shard_map/ppermute | solution.py:166
  92.9 5.5 %collective-permute-done.8 = f16[4,8,3584]{2,1,0:T(8,128)(2,1)S(1)} collective-permute-done((f16[4,8,3584]{2,1,0:T(8,128)(2,1)S(1)}, f16[4,8,3584]{2,1,0:T(8,128)(2,1)S(1)}, u32[]{:S(2)}, u32[]{:S(2)}) %collective-permute-start.8) | collective-permute-done | bytes 229408 | tf_op jit(solution)/shard_map/ppermute | solution.py:166
  98.7 4.0 %collective-permute-start.13 = (f16[1,8,3584]{2,1,0:T(8,128)(2,1)S(1)}, f16[1,8,3584]{2,1,0:T(8,128)(2,1)S(1)}, u32[]{:S(2)}, u32[]{:S(2)}) collective-permute-start(f16[1,8,3584]{2,1,0:T(8,128)(2,1)S(1)} %convert_element_type.52), channel_id=1, source_target_pairs={{0,384},{128,0},{256,128},{384,256},{1,385},{129,1},{257,129},{385... | collective-permute-start | bytes 172040 | tf_op jit(solution)/shard_map/ppermute | solution.py:166
  102.7 5.3 %collective-permute-start.12 = (f16[1,8,3584]{2,1,0:T(8,128)(2,1)S(1)}, f16[1,8,3584]{2,1,0:T(8,128)(2,1)S(1)}, u32[]{:S(2)}, u32[]{:S(2)}) collective-permute-start(f16[1,8,3584]{2,1,0:T(8,128)(2,1)S(1)} %convert_element_type.50), channel_id=1, source_target_pairs={{0,256},{128,384},{256,0},{384,128},{1,257},{129,385},{257,1},{385... | collective-permute-start | bytes 172040 | tf_op jit(solution)/shard_map/ppermute | solution.py:166
  108.1 4.3 %collective-permute-start.11 = (f16[1,8,3584]{2,1,0:T(8,128)(2,1)S(1)}, f16[1,8,3584]{2,1,0:T(8,128)(2,1)S(1)}, u32[]{:S(2)}, u32[]{:S(2)}) collective-permute-start(f16[1,8,3584]{2,1,0:T(8,128)(2,1)S(1)} %convert_element_type.48), channel_id=1, source_target_pairs={{0,128},{128,256},{256,384},{384,0},{1,129},{129,257},{257,385},{3... | collective-permute-start | bytes 172040 | tf_op jit(solution)/shard_map/ppermute | solution.py:166
  112.4 1.4 %convert_element_type.55.packed_ref = f32[16,8,3584]{2,1,0:T(8,128)S(1)} convert(f16[16,8,3584]{2,1,0:T(8,128)(2,1)} %all-to-all-done.1) | non-fusion elementwise | flops 458752 | bytes 2752512 | tf_op jit(solution)/shard_map/convert_element_type | solution.py:151
  113.7 0.8 text_sum.1
  (42 shorter events, 4.4 us)
Async XLA Ops:
  0.6 18.9 %collective-permute-start.1 = (bf16[24,1152]{1,0:T(8,128)(2,1)}, bf16[24,1152]{1,0:T(8,128)(2,1)S(1)}, u32[]{:S(2)}, u32[]{:S(2)}) collective-permute-start(bf16[24,1152]{1,0:T(8,128)(2,1)} %param.4), channel_id=1, source_target_pairs={{256,0},{384,128},{0,256},{128,384},{257,1},{385,129},{1,257},{129... | collective-permute-start | bytes 165896 | tf_op jit(solution)/shard_map/ppermute | solution.py:157
  12.1 7.4 %collective-permute-start = (bf16[24,1152]{1,0:T(8,128)(2,1)}, bf16[24,1152]{1,0:T(8,128)(2,1)S(1)}, u32[]{:S(2)}, u32[]{:S(2)}) collective-permute-start(bf16[24,1152]{1,0:T(8,128)(2,1)} %param.4), channel_id=1, source_target_pairs={{128,0},{256,128},{384,256},{0,384},{129,1},{257,129},{385,257},{1... | collective-permute-start | bytes 165896 | tf_op jit(solution)/shard_map/ppermute | solution.py:157
  14.1 7.3 %collective-permute-start.2 = (bf16[24,1152]{1,0:T(8,128)(2,1)}, bf16[24,1152]{1,0:T(8,128)(2,1)S(1)}, u32[]{:S(2)}, u32[]{:S(2)}) collective-permute-start(bf16[24,1152]{1,0:T(8,128)(2,1)} %param.4), channel_id=1, source_target_pairs={{384,0},{0,128},{128,256},{256,384},{385,1},{1,129},{129,257},{257... | collective-permute-start | bytes 165896 | tf_op jit(solution)/shard_map/ppermute | solution.py:157
  21.3 20.2 %collective-permute-start.3 = (bf16[96,1152]{1,0:T(8,128)(2,1)S(1)}, bf16[96,1152]{1,0:T(8,128)(2,1)S(1)}, u32[]{:S(2)}, u32[]{:S(2)}) collective-permute-start(bf16[96,1152]{1,0:T(8,128)(2,1)S(1)} %get-tuple-element.26), channel_id=1, source_target_pairs={{32,0},{64,32},{96,64},{0,96},{33,1},{65,33},{97,65},{1,97},{34,2}... | collective-permute-start | bytes 663560 | tf_op jit(solution)/shard_map/ppermute | solution.py:157
  27.5 29.5 %all-to-all-start = ((bf16[16,24,1152]{2,1,0:T(8,128)(2,1)}), bf16[16,24,1152]{2,1,0:T(8,128)(2,1)S(1)}, u32[]{:S(2)}, u32[]{:S(2)}) async-start(bf16[16,24,1152]{2,1,0:T(8,128)(2,1)} %broadcast_in_dim.2), calls=%async_computation | async-start | bytes 1769472 | tf_op jit(solution)/shard_map/all_to_all | solution.py:144
  35.9 12.8 %collective-permute-start.5 = (bf16[96,1152]{1,0:T(8,128)(2,1)S(1)}, bf16[96,1152]{1,0:T(8,128)(2,1)S(1)}, u32[]{:S(2)}, u32[]{:S(2)}) collective-permute-start(bf16[96,1152]{1,0:T(8,128)(2,1)S(1)} %get-tuple-element.26), channel_id=1, source_target_pairs={{96,0},{0,32},{32,64},{64,96},{97,1},{1,33},{33,65},{65,97},{98,2}... | collective-permute-start | bytes 663560 | tf_op jit(solution)/shard_map/ppermute | solution.py:157
  37.9 10.8 %collective-permute-start.4 = (bf16[96,1152]{1,0:T(8,128)(2,1)S(1)}, bf16[96,1152]{1,0:T(8,128)(2,1)S(1)}, u32[]{:S(2)}, u32[]{:S(2)}) collective-permute-start(bf16[96,1152]{1,0:T(8,128)(2,1)S(1)} %get-tuple-element.26), channel_id=1, source_target_pairs={{64,0},{96,32},{0,64},{32,96},{65,1},{97,33},{1,65},{33,97},{66,2}... | collective-permute-start | bytes 663560 | tf_op jit(solution)/shard_map/ppermute | solution.py:157
  48.8 11.5 %copy-start.2 = (bf16[384,1152]{1,0:T(8,128)(2,1)}, bf16[384,1152]{1,0:T(8,128)(2,1)S(1)}, u32[]{:S(2)}) copy-start(bf16[384,1152]{1,0:T(8,128)(2,1)S(1)} %constant_dynamic-update-slice_fusion.4.image_ref) | copy-start | bytes 2654212
  48.8 7.1 %collective-permute-start.6 = (bf16[384,1152]{1,0:T(8,128)(2,1)S(1)}, bf16[384,1152]{1,0:T(8,128)(2,1)S(1)}, u32[]{:S(2)}, u32[]{:S(2)}) collective-permute-start(bf16[384,1152]{1,0:T(8,128)(2,1)S(1)} %constant_dynamic-update-slice_fusion.4.image_ref), channel_id=1, source_target_pairs={{0,16},{16,0},{1,17},{17,1},{2,18},{18,2},{3,19},{19,3},{4,20},{20... | collective-permute-start | bytes 2654216 | tf_op jit(solution)/shard_map/ppermute | solution.py:182
  57.1 3.2 %copy-start = (bf16[16,24,1152]{2,1,0:T(8,128)(2,1)}, bf16[16,24,1152]{2,1,0:T(8,128)(2,1)S(1)}, u32[]{:S(2)}) copy-start(bf16[16,24,1152]{2,1,0:T(8,128)(2,1)S(1)} %all-to-all-done) | copy-start | bytes 2654212
  60.3 1.2 %copy-start.4 = (f32[384,1152]{1,0:T(8,128)}, f32[384,1152]{1,0:T(8,128)S(1)}, u32[]{:S(2)}) copy-start(f32[384,1152]{1,0:T(8,128)S(1)} %get-tuple-element.14.text_before_ref) | copy-start | bytes 5308420
  61.5 18.1 %collective-permute-start.7 = (f32[384,1152]{1,0:T(8,128)}, f32[384,1152]{1,0:T(8,128)S(1)}, u32[]{:S(2)}, u32[]{:S(2)}) collective-permute-start(f32[384,1152]{1,0:T(8,128)} %get-tuple-element.16), channel_id=1, source_target_pairs={{0,16},{16,0},{1,17},{17,1},{2,18},{18,2},{3,19},{19,3},{4,20},{20... | collective-permute-start | bytes 5308424 | tf_op jit(solution)/shard_map/ppermute | solution.py:219
  67.7 1.2 %copy-start.1 = (bf16[16,24,1152]{2,1,0:T(8,128)(2,1)S(1)}, bf16[16,24,1152]{2,1,0:T(8,128)(2,1)}, u32[]{:S(2)}) copy-start(bf16[16,24,1152]{2,1,0:T(8,128)(2,1)} %copy-done) | copy-start | bytes 2654212
  68.9 1.2 %copy-start.3 = (bf16[384,1152]{1,0:T(8,128)(2,1)S(1)}, bf16[384,1152]{1,0:T(8,128)(2,1)}, u32[]{:S(2)}) copy-start(bf16[384,1152]{1,0:T(8,128)(2,1)} %copy-done.2) | copy-start | bytes 2654212
  70.0 1.5 %copy-start.5 = (f32[384,1152]{1,0:T(8,128)S(1)}, f32[384,1152]{1,0:T(8,128)}, u32[]{:S(2)}) copy-start(f32[384,1152]{1,0:T(8,128)} %copy-done.4) | copy-start | bytes 5308420
  75.2 37.2 %all-to-all-start.1 = ((f16[16,8,3584]{2,1,0:T(8,128)(2,1)}), f16[16,8,3584]{2,1,0:T(8,128)(2,1)}, u32[]{:S(2)}, u32[]{:S(2)}) async-start(f16[16,8,3584]{2,1,0:T(8,128)(2,1)} %convert_element_type.54), calls=%async_computation.1 | async-start | bytes 1835008 | tf_op jit(solution)/shard_map/all_to_all | solution.py:150
  79.9 9.2 %collective-permute-start.10 = (f16[4,8,3584]{2,1,0:T(8,128)(2,1)S(1)}, f16[4,8,3584]{2,1,0:T(8,128)(2,1)S(1)}, u32[]{:S(2)}, u32[]{:S(2)}) collective-permute-start(f16[4,8,3584]{2,1,0:T(8,128)(2,1)S(1)} %convert_element_type.46), channel_id=1, source_target_pairs={{0,96},{32,0},{64,32},{96,64},{1,97},{33,1},{65,33},{97,65},{2,98}... | collective-permute-start | bytes 688136 | tf_op jit(solution)/shard_map/ppermute | solution.py:166
  82.4 10.5 %collective-permute-start.9 = (f16[4,8,3584]{2,1,0:T(8,128)(2,1)S(1)}, f16[4,8,3584]{2,1,0:T(8,128)(2,1)S(1)}, u32[]{:S(2)}, u32[]{:S(2)}) collective-permute-start(f16[4,8,3584]{2,1,0:T(8,128)(2,1)S(1)} %convert_element_type.44), channel_id=1, source_target_pairs={{0,64},{32,96},{64,0},{96,32},{1,65},{33,97},{65,1},{97,33},{2,66}... | collective-permute-start | bytes 688136 | tf_op jit(solution)/shard_map/ppermute | solution.py:166
  84.6 13.8 %collective-permute-start.8 = (f16[4,8,3584]{2,1,0:T(8,128)(2,1)S(1)}, f16[4,8,3584]{2,1,0:T(8,128)(2,1)S(1)}, u32[]{:S(2)}, u32[]{:S(2)}) collective-permute-start(f16[4,8,3584]{2,1,0:T(8,128)(2,1)S(1)} %convert_element_type.42), channel_id=1, source_target_pairs={{0,32},{32,64},{64,96},{96,0},{1,33},{33,65},{65,97},{97,1},{2,34}... | collective-permute-start | bytes 688136 | tf_op jit(solution)/shard_map/ppermute | solution.py:166
  98.7 15.8 %collective-permute-start.13 = (f16[1,8,3584]{2,1,0:T(8,128)(2,1)S(1)}, f16[1,8,3584]{2,1,0:T(8,128)(2,1)S(1)}, u32[]{:S(2)}, u32[]{:S(2)}) collective-permute-start(f16[1,8,3584]{2,1,0:T(8,128)(2,1)S(1)} %convert_element_type.52), channel_id=1, source_target_pairs={{0,384},{128,0},{256,128},{384,256},{1,385},{129,1},{257,129},{385... | collective-permute-start | bytes 172040 | tf_op jit(solution)/shard_map/ppermute | solution.py:166
  102.7 11.9 %collective-permute-start.12 = (f16[1,8,3584]{2,1,0:T(8,128)(2,1)S(1)}, f16[1,8,3584]{2,1,0:T(8,128)(2,1)S(1)}, u32[]{:S(2)}, u32[]{:S(2)}) collective-permute-start(f16[1,8,3584]{2,1,0:T(8,128)(2,1)S(1)} %convert_element_type.50), channel_id=1, source_target_pairs={{0,256},{128,384},{256,0},{384,128},{1,257},{129,385},{257,1},{385... | collective-permute-start | bytes 172040 | tf_op jit(solution)/shard_map/ppermute | solution.py:166
  108.1 7.1 %collective-permute-start.11 = (f16[1,8,3584]{2,1,0:T(8,128)(2,1)S(1)}, f16[1,8,3584]{2,1,0:T(8,128)(2,1)S(1)}, u32[]{:S(2)}, u32[]{:S(2)}) collective-permute-start(f16[1,8,3584]{2,1,0:T(8,128)(2,1)S(1)} %convert_element_type.48), channel_id=1, source_target_pairs={{0,128},{128,256},{256,384},{384,0},{1,129},{129,257},{257,385},{3... | collective-permute-start | bytes 172040 | tf_op jit(solution)/shard_map/ppermute | solution.py:166

commit v3 on v2

--- a/solution.py
+++ b/solution.py
@@ -1,5 +1,3 @@
-import functools
-
 import jax
 import jax.numpy as jnp
 from jax import lax
@@ -25,8 +23,14 @@
     logits = scale_value * products + bias_value
     if same is None:
         return (scale_value / (1.0 + jnp.exp(-logits))).astype(jnp.bfloat16)
-    magnitude = scale_value / (1.0 + jnp.exp(jnp.where(same, logits, -logits)))
-    return jnp.where(same, -magnitude, magnitude).astype(jnp.bfloat16)
+    count = same.shape[1]
+    first = logits[:, :count]
+    magnitude = scale_value / (1.0 + jnp.exp(jnp.where(same, first, -first)))
+    weight = jnp.where(same, -magnitude, magnitude)
+    if count < logits.shape[1]:
+        rest = scale_value / (1.0 + jnp.exp(-logits[:, count:]))
+        weight = jnp.concatenate([weight, rest], axis=1)
+    return weight.astype(jnp.bfloat16)
 
 
 def pack_into(packed_ref, block, values):
@@ -43,44 +47,43 @@
     packed_ref[block, :, rows // FOLD * width :] = tail
 
 
-def first_kernel(numbers_ref, text_ref, image_ref, text_part_ref, image_part_ref):
-    text = text_ref[...]
-    image = image_ref[...]
-    weight = weights_of(text, image, numbers_ref[0], numbers_ref[1], None)
-    image_part_ref[...] = lax.dot_general(
-        weight, text, (((0,), (0,)), ((), ())), preferred_element_type=jnp.float32
-    )
-    text_part_ref[...] = jnp.dot(weight, image, preferred_element_type=jnp.float32)
-
-
-def second_kernel(
+def block_kernel(
     place_ref,
     numbers_ref,
     text_ref,
-    image_ref,
-    text_before_ref,
+    own_ref,
+    other_ref,
     packed_ref,
-    image_part_ref,
+    own_part_ref,
+    other_part_ref,
     total_ref,
 ):
     rows = text_ref.shape[0]
-    count = image_ref.shape[0]
+    scale_value, bias_value = numbers_ref[0], numbers_ref[1]
+    text = text_ref[...]
+
+    def back(weight):
+        return lax.dot_general(
+            weight, text, (((0,), (0,)), ((), ())), preferred_element_type=jnp.float32
+        )
+
+    other = other_ref[...]
+    weight = weights_of(text, other, scale_value, bias_value, None)
+    other_part_ref[...] = back(weight)
+    total_ref[...] = jnp.dot(weight, other, preferred_element_type=jnp.float32)
+
+    own = own_ref[...]
+    count = min(LANES, own.shape[0])
     text_at = lax.broadcasted_iota(jnp.int32, (rows, count), 0) - place_ref[0]
-    image_at = lax.broadcasted_iota(jnp.int32, (rows, count), 1)
-    same = (text_at == image_at) & (text_at < place_ref[1])
-    text = text_ref[...]
-    image = image_ref[...]
-    weight = weights_of(text, image, numbers_ref[0], numbers_ref[1], same)
-    total_ref[...] = text_before_ref[...] + jnp.dot(
-        weight, image, preferred_element_type=jnp.float32
-    )
+    image_at = lax.broadcasted_iota(jnp.int32, (rows, count), 1) - place_ref[1]
+    same = (text_at == image_at) & (text_at >= 0) & (text_at < place_ref[2])
+    weight = weights_of(text, own, scale_value, bias_value, same)
+    own_part_ref[...] = back(weight)
+    total_ref[...] += jnp.dot(weight, own, preferred_element_type=jnp.float32)
     blocks = packed_ref.shape[0]
     block_rows = rows // blocks
     for block in range(blocks):
         pack_into(packed_ref, block, total_ref[pl.ds(block * block_rows, block_rows), :])
-    image_part_ref[...] = lax.dot_general(
-        weight, text, (((0,), (0,)), ((), ())), preferred_element_type=jnp.float32
-    )
 
 
 def unpacked(packed_ref, block, width, k):
@@ -101,34 +104,19 @@
             pack_into(packed_ref, block, own_ref[part, :] + arrived_ref[part, :])
 
 
-def middle_kernel(places, *refs):
-    before_ref, arrived_refs = refs[0], refs[1:places]
-    kept_ref, packed_refs = refs[places], refs[places + 1 :]
+def middle_kernel(*refs):
+    before_ref, arrived_refs, packed_ref = refs[0], refs[1:-1], refs[-1]
     width = before_ref.shape[-1]
-    block_rows = kept_ref.shape[0]
-    for block in range(len(packed_refs) + 1):
+    blocks = packed_ref.shape[0]
+    block_rows = before_ref.shape[0] // blocks
+    for block in range(blocks):
         stretches = []
         for k in range(block_rows // FOLD):
             total = before_ref[pl.ds(block * block_rows + k * FOLD, FOLD), :]
             for arrived_ref in arrived_refs:
                 total = total + unpacked(arrived_ref, block, width, k)
             stretches.append(total)
-        total = jnp.concatenate(stretches, axis=0)
-        if block == 0:
-            kept_ref[...] = total
-        else:
-            pack_into(packed_refs[block - 1], 0, total)
-
-
-def last_kernel(*refs):
-    before_ref, arrived_refs, out_ref = refs[0], refs[1:-1], refs[-1]
-    rows, width = out_ref.shape
-    for k in range(rows // FOLD):
-        part = pl.ds(k * FOLD, FOLD)
-        total = before_ref[part, :]
-        for arrived_ref in arrived_refs:
-            total = total + unpacked(arrived_ref, 0, width, k)
-        out_ref[part, :] = total
+        pack_into(packed_ref, block, jnp.concatenate(stretches, axis=0))
 
 
 def sum_kernel(packed_ref, out_ref):
@@ -174,14 +162,15 @@
     row_count, feature_count = text_embed.shape
     text_places = lax.axis_size(TEXT_AXES)
     x_places, z_places = lax.axis_size("x"), lax.axis_size("z_hi")
-    text_place = lax.axis_index(TEXT_AXES)
+    text_place, z_place = lax.axis_index(TEXT_AXES), lax.axis_index("z_hi")
     swap = [(0, 1), (1, 0)]
 
     texts = spread(text_embed, TEXT_AXES, text_places).reshape(-1, feature_count)
-    images = gather_ring(gather_ring(image_embed, "z_hi"), "x")
+    column = spread(image_embed, "z_hi", z_places).reshape(-1, feature_count)
+    images = gather_ring(column, "x")
     other_images = lax.ppermute(images, "core", swap)
     numbers = jnp.concatenate([logit_scale, logit_bias])
-    place = jnp.stack([text_place * row_count, jnp.int32(row_count)])
+    place = jnp.stack([text_place * row_count, z_place * row_count, jnp.int32(row_count)])
     smem = pl.BlockSpec(memory_space=pltpu.SMEM)
     vmem = pl.BlockSpec(memory_space=pltpu.VMEM)
     text_rows, image_rows = texts.shape[0], images.shape[0]
@@ -193,7 +182,7 @@
             in_specs=in_specs,
             out_specs=jax.tree.map(lambda _: vmem, out_shape),
             scratch_shapes=scratch,
-            compiler_params=pltpu.CompilerParams(vmem_limit_bytes=32 * 2**20),
+            compiler_params=pltpu.CompilerParams(vmem_limit_bytes=24 * 2**20),
             cost_estimate=pl.CostEstimate(
                 flops=work * feature_count,
                 bytes_accessed=4 * (text_rows + image_rows) * feature_count,
@@ -211,17 +200,13 @@
     text_shape = wide(text_rows, feature_count)
     image_shape = wide(image_rows, feature_count)
     result = wide(row_count, feature_count)
-    work = 6 * text_rows * image_rows
-    text_part, other_part = call(
-        first_kernel, "other_block", [smem, vmem, vmem], (text_shape, image_shape),
-        numbers, texts, other_images, work=work,
+    text_packed, own_part, other_part = call(
+        block_kernel, "block", [smem, smem, vmem, vmem, vmem],
+        (packed(text_places), image_shape, image_shape),
+        place, numbers, texts, images, other_images,
+        work=12 * text_rows * image_rows, scratch=[pltpu.VMEM(text_shape.shape, jnp.float32)],
     )
     arrived = lax.ppermute(other_part, "core", swap)
-    text_packed, own_part = call(
-        second_kernel, "own_block", [smem, smem, vmem, vmem, vmem],
-        (packed(text_places), image_shape), place, numbers, texts, images, text_part,
-        work=work, scratch=[pltpu.VMEM(text_shape.shape, jnp.float32)],
-    )
     text_arrived = exchange(text_packed, TEXT_AXES)
     text_out = call(sum_kernel, "text_sum", [vmem], result, text_arrived)
     kept, *packed_x = call(
@@ -229,13 +214,11 @@
         (wide(z_places * row_count, feature_count), *[packed(z_places)] * (x_places - 1)),
         own_part, arrived,
     )
-    kept, *packed_z = call(
-        functools.partial(middle_kernel, x_places), "image_z", [vmem] * x_places, (result, *[packed(1)] * (z_places - 1)),
+    packed_z = call(
+        middle_kernel, "image_z", [vmem] * x_places, packed(z_places),
         kept, *send_ring(packed_x, "x"),
     )
-    image_out = call(
-        last_kernel, "image_sum", [vmem] * z_places, result, kept, *send_ring(packed_z, "z_hi")
-    )
+    image_out = call(sum_kernel, "image_sum", [vmem], result, exchange(packed_z, "z_hi"))
     return (image_out, text_out)
 
 

time: 118 us -> 112 us (0.949)
  the two profiles are of different devices: /device:TPU:1 before, /device:TPU:2 now
where the time goes in v3:
time: 112 us; the launch traced here: 111 us
  starting transfers between devices  42.6 us (38%)
  waiting for transfers between devices  29.8 us (27%)
  blocking collectives  20.9 us (19%)
  Pallas kernels  7.31 us (7%)
  local copies, waits for them, and re-layouts  4.77 us (4%)
  other arithmetic  3.53 us (3%)
  between operations  2.13 us (2%)
    all_to_all x1, blocking collectives, spread(): lax.all_to_all(jnp.broadcast_to(array[None], (count, *array.shape)), axes...  20.9 us
    all_to_all x2, waiting for transfers between devices, exchange(): arrived = lax.all_to_all(packed.astype(jnp.float16), axes, 0, 0, tiled=True)  13.8 us
    all_to_all x2, starting transfers between devices, exchange(): arrived = lax.all_to_all(packed.astype(jnp.float16), axes, 0, 0, tiled=True)  10.5 us
    ppermute x3, starting transfers between devices, gather_ring(): lax.ppermute(array, axis, [((i + k) % size, i) for i in range(size)])  10.5 us
    ppermute x3, starting transfers between devices, send_ring(): lax.ppermute(array.astype(jnp.float16), axis, [(i, (i + k) % size) for i...  10.3 us
    ppermute x3, waiting for transfers between devices, send_ring(): lax.ppermute(array.astype(jnp.float16), axis, [(i, (i + k) % size) for i...  7.7 us
    all_to_all x1, starting transfers between devices, spread(): lax.all_to_all(jnp.broadcast_to(array[None], (count, *array.shape)), axes...  7.52 us
    pallas_call x5, Pallas kernels, call(): pl.pallas_call(kernel, out_shape=out_shape, in_specs=in_specs, out_specs=...  7.31 us
  transfers between devices with their start and end apart: 11, of which 8 were waited for; matrix products, arithmetic and copies ran while one was open for 3% of the time, Pallas kernels for 1%

profile of v3, /device:TPU:2, one launch (start us, length us, event | category | flops | bytes accessed | tf_op | source)
XLA Modules:
  0.0 111.0 jit_solution(3431612999675268139)
XLA Ops:
  0.6 0.8 broadcast_in_dim.5
  1.5 20.9 %all_to_all.20 = bf16[4,24,1152]{2,1,0:T(8,128)(2,1)S(1)} all-to-all(bf16[4,24,1152]{2,1,0:T(8,128)(2,1)S(1)} %broadcast_in_dim.5), channel_id=1, replica_groups=mesh['z_hi'=4,'x'=4,'core'=2,'y'=8,'z_lo'=2] {'z_hi'}, dimensions={0} | all-to-all | bytes 442368 | tf_op jit(solution)/shard_map/all_to_all | solution.py:132
  22.3 1.8 %broadcast_in_dim.4 = bf16[16,24,1152]{2,1,0:T(8,128)(2,1)} broadcast(bf16[24,1152]{1,0:T(8,128)(2,1)} %param.5), dimensions={1,2} | broadcast | bytes 940032 | tf_op jit(solution)/shard_map/broadcast_in_dim | solution.py:133
  24.1 7.5 %all-to-all-start = ((bf16[16,24,1152]{2,1,0:T(8,128)(2,1)}), bf16[16,24,1152]{2,1,0:T(8,128)(2,1)S(1)}, u32[]{:S(2)}, u32[]{:S(2)}) async-start(bf16[16,24,1152]{2,1,0:T(8,128)(2,1)} %broadcast_in_dim.4), calls=%async_computation | async-start | bytes 1769472 | tf_op jit(solution)/shard_map/all_to_all | solution.py:132
  31.6 3.4 %collective-permute-start.2 = (bf16[96,1152]{1,0:T(8,128)(2,1)S(1)}, bf16[96,1152]{1,0:T(8,128)(2,1)S(1)}, u32[]{:S(2)}, u32[]{:S(2)}) collective-permute-start(bf16[96,1152]{1,0:T(8,128)(2,1)S(1)} %bitcast.5), channel_id=1, source_target_pairs={{96,0},{0,32},{32,64},{64,96},{97,1},{1,33},{33,65},{65,97},{98,2}... | collective-permute-start | bytes 663560 | tf_op jit(solution)/shard_map/ppermute | solution.py:145
  35.1 3.0 %collective-permute-start.1 = (bf16[96,1152]{1,0:T(8,128)(2,1)S(1)}, bf16[96,1152]{1,0:T(8,128)(2,1)S(1)}, u32[]{:S(2)}, u32[]{:S(2)}) collective-permute-start(bf16[96,1152]{1,0:T(8,128)(2,1)S(1)} %bitcast.6), channel_id=1, source_target_pairs={{64,0},{96,32},{0,64},{32,96},{65,1},{97,33},{1,65},{33,97},{66,2}... | collective-permute-start | bytes 663560 | tf_op jit(solution)/shard_map/ppermute | solution.py:145
  38.1 4.1 %collective-permute-start = (bf16[96,1152]{1,0:T(8,128)(2,1)S(1)}, bf16[96,1152]{1,0:T(8,128)(2,1)S(1)}, u32[]{:S(2)}, u32[]{:S(2)}) collective-permute-start(bf16[96,1152]{1,0:T(8,128)(2,1)S(1)} %bitcast.7), channel_id=1, source_target_pairs={{32,0},{64,32},{96,64},{0,96},{33,1},{65,33},{97,65},{1,97},{34,2}... | collective-permute-start | bytes 663560 | tf_op jit(solution)/shard_map/ppermute | solution.py:145
  42.2 4.2 %collective-permute-done.1 = bf16[96,1152]{1,0:T(8,128)(2,1)S(1)} collective-permute-done((bf16[96,1152]{1,0:T(8,128)(2,1)S(1)}, bf16[96,1152]{1,0:T(8,128)(2,1)S(1)}, u32[]{:S(2)}, u32[]{:S(2)}) %collective-permute-start.1) | collective-permute-done | bytes 221216 | tf_op jit(solution)/shard_map/ppermute | solution.py:145
  46.3 2.3 %collective-permute-done = bf16[96,1152]{1,0:T(8,128)(2,1)S(1)} collective-permute-done((bf16[96,1152]{1,0:T(8,128)(2,1)S(1)}, bf16[96,1152]{1,0:T(8,128)(2,1)S(1)}, u32[]{:S(2)}, u32[]{:S(2)}) %collective-permute-start) | collective-permute-done | bytes 221216 | tf_op jit(solution)/shard_map/ppermute | solution.py:145
  48.7 1.9 %collective-permute-start.3 = (bf16[384,1152]{1,0:T(8,128)(2,1)S(1)}, bf16[384,1152]{1,0:T(8,128)(2,1)S(1)}, u32[]{:S(2)}, u32[]{:S(2)}) collective-permute-start(bf16[384,1152]{1,0:T(8,128)(2,1)S(1)} %pad_maximum_fusion.own_ref), channel_id=1, source_target_pairs={{0,16},{16,0},{1,17},{17,1},{2,18},{18,2},{3,19},{19,3},{4,20},{20... | collective-permute-start | bytes 2654216 | tf_op jit(solution)/shard_map/ppermute | solution.py:171
  52.1 0.9 collective-permute-done.3.other_ref
  53.0 1.0 copy-done
  54.0 0.9 all-to-all-done
  54.9 1.2 %copy-done.1 = bf16[384,1152]{1,0:T(8,128)(2,1)S(1)} copy-done((bf16[384,1152]{1,0:T(8,128)(2,1)S(1)}, bf16[384,1152]{1,0:T(8,128)(2,1)}, u32[]{:S(2)}) %copy-start.1) | copy-done | bytes 884760
  56.0 5.2 %block.1 = (f32[16,8,3584]{2,1,0:T(8,128)S(1)}, f32[384,1152]{1,0:T(8,128)S(1)}, f32[384,1152]{1,0:T(8,128)}) custom-call(s32[3]{0:T(128)S(1)} %pad_add_fusion.place_ref, f32[2]{0:T(128)S(1)} %pad_maximum_fusion.1.numbers_ref, bf16[384,1152]{1,0:T(8,128)(2,1)S(1)} %bitcast.4, bf16[384,1152]{1,0:T(8,128)(2,1)S(1)} %pad_maximum_fusion.own_ref, ...), custom_call_target="tpu_custom_call" | custom-call | flops 2038431744 | bytes 3538944 | tf_op jit(solution)/shard_map/block/pallas_call | solution.py:179
  61.2 1.9 %collective-permute-start.4 = (f32[384,1152]{1,0:T(8,128)}, f32[384,1152]{1,0:T(8,128)S(1)}, u32[]{:S(2)}, u32[]{:S(2)}) collective-permute-start(f32[384,1152]{1,0:T(8,128)} %get-tuple-element.10), channel_id=1, source_target_pairs={{0,16},{16,0},{1,17},{17,1},{2,18},{18,2},{3,19},{19,3},{4,20},{20... | collective-permute-start | bytes 5308424 | tf_op jit(solution)/shard_map/ppermute | solution.py:209
  63.1 1.0 convert_element_type.38
  64.2 7.1 %all-to-all-start.3 = ((f16[16,8,3584]{2,1,0:T(8,128)(2,1)}), f16[16,8,3584]{2,1,0:T(8,128)(2,1)}, u32[]{:S(2)}, u32[]{:S(2)}) async-start(f16[16,8,3584]{2,1,0:T(8,128)(2,1)} %convert_element_type.38), calls=%async_computation.3 | async-start | bytes 1835008 | tf_op jit(solution)/shard_map/all_to_all | solution.py:138
  71.3 0.3 image_x.1
  71.7 2.3 %collective-permute-start.7 = (f16[4,8,3584]{2,1,0:T(8,128)(2,1)S(1)}, f16[4,8,3584]{2,1,0:T(8,128)(2,1)S(1)}, u32[]{:S(2)}, u32[]{:S(2)}) collective-permute-start(f16[4,8,3584]{2,1,0:T(8,128)(2,1)S(1)} %convert_element_type.34), channel_id=1, source_target_pairs={{0,96},{32,0},{64,32},{96,64},{1,97},{33,1},{65,33},{97,65},{2,98}... | collective-permute-start | bytes 688136 | tf_op jit(solution)/shard_map/ppermute | solution.py:154
  74.0 3.5 %collective-permute-start.6 = (f16[4,8,3584]{2,1,0:T(8,128)(2,1)S(1)}, f16[4,8,3584]{2,1,0:T(8,128)(2,1)S(1)}, u32[]{:S(2)}, u32[]{:S(2)}) collective-permute-start(f16[4,8,3584]{2,1,0:T(8,128)(2,1)S(1)} %convert_element_type.32), channel_id=1, source_target_pairs={{0,64},{32,96},{64,0},{96,32},{1,65},{33,97},{65,1},{97,33},{2,66}... | collective-permute-start | bytes 688136 | tf_op jit(solution)/shard_map/ppermute | solution.py:154
  77.6 4.4 %collective-permute-start.5 = (f16[4,8,3584]{2,1,0:T(8,128)(2,1)S(1)}, f16[4,8,3584]{2,1,0:T(8,128)(2,1)S(1)}, u32[]{:S(2)}, u32[]{:S(2)}) collective-permute-start(f16[4,8,3584]{2,1,0:T(8,128)(2,1)S(1)} %convert_element_type.30), channel_id=1, source_target_pairs={{0,32},{32,64},{64,96},{96,0},{1,33},{33,65},{65,97},{97,1},{2,34}... | collective-permute-start | bytes 688136 | tf_op jit(solution)/shard_map/ppermute | solution.py:154
  82.0 4.2 %collective-permute-done.6 = f16[4,8,3584]{2,1,0:T(8,128)(2,1)S(1)} collective-permute-done((f16[4,8,3584]{2,1,0:T(8,128)(2,1)S(1)}, f16[4,8,3584]{2,1,0:T(8,128)(2,1)S(1)}, u32[]{:S(2)}, u32[]{:S(2)}) %collective-permute-start.6) | collective-permute-done | bytes 229408 | tf_op jit(solution)/shard_map/ppermute | solution.py:154
  86.3 3.5 %collective-permute-done.5 = f16[4,8,3584]{2,1,0:T(8,128)(2,1)S(1)} collective-permute-done((f16[4,8,3584]{2,1,0:T(8,128)(2,1)S(1)}, f16[4,8,3584]{2,1,0:T(8,128)(2,1)S(1)}, u32[]{:S(2)}, u32[]{:S(2)}) %collective-permute-start.5) | collective-permute-done | bytes 229408 | tf_op jit(solution)/shard_map/ppermute | solution.py:154
  89.8 0.3 image_z.1
  90.1 0.7 convert_element_type.36
  90.8 7.1 %all-to-all-done.3 = f16[16,8,3584]{2,1,0:T(8,128)(2,1)} async-done(((f16[16,8,3584]{2,1,0:T(8,128)(2,1)}), f16[16,8,3584]{2,1,0:T(8,128)(2,1)}, u32[]{:S(2)}, u32[]{:S(2)}) %all-to-all-start.3) | async-done | bytes 917536 | tf_op jit(solution)/shard_map/all_to_all | solution.py:138
  97.9 3.4 %all-to-all-start.2 = ((f16[4,8,3584]{2,1,0:T(8,128)(2,1)}), f16[4,8,3584]{2,1,0:T(8,128)(2,1)S(1)}, u32[]{:S(2)}, u32[]{:S(2)}) async-start(f16[4,8,3584]{2,1,0:T(8,128)(2,1)} %convert_element_type.36), calls=%async_computation.2 | async-start | bytes 458752 | tf_op jit(solution)/shard_map/all_to_all | solution.py:138
  101.3 1.4 %convert_element_type.39.packed_ref = f32[16,8,3584]{2,1,0:T(8,128)S(1)} convert(f16[16,8,3584]{2,1,0:T(8,128)(2,1)} %all-to-all-done.3) | non-fusion elementwise | flops 458752 | bytes 2752512 | tf_op jit(solution)/shard_map/convert_element_type | solution.py:139
  102.6 0.8 text_sum.1
  103.5 6.7 %all-to-all-done.2 = f16[4,8,3584]{2,1,0:T(8,128)(2,1)S(1)} async-done(((f16[4,8,3584]{2,1,0:T(8,128)(2,1)}), f16[4,8,3584]{2,1,0:T(8,128)(2,1)S(1)}, u32[]{:S(2)}, u32[]{:S(2)}) %all-to-all-start.2) | async-done | bytes 229408 | tf_op jit(solution)/shard_map/all_to_all | solution.py:138
  110.3 0.7 image_sum.1
  (15 shorter events, 0.4 us)
Async XLA Ops:
  24.1 30.8 %all-to-all-start = ((bf16[16,24,1152]{2,1,0:T(8,128)(2,1)}), bf16[16,24,1152]{2,1,0:T(8,128)(2,1)S(1)}, u32[]{:S(2)}, u32[]{:S(2)}) async-start(bf16[16,24,1152]{2,1,0:T(8,128)(2,1)} %broadcast_in_dim.4), calls=%async_computation | async-start | bytes 1769472 | tf_op jit(solution)/shard_map/all_to_all | solution.py:132
  31.6 10.5 %collective-permute-start.2 = (bf16[96,1152]{1,0:T(8,128)(2,1)S(1)}, bf16[96,1152]{1,0:T(8,128)(2,1)S(1)}, u32[]{:S(2)}, u32[]{:S(2)}) collective-permute-start(bf16[96,1152]{1,0:T(8,128)(2,1)S(1)} %bitcast.5), channel_id=1, source_target_pairs={{96,0},{0,32},{32,64},{64,96},{97,1},{1,33},{33,65},{65,97},{98,2}... | collective-permute-start | bytes 663560 | tf_op jit(solution)/shard_map/ppermute | solution.py:145
  35.1 11.3 %collective-permute-start.1 = (bf16[96,1152]{1,0:T(8,128)(2,1)S(1)}, bf16[96,1152]{1,0:T(8,128)(2,1)S(1)}, u32[]{:S(2)}, u32[]{:S(2)}) collective-permute-start(bf16[96,1152]{1,0:T(8,128)(2,1)S(1)} %bitcast.6), channel_id=1, source_target_pairs={{64,0},{96,32},{0,64},{32,96},{65,1},{97,33},{1,65},{33,97},{66,2}... | collective-permute-start | bytes 663560 | tf_op jit(solution)/shard_map/ppermute | solution.py:145
  38.1 10.5 %collective-permute-start = (bf16[96,1152]{1,0:T(8,128)(2,1)S(1)}, bf16[96,1152]{1,0:T(8,128)(2,1)S(1)}, u32[]{:S(2)}, u32[]{:S(2)}) collective-permute-start(bf16[96,1152]{1,0:T(8,128)(2,1)S(1)} %bitcast.7), channel_id=1, source_target_pairs={{32,0},{64,32},{96,64},{0,96},{33,1},{65,33},{97,65},{1,97},{34,2}... | collective-permute-start | bytes 663560 | tf_op jit(solution)/shard_map/ppermute | solution.py:145
  48.7 4.3 %collective-permute-start.3 = (bf16[384,1152]{1,0:T(8,128)(2,1)S(1)}, bf16[384,1152]{1,0:T(8,128)(2,1)S(1)}, u32[]{:S(2)}, u32[]{:S(2)}) collective-permute-start(bf16[384,1152]{1,0:T(8,128)(2,1)S(1)} %pad_maximum_fusion.own_ref), channel_id=1, source_target_pairs={{0,16},{16,0},{1,17},{17,1},{2,18},{18,2},{3,19},{19,3},{4,20},{20... | collective-permute-start | bytes 2654216 | tf_op jit(solution)/shard_map/ppermute | solution.py:171
  53.0 1.0 copy-start
  54.9 1.2 %copy-start.1 = (bf16[384,1152]{1,0:T(8,128)(2,1)S(1)}, bf16[384,1152]{1,0:T(8,128)(2,1)}, u32[]{:S(2)}) copy-start(bf16[384,1152]{1,0:T(8,128)(2,1)} %copy-done) | copy-start | bytes 2654212
  61.2 10.1 %collective-permute-start.4 = (f32[384,1152]{1,0:T(8,128)}, f32[384,1152]{1,0:T(8,128)S(1)}, u32[]{:S(2)}, u32[]{:S(2)}) collective-permute-start(f32[384,1152]{1,0:T(8,128)} %get-tuple-element.10), channel_id=1, source_target_pairs={{0,16},{16,0},{1,17},{17,1},{2,18},{18,2},{3,19},{19,3},{4,20},{20... | collective-permute-start | bytes 5308424 | tf_op jit(solution)/shard_map/ppermute | solution.py:209
  64.2 33.7 %all-to-all-start.3 = ((f16[16,8,3584]{2,1,0:T(8,128)(2,1)}), f16[16,8,3584]{2,1,0:T(8,128)(2,1)}, u32[]{:S(2)}, u32[]{:S(2)}) async-start(f16[16,8,3584]{2,1,0:T(8,128)(2,1)} %convert_element_type.38), calls=%async_computation.3 | async-start | bytes 1835008 | tf_op jit(solution)/shard_map/all_to_all | solution.py:138
  71.7 10.3 %collective-permute-start.7 = (f16[4,8,3584]{2,1,0:T(8,128)(2,1)S(1)}, f16[4,8,3584]{2,1,0:T(8,128)(2,1)S(1)}, u32[]{:S(2)}, u32[]{:S(2)}) collective-permute-start(f16[4,8,3584]{2,1,0:T(8,128)(2,1)S(1)} %convert_element_type.34), channel_id=1, source_target_pairs={{0,96},{32,0},{64,32},{96,64},{1,97},{33,1},{65,33},{97,65},{2,98}... | collective-permute-start | bytes 688136 | tf_op jit(solution)/shard_map/ppermute | solution.py:154
  74.0 12.2 %collective-permute-start.6 = (f16[4,8,3584]{2,1,0:T(8,128)(2,1)S(1)}, f16[4,8,3584]{2,1,0:T(8,128)(2,1)S(1)}, u32[]{:S(2)}, u32[]{:S(2)}) collective-permute-start(f16[4,8,3584]{2,1,0:T(8,128)(2,1)S(1)} %convert_element_type.32), channel_id=1, source_target_pairs={{0,64},{32,96},{64,0},{96,32},{1,65},{33,97},{65,1},{97,33},{2,66}... | collective-permute-start | bytes 688136 | tf_op jit(solution)/shard_map/ppermute | solution.py:154
  77.6 12.2 %collective-permute-start.5 = (f16[4,8,3584]{2,1,0:T(8,128)(2,1)S(1)}, f16[4,8,3584]{2,1,0:T(8,128)(2,1)S(1)}, u32[]{:S(2)}, u32[]{:S(2)}) collective-permute-start(f16[4,8,3584]{2,1,0:T(8,128)(2,1)S(1)} %convert_element_type.30), channel_id=1, source_target_pairs={{0,32},{32,64},{64,96},{96,0},{1,33},{33,65},{65,97},{97,1},{2,34}... | collective-permute-start | bytes 688136 | tf_op jit(solution)/shard_map/ppermute | solution.py:154
  97.9 12.3 %all-to-all-start.2 = ((f16[4,8,3584]{2,1,0:T(8,128)(2,1)}), f16[4,8,3584]{2,1,0:T(8,128)(2,1)S(1)}, u32[]{:S(2)}, u32[]{:S(2)}) async-start(f16[4,8,3584]{2,1,0:T(8,128)(2,1)} %convert_element_type.36), calls=%async_computation.2 | async-start | bytes 458752 | tf_op jit(solution)/shard_map/all_to_all | solution.py:138

commit v4 on v0

v4 whole, which is shorter than its diff:
```python
import jax
import jax.numpy as jnp
import numpy as np
from jax import lax
from jax.experimental import pallas as pl
from jax.experimental.pallas import tpu as pltpu
from jax.sharding import Mesh, PartitionSpec as P

MESH_AXES = ("z_hi", "x_hi", "x_lo", "core", "y", "z_lo")
IMAGE_AXES = ("x_lo", "z_hi", "z_lo")
TEXT_AXES = ("x_hi", "y")
LANES = 128
FOLD = 8


def finer_mesh(mesh):
    return Mesh(mesh.devices.reshape(4, 2, 2, 2, 8, 2), MESH_AXES)


def exchange_groups(sizes):
    places = np.arange(np.prod(sizes)).reshape(sizes)
    groups = []
    for core, axes in enumerate((IMAGE_AXES, TEXT_AXES)):
        part = np.take(places, core, axis=MESH_AXES.index("core"))
        names = [name for name in MESH_AXES if name != "core"]
        fixed = [name for name in names if name not in axes]
        order = [names.index(name) for name in (*fixed, *axes)]
        length = np.prod([sizes[MESH_AXES.index(name)] for name in axes])
        groups += part.transpose(order).reshape(-1, length).tolist()
    return groups


def weights_of(mine, other, scale_value, bias_value, same=None):
    products = lax.dot_general(
        mine, other, (((1,), (1,)), ((), ())), preferred_element_type=jnp.float32
    )
    logits = scale_value * products + bias_value
    if same is None:
        return (scale_value / (1.0 + jnp.exp(-logits))).astype(jnp.bfloat16)
    magnitude = scale_value / (1.0 + jnp.exp(jnp.where(same, logits, -logits)))
    return jnp.where(same, -magnitude, magnitude).astype(jnp.bfloat16)


def pack_into(packed_ref, block, values):
    rows, width = values.shape
    largest = jnp.max(jnp.abs(values), axis=-1, keepdims=True)
    power = jnp.floor(jnp.log2(jnp.maximum(largest, 2.0**-100)))
    scaled = values * jnp.exp2(13.0 - power)
    lane = lax.broadcasted_iota(jnp.int32, (FOLD, LANES), 1)
    tail = jnp.zeros((FOLD, LANES), jnp.float32)
    for k in range(rows // FOLD):
        part = slice(k * FOLD, (k + 1) * FOLD)
        packed_ref[block, :, k * width : (k + 1) * width] = scaled[part, :]
        tail = jnp.where(lane == k, power[part, :], tail)
    packed_ref[block, :, rows // FOLD * width :] = tail


def block_kernel(chip_rows, place_ref, numbers_ref, mine_ref, other_ref, packed_ref, total_ref):
    rows = mine_ref.shape[0]
    scale_value, bias_value = numbers_ref[0], numbers_ref[1]
    other = other_ref[...]
    step = rows // 3
    for start in range(0, rows, step):
        part = pl.ds(start, step)
        weight = weights_of(mine_ref[part, :], other, scale_value, bias_value)
        total_ref[part, :] = jnp.dot(weight, other, preferred_element_type=jnp.float32)

    shape = (chip_rows, other.shape[0])
    band = pl.ds(pl.multiple_of(place_ref[0] * chip_rows, 16), chip_rows)
    row = lax.broadcasted_iota(jnp.int32, shape, 0)
    column = lax.broadcasted_iota(jnp.int32, shape, 1) - place_ref[1] * chip_rows
    weight = weights_of(mine_ref[band, :], other, scale_value, bias_value, row == column)
    total_ref[band, :] = jnp.dot(weight, other, preferred_element_type=jnp.float32)

    blocks = packed_ref.shape[0]
    block_rows = rows // blocks
    for block in range(blocks):
        pack_into(packed_ref, block, total_ref[pl.ds(block * block_rows, block_rows), :])


def sum_kernel(core_ref, packed_ref, own_ref, sent_ref):
    rows, width = own_ref.shape
    folds = rows // FOLD
    for out_ref, core in ((own_ref, core_ref[0]), (sent_ref, 1 - core_ref[0])):
        for k in range(folds):
            total = jnp.zeros((FOLD, width), jnp.float32)
            for place in range(packed_ref.shape[0] // 2):
                block = 2 * place + core
                factor = jnp.exp2(packed_ref[block, :, folds * width :] - 13.0)[:, k : k + 1]
                total = total + packed_ref[block, :, k * width : (k + 1) * width] * factor
            out_ref[pl.ds(k * FOLD, FOLD), :] = total


def local(image_embed, text_embed, logit_scale, logit_bias):
    row_count, feature_count = text_embed.shape
    sizes = tuple(lax.axis_size(name) for name in MESH_AXES)
    groups = exchange_groups(sizes)
    places = len(groups[0])
    core = lax.axis_index("core")
    image_core = core == 0
    swap = [(0, 1), (1, 0)]

    def exchange(array):
        return lax.all_to_all(
            array, MESH_AXES, 0, 0, axis_index_groups=groups, tiled=True
        )

    kept = jnp.where(image_core, image_embed, text_embed)
    arrived = lax.ppermute(jnp.where(image_core, text_embed, image_embed), "core", swap)
    chip = jnp.concatenate(
        [jnp.where(image_core, kept, arrived), jnp.where(image_core, arrived, kept)], axis=0
    )
    mine = exchange(jnp.broadcast_to(chip[None], (places, *chip.shape)))
    mine = mine.reshape(-1, feature_count)
    other = lax.ppermute(mine, "core", swap)

    numbers = jnp.concatenate([logit_scale, logit_bias])
    image_place, text_place = lax.axis_index(IMAGE_AXES), lax.axis_index(TEXT_AXES)
    place = jnp.where(
        image_core, jnp.stack([image_place, text_place]), jnp.stack([text_place, image_place])
    )
    smem = pl.BlockSpec(memory_space=pltpu.SMEM)
    vmem = pl.BlockSpec(memory_space=pltpu.VMEM)
    params = pltpu.CompilerParams(vmem_limit_bytes=24 * 2**20)
    rows = mine.shape[0]
    width = row_count // FOLD * feature_count + LANES
    packed = pl.pallas_call(
        lambda *refs: block_kernel(2 * row_count, *refs),
        out_shape=jax.ShapeDtypeStruct((2 * places, FOLD, width), jnp.float32),
        in_specs=[smem, smem, vmem, vmem],
        out_specs=vmem,
        scratch_shapes=[pltpu.VMEM((rows, feature_count), jnp.float32)],
        compiler_params=params,
        cost_estimate=pl.CostEstimate(
            flops=4 * rows * rows * feature_count,
            bytes_accessed=8 * rows * feature_count,
            transcendentals=rows * rows,
        ),
        name="block",
    )(place, numbers, mine, other)
    sums = exchange(packed.astype(jnp.float16)).astype(jnp.float32)
    result = jax.ShapeDtypeStruct((row_count, feature_count), jnp.float32)
    own, sent = pl.pallas_call(
        sum_kernel,
        out_shape=(result, result),
        in_specs=[smem, vmem],
        out_specs=(vmem, vmem),
        compiler_params=params,
        cost_estimate=pl.CostEstimate(
            flops=4 * rows * feature_count,
            bytes_accessed=4 * rows * feature_count,
            transcendentals=0,
        ),
        name="sum_parts",
    )(core[None], sums)
    sibling = lax.ppermute(sent, "core", swap)
    return (jnp.where(image_core, own, sibling), jnp.where(image_core, sibling, own))


def solution(mesh):
    rows = P(MESH_AXES, None)
    return jax.shard_map(
        local,
        mesh=finer_mesh(mesh),
        in_specs=(rows, rows, P(), P()),
        out_specs=(rows, rows),
        check_vma=False,
    )
```

time: 427 us -> 94.2 us (0.22)
  waiting for transfers between devices: 260 us -> 3.99 us
  matrix products: 73.3 us -> 0 us
  blocking collectives: 0 us -> 64.3 us
  starting transfers between devices: 71.6 us -> 14.5 us
  between operations: 15.4 us -> 2.02 us
  Pallas kernels: 0 us -> 5.67 us
    unnamed x3 -> x0, waiting for transfers between devices: 107 us -> none
    ppermute x31 -> x3, waiting for transfers between devices: 85 us -> 3.99 us  [the longest x1 1.84 us: local(): other = lax.ppermute(mine, 'core', swap)]
    dot_general x33 -> x0, matrix products: 73.3 us -> none  [the longest x16 63.7 us: score_tile(): lax.dot_general(text_block, gathered, (((1,), (1,)), ((), ())), preferred...]
    all_gather x1 -> x0, waiting for transfers between devices: 67.4 us -> none  [local(): gathered = lax.all_gather(image_embed, 'group', axis=0, tiled=True)]
    all_to_all x0 -> x2, blocking collectives: none -> 64.3 us  [exchange(): lax.all_to_all(array, MESH_AXES, 0, 0, axis_index_groups=groups, tiled=True)]
    ppermute x31 -> x3, starting transfers between devices: 71.5 us -> 14.5 us  [the longest x1 8.79 us: local(): lax.ppermute(jnp.where(image_core, text_embed, image_embed), 'core', swap)]
    pallas_call x0 -> x2, Pallas kernels: none -> 5.67 us  [the longest x1 5.32 us: local(): pl.pallas_call(lambda *refs: block_kernel(2 * row_count, *refs), out_shap...]
  transfers between devices with their start and end apart: 33 -> 3, of which waited for: 18 -> 3; matrix products, arithmetic and copies ran while one was open for 16% -> 0% of each run, Pallas kernels for 0% -> 0%
where the time goes in v4:
time: 94.2 us; the launch traced here: 93.8 us
  blocking collectives  64.3 us (68%)
  starting transfers between devices  14.5 us (15%)
  Pallas kernels  5.67 us (6%)
  waiting for transfers between devices  3.99 us (4%)
  other arithmetic  3.16 us (3%)
  between operations  2.02 us (2%)
    all_to_all x2, blocking collectives, exchange(): lax.all_to_all(array, MESH_AXES, 0, 0, axis_index_groups=groups, tiled=True)  64.3 us
    ppermute x1, starting transfers between devices, local(): lax.ppermute(jnp.where(image_core, text_embed, image_embed), 'core', swap)  8.79 us
    pallas_call x1, Pallas kernels, local(): pl.pallas_call(lambda *refs: block_kernel(2 * row_count, *refs), out_shap...  5.32 us
    ppermute x1, starting transfers between devices, local(): other = lax.ppermute(mine, 'core', swap)  3.84 us
    ppermute x1, starting transfers between devices, local(): sibling = lax.ppermute(sent, 'core', swap)  1.92 us
  transfers between devices with their start and end apart: 3, of which 3 were waited for; matrix products, arithmetic and copies ran while one was open for 0% of the time, Pallas kernels for 0%

profile of v4, /device:TPU:1, one launch (start us, length us, event | category | flops | bytes accessed | tf_op | source)
XLA Modules:
  0.0 93.8 jit_solution(5350419107062058351)
XLA Ops:
  0.6 0.8 broadcast_select_fusion.4
  1.5 8.8 %collective-permute-start = (bf16[24,1152]{1,0:T(8,128)(2,1)S(1)}, bf16[24,1152]{1,0:T(8,128)(2,1)S(1)}, u32[]{:S(2)}, u32[]{:S(2)}) collective-permute-start(bf16[24,1152]{1,0:T(8,128)(2,1)S(1)} %broadcast_select_fusion.4), channel_id=1, source_target_pairs={{0,16},{16,0},{1,17},{17,1},{2,18},{18,2},{3,19},{19,3},{4,20},{20... | collective-permute-start | bytes 165896 | tf_op jit(solution)/shard_map/ppermute | solution.py:109
  10.3 0.9 collective-permute-done
  11.1 0.8 broadcast_select_fusion.3
  12.0 0.1 broadcast_in_dim.10
  12.1 29.6 %all_to_all.10 = bf16[16,48,1152]{2,1,0:T(8,128)(2,1)S(1)} all-to-all(bf16[16,48,1152]{2,1,0:T(8,128)(2,1)S(1)} %broadcast_in_dim.10), channel_id=1, replica_groups={{0,1,128,129,256,257,384,385,32,33,160,161,288,289,416,417},{2,3,130,13..., dimensions={0} | all-to-all | bytes 3538944 | tf_op jit(solution)/shard_map/all_to_all | solution.py:104
  41.7 3.8 %collective-permute-start.1 = (bf16[768,1152]{1,0:T(8,128)(2,1)S(1)}, bf16[768,1152]{1,0:T(8,128)(2,1)S(1)}, u32[]{:S(2)}, u32[]{:S(2)}) collective-permute-start(bf16[768,1152]{1,0:T(8,128)(2,1)S(1)} %bitcast.4), channel_id=1, source_target_pairs={{0,16},{16,0},{1,17},{17,1},{2,18},{18,2},{3,19},{19,3},{4,20},{20... | collective-permute-start | bytes 5308424 | tf_op jit(solution)/shard_map/ppermute | solution.py:115
  46.8 0.1 pad_maximum_fusion.1.refs_1_
  46.9 0.1 broadcast_select_fusion.6.refs_0_
  47.0 1.8 %collective-permute-done.1.refs_3_ = bf16[768,1152]{1,0:T(8,128)(2,1)S(1)} collective-permute-done((bf16[768,1152]{1,0:T(8,128)(2,1)S(1)}, bf16[768,1152]{1,0:T(8,128)(2,1)S(1)}, u32[]{:S(2)}, u32[]{:S(2)}) %collective-permute-start.1) | collective-permute-done | bytes 1769504 | tf_op jit(solution)/shard_map/ppermute | solution.py:115
  48.8 5.3 %block.1 = f32[32,8,3584]{2,1,0:T(8,128)S(1)} custom-call(s32[2]{0:T(128)S(1)} %broadcast_select_fusion.6.refs_0_, f32[2]{0:T(128)S(1)} %pad_maximum_fusion.1.refs_1_, bf16[768,1152]{1,0:T(8,128)(2,1)S(1)} %bitcast.5, bf16[768,1152]{1,0:T(8,128)(2,1)S(1)} %collective-permute-done.1.refs_3_), custom_call_target="tpu_custom_call" | custom-call | flops 2717908992 | bytes 7077888 | tf_op jit(solution)/shard_map/block/pallas_call | solution.py:127
  54.1 0.2 convert_element_type.6
  54.4 34.7 %all_to_all.11 = f16[32,8,3584]{2,1,0:T(8,128)(2,1)S(1)} all-to-all(f16[32,8,3584]{2,1,0:T(8,128)(2,1)S(1)} %convert_element_type.6), channel_id=1, replica_groups={{0,1,128,129,256,257,384,385,32,33,160,161,288,289,416,417},{2,3,130,13..., dimensions={0} | all-to-all | bytes 3670016 | tf_op jit(solution)/shard_map/all_to_all | solution.py:104
  89.1 0.4 convert_element_type.7.packed_ref
  89.5 0.4 sum_parts.1
  89.9 1.9 %collective-permute-start.2 = (f32[24,1152]{1,0:T(8,128)S(1)}, f32[24,1152]{1,0:T(8,128)S(1)}, u32[]{:S(2)}, u32[]{:S(2)}) collective-permute-start(f32[24,1152]{1,0:T(8,128)S(1)} %get-tuple-element.5), channel_id=1, source_target_pairs={{0,16},{16,0},{1,17},{17,1},{2,18},{18,2},{3,19},{19,3},{4,20},{20... | collective-permute-start | bytes 331784 | tf_op jit(solution)/shard_map/ppermute | solution.py:156
  91.8 1.3 %collective-permute-done.2 = f32[24,1152]{1,0:T(8,128)S(1)} collective-permute-done((f32[24,1152]{1,0:T(8,128)S(1)}, f32[24,1152]{1,0:T(8,128)S(1)}, u32[]{:S(2)}, u32[]{:S(2)}) %collective-permute-start.2) | collective-permute-done | bytes 110624 | tf_op jit(solution)/shard_map/ppermute | solution.py:156
  93.1 0.7 broadcast_select_fusion
  (1 shorter events, 0.0 us)
Async XLA Ops:
  1.5 9.7 %collective-permute-start = (bf16[24,1152]{1,0:T(8,128)(2,1)S(1)}, bf16[24,1152]{1,0:T(8,128)(2,1)S(1)}, u32[]{:S(2)}, u32[]{:S(2)}) collective-permute-start(bf16[24,1152]{1,0:T(8,128)(2,1)S(1)} %broadcast_select_fusion.4), channel_id=1, source_target_pairs={{0,16},{16,0},{1,17},{17,1},{2,18},{18,2},{3,19},{19,3},{4,20},{20... | collective-permute-start | bytes 165896 | tf_op jit(solution)/shard_map/ppermute | solution.py:109
  41.7 7.1 %collective-permute-start.1 = (bf16[768,1152]{1,0:T(8,128)(2,1)S(1)}, bf16[768,1152]{1,0:T(8,128)(2,1)S(1)}, u32[]{:S(2)}, u32[]{:S(2)}) collective-permute-start(bf16[768,1152]{1,0:T(8,128)(2,1)S(1)} %bitcast.4), channel_id=1, source_target_pairs={{0,16},{16,0},{1,17},{17,1},{2,18},{18,2},{3,19},{19,3},{4,20},{20... | collective-permute-start | bytes 5308424 | tf_op jit(solution)/shard_map/ppermute | solution.py:115
  89.9 3.2 %collective-permute-start.2 = (f32[24,1152]{1,0:T(8,128)S(1)}, f32[24,1152]{1,0:T(8,128)S(1)}, u32[]{:S(2)}, u32[]{:S(2)}) collective-permute-start(f32[24,1152]{1,0:T(8,128)S(1)} %get-tuple-element.5), channel_id=1, source_target_pairs={{0,16},{16,0},{1,17},{17,1},{2,18},{18,2},{3,19},{19,3},{4,20},{20... | collective-permute-start | bytes 331784 | tf_op jit(solution)/shard_map/ppermute | solution.py:156

commit v5 on v4

v5 whole, which is shorter than its diff:
```python
import jax
import jax.numpy as jnp
import numpy as np
from jax import lax
from jax.experimental import pallas as pl
from jax.experimental.pallas import tpu as pltpu
from jax.sharding import Mesh, PartitionSpec as P

MESH_AXES = ("z_hi", "x", "core", "y", "z_lo")
IMAGE_AXES = ("z_hi", "z_lo")
TEXT_AXES = ("y",)
LANES = 128
FOLD = 8


def finer_mesh(mesh):
    return Mesh(mesh.devices.reshape(4, 4, 2, 8, 2), MESH_AXES)


def exchange_groups(sizes):
    places = np.arange(np.prod(sizes)).reshape(sizes)
    groups = []
    for core, axes in enumerate((IMAGE_AXES, TEXT_AXES)):
        part = np.take(places, core, axis=MESH_AXES.index("core"))
        names = [name for name in MESH_AXES if name != "core"]
        fixed = [name for name in names if name not in axes]
        order = [names.index(name) for name in (*fixed, *axes)]
        length = np.prod([sizes[MESH_AXES.index(name)] for name in axes])
        groups += part.transpose(order).reshape(-1, length).tolist()
    return groups


def x_pairs(count):
    pairs = []
    for x in range(count):
        for core in range(2):
            step = 1 if (x + core) % 2 == 0 else -1
            pairs.append((2 * x + core, 2 * ((x + step) % count) + core))
    return pairs


def weights_of(mine, other, scale_value, bias_value, same=None):
    products = lax.dot_general(
        mine, other, (((1,), (1,)), ((), ())), preferred_element_type=jnp.float32
    )
    logits = scale_value * products + bias_value
    if same is None:
        return (scale_value / (1.0 + jnp.exp(-logits))).astype(jnp.bfloat16)
    magnitude = scale_value / (1.0 + jnp.exp(jnp.where(same, logits, -logits)))
    return jnp.where(same, -magnitude, magnitude).astype(jnp.bfloat16)


def pack_into(packed_ref, block, values):
    rows, width = values.shape
    largest = jnp.max(jnp.abs(values), axis=-1, keepdims=True)
    power = jnp.floor(jnp.log2(jnp.maximum(largest, 2.0**-100)))
    scaled = values * jnp.exp2(13.0 - power)
    lane = lax.broadcasted_iota(jnp.int32, (FOLD, LANES), 1)
    tail = jnp.zeros((FOLD, LANES), jnp.float32)
    for k in range(rows // FOLD):
        part = slice(k * FOLD, (k + 1) * FOLD)
        packed_ref[block, :, k * width : (k + 1) * width] = scaled[part, :]
        tail = jnp.where(lane == k, power[part, :], tail)
    packed_ref[block, :, rows // FOLD * width :] = tail


def near_kernel(chip_rows, place_ref, numbers_ref, mine_ref, other_ref, out_ref):
    scale_value, bias_value = numbers_ref[0], numbers_ref[1]
    other = other_ref[...]
    weight = weights_of(mine_ref[...], other, scale_value, bias_value)
    out_ref[...] = jnp.dot(weight, other, preferred_element_type=jnp.float32)

    shape = (chip_rows, other.shape[0])
    band = pl.ds(pl.multiple_of(place_ref[0] * chip_rows, 16), chip_rows)
    row = lax.broadcasted_iota(jnp.int32, shape, 0)
    column = lax.broadcasted_iota(jnp.int32, shape, 1) - place_ref[1] * chip_rows
    weight = weights_of(mine_ref[band, :], other, scale_value, bias_value, row == column)
    out_ref[band, :] = jnp.dot(weight, other, preferred_element_type=jnp.float32)


def far_kernel(numbers_ref, mine_ref, near_ref, far_ref, packed_ref, total_ref):
    scale_value, bias_value = numbers_ref[0], numbers_ref[1]
    mine, near, far = mine_ref[...], near_ref[...], far_ref[...]
    weight = weights_of(mine, near, scale_value, bias_value)
    total_ref[...] = jnp.dot(weight, near, preferred_element_type=jnp.float32)
    weight = weights_of(mine, far, scale_value, bias_value)
    total_ref[...] += jnp.dot(weight, far, preferred_element_type=jnp.float32)
    blocks = packed_ref.shape[0]
    block_rows = mine.shape[0] // blocks
    for block in range(blocks):
        pack_into(packed_ref, block, total_ref[pl.ds(block * block_rows, block_rows), :])


def rest_kernel(numbers_ref, mine_ref, other_ref, before_ref, out_ref):
    other = other_ref[...]
    weight = weights_of(mine_ref[...], other, numbers_ref[0], numbers_ref[1])
    out_ref[...] = before_ref[...] + jnp.dot(weight, other, preferred_element_type=jnp.float32)


def unpacked(packed_ref, block, width, k):
    folds = (packed_ref.shape[-1] - LANES) // width
    factor = jnp.exp2(packed_ref[block, :, folds * width :] - 13.0)[:, k : k + 1]
    return packed_ref[block, :, k * width : (k + 1) * width] * factor


def add_kernel(before_ref, arrived_ref, packed_ref):
    rows, width = before_ref.shape
    blocks = packed_ref.shape[0]
    block_rows = rows // blocks
    for block in range(blocks):
        stretches = [
            before_ref[pl.ds(block * block_rows + k * FOLD, FOLD), :]
            + unpacked(arrived_ref, block, width, k)
            for k in range(block_rows // FOLD)
        ]
        pack_into(packed_ref, block, jnp.concatenate(stretches, axis=0))


def sum_kernel(core_ref, packed_ref, own_ref, sent_ref):
    rows, width = own_ref.shape
    for out_ref, core in ((own_ref, core_ref[0]), (sent_ref, 1 - core_ref[0])):
        for k in range(rows // FOLD):
            total = jnp.zeros((FOLD, width), jnp.float32)
            for place in range(packed_ref.shape[0] // 2):
                total = total + unpacked(packed_ref, 2 * place + core, width, k)
            out_ref[pl.ds(k * FOLD, FOLD), :] = total


def local(image_embed, text_embed, logit_scale, logit_bias):
    row_count, feature_count = text_embed.shape
    sizes = tuple(lax.axis_size(name) for name in MESH_AXES)
    groups = exchange_groups(sizes)
    places = len(groups[0])
    core = lax.axis_index("core")
    image_core = core == 0
    swap = [(0, 1), (1, 0)]

    def exchange(array):
        return lax.all_to_all(
            array, MESH_AXES, 0, 0, axis_index_groups=groups, tiled=True
        )

    def along_x(array):
        return lax.ppermute(array, ("x", "core"), x_pairs(lax.axis_size("x")))

    kept = jnp.where(image_core, image_embed, text_embed)
    arrived = lax.ppermute(jnp.where(image_core, text_embed, image_embed), "core", swap)
    chip = jnp.concatenate(
        [jnp.where(image_core, kept, arrived), jnp.where(image_core, arrived, kept)], axis=0
    )
    near = exchange(jnp.broadcast_to(chip[None], (places, *chip.shape)))
    near = near.reshape(-1, feature_count)
    far = along_x(near)
    other_near = lax.ppermute(near, "core", swap)
    other_far = lax.ppermute(far, "core", swap)

    numbers = jnp.concatenate([logit_scale, logit_bias])
    image_place, text_place = lax.axis_index(IMAGE_AXES), lax.axis_index(TEXT_AXES)
    place = jnp.where(
        image_core, jnp.stack([image_place, text_place]), jnp.stack([text_place, image_place])
    )
    smem = pl.BlockSpec(memory_space=pltpu.SMEM)
    vmem = pl.BlockSpec(memory_space=pltpu.VMEM)
    rows = near.shape[0]
    width = row_count // FOLD * feature_count + LANES

    def wide(*shape):
        return jax.ShapeDtypeStruct(shape, jnp.float32)

    def call(kernel, name, in_specs, out_shape, *arguments, blocks=0, scratch=()):
        return pl.pallas_call(
            kernel,
            out_shape=out_shape,
            in_specs=in_specs,
            out_specs=jax.tree.map(lambda _: vmem, out_shape),
            scratch_shapes=scratch,
            compiler_params=pltpu.CompilerParams(vmem_limit_bytes=20 * 2**20),
            cost_estimate=pl.CostEstimate(
                flops=4 * blocks * rows * rows * feature_count,
                bytes_accessed=8 * rows * feature_count,
                transcendentals=blocks * rows * rows,
            ),
            name=name,
        )(*arguments)

    total = wide(rows, feature_count)
    packed = wide(2 * places, FOLD, width)
    result = wide(row_count, feature_count)
    near_part = call(
        lambda *refs: near_kernel(2 * row_count, *refs), "near_near", [smem, smem, vmem, vmem],
        total, place, numbers, near, other_near, blocks=1,
    )
    far_packed = call(
        far_kernel, "far_rows", [smem, vmem, vmem, vmem], packed,
        numbers, far, other_near, other_far,
        blocks=2, scratch=[pltpu.VMEM(total.shape, jnp.float32)],
    )
    arrived = along_x(far_packed.astype(jnp.float16)).astype(jnp.float32)
    near_part = call(
        rest_kernel, "near_far", [smem, vmem, vmem, vmem], total,
        numbers, near, other_far, near_part, blocks=1,
    )
    near_packed = call(add_kernel, "add_x", [vmem, vmem], packed, near_part, arrived)
    sums = exchange(near_packed.astype(jnp.float16)).astype(jnp.float32)
    own, sent = call(
        sum_kernel, "sum_parts", [smem, vmem], (result, result), core[None], sums
    )
    sibling = lax.ppermute(sent, "core", swap)
    return (jnp.where(image_core, own, sibling), jnp.where(image_core, sibling, own))


def solution(mesh):
    rows = P(MESH_AXES, None)
    return jax.shard_map(
        local,
        mesh=finer_mesh(mesh),
        in_specs=(rows, rows, P(), P()),
        out_specs=(rows, rows),
        check_vma=False,
    )
```

time: 94.2 us -> 103 us (1.093)
  blocking collectives: 64.3 us -> 41.4 us
  starting transfers between devices: 14.5 us -> 30.1 us
  waiting for transfers between devices: 3.99 us -> 15.4 us
  Pallas kernels: 5.67 us -> 8.71 us
  other arithmetic: 3.16 us -> 5.19 us
    all_to_all x2, blocking collectives: 64.3 us -> 41.4 us  [exchange(): lax.all_to_all(array, MESH_AXES, 0, 0, axis_index_groups=groups, tiled=True)]
    ppermute x1 -> x4, starting transfers between devices: 3.84 us -> 19.2 us  [the longest x2 7.9 us: along_x(): return lax.ppermute(array, ('x', 'core'), x_pairs(lax.axis_size('x')))]
    ppermute x1 -> x4, waiting for transfers between devices: 1.84 us -> 13.4 us  [the longest x2 12.8 us: along_x(): return lax.ppermute(array, ('x', 'core'), x_pairs(lax.axis_size('x')))]
    pallas_call x2 -> x5, Pallas kernels: 5.67 us -> 8.71 us  [call(): pl.pallas_call(kernel, out_shape=out_shape, in_specs=in_specs, out_specs=...]
    convert_element_type x2 -> x4, other arithmetic: 0.63 us -> 2.66 us  [the longest x2 2.39 us: local(): arrived = along_x(far_packed.astype(jnp.float16)).astype(jnp.float32)]
  transfers between devices with their start and end apart: 3 -> 6, of which waited for: 3 -> 5; matrix products, arithmetic and copies ran while one was open for 0% -> 0% of each run, Pallas kernels for 0% -> 4%
where the time goes in v5:
time: 103 us
  blocking collectives  41.4 us (40%)
  starting transfers between devices  30.1 us (29%)
  waiting for transfers between devices  15.4 us (15%)
  Pallas kernels  8.71 us (8%)
  other arithmetic  5.19 us (5%)
  between operations  2.06 us (2%)
    all_to_all x2, blocking collectives, exchange(): lax.all_to_all(array, MESH_AXES, 0, 0, axis_index_groups=groups, tiled=True)  41.4 us
    ppermute x2, waiting for transfers between devices, along_x(): return lax.ppermute(array, ('x', 'core'), x_pairs(lax.axis_size('x')))  12.8 us
    ppermute x1, starting transfers between devices, local(): lax.ppermute(jnp.where(image_core, text_embed, image_embed), 'core', swap)  8.79 us
    pallas_call x5, Pallas kernels, call(): pl.pallas_call(kernel, out_shape=out_shape, in_specs=in_specs, out_specs=...  8.71 us
    ppermute x2, starting transfers between devices, along_x(): return lax.ppermute(array, ('x', 'core'), x_pairs(lax.axis_size('x')))  7.9 us
    ppermute x1, starting transfers between devices, local(): other_far = lax.ppermute(far, 'core', swap)  5.69 us
    ppermute x1, starting transfers between devices, local(): other_near = lax.ppermute(near, 'core', swap)  5.62 us
    convert_element_type x2, other arithmetic, local(): arrived = along_x(far_packed.astype(jnp.float16)).astype(jnp.float32)  2.39 us
  transfers between devices with their start and end apart: 6, of which 5 were waited for; matrix products, arithmetic and copies ran while one was open for 0% of the time, Pallas kernels for 4%

profile of v5, /device:TPU:1, one launch (start us, length us, event | category | flops | bytes accessed | tf_op | source)
XLA Modules:
  0.0 102.9 jit_solution(17537646423651192089)
XLA Ops:
  0.6 0.8 broadcast_select_fusion.4
  1.5 8.8 %collective-permute-start = (bf16[24,1152]{1,0:T(8,128)(2,1)S(1)}, bf16[24,1152]{1,0:T(8,128)(2,1)S(1)}, u32[]{:S(2)}, u32[]{:S(2)}) collective-permute-start(bf16[24,1152]{1,0:T(8,128)(2,1)S(1)} %broadcast_select_fusion.4), channel_id=1, source_target_pairs={{0,16},{16,0},{1,17},{17,1},{2,18},{18,2},{3,19},{19,3},{4,20},{20... | collective-permute-start | bytes 165896 | tf_op jit(solution)/shard_map/ppermute | solution.py:147
  10.3 0.9 collective-permute-done
  11.1 0.8 broadcast_select_fusion.3
  12.0 0.1 broadcast_in_dim.10
  12.1 18.4 %all_to_all.10 = bf16[8,48,1152]{2,1,0:T(8,128)(2,1)S(1)} all-to-all(bf16[8,48,1152]{2,1,0:T(8,128)(2,1)S(1)} %broadcast_in_dim.10), channel_id=1, replica_groups={{0,1,128,129,256,257,384,385},{2,3,130,131,258,259,386,387},{4,5,132,13..., dimensions={0} | all-to-all | bytes 1769472 | tf_op jit(solution)/shard_map/all_to_all | solution.py:139
  30.5 3.5 %collective-permute-start.1 = (bf16[384,1152]{1,0:T(8,128)(2,1)S(1)}, bf16[384,1152]{1,0:T(8,128)(2,1)S(1)}, u32[]{:S(2)}, u32[]{:S(2)}) collective-permute-start(bf16[384,1152]{1,0:T(8,128)(2,1)S(1)} %bitcast.4), channel_id=1, source_target_pairs={{0,32},{16,112},{32,0},{48,80},{64,96},{80,48},{96,64},{112,16},{1... | collective-permute-start | bytes 2654216 | tf_op jit(solution)/shard_map/ppermute | solution.py:144
  34.0 5.6 %collective-permute-start.3 = (bf16[384,1152]{1,0:T(8,128)(2,1)S(1)}, bf16[384,1152]{1,0:T(8,128)(2,1)S(1)}, u32[]{:S(2)}, u32[]{:S(2)}) collective-permute-start(bf16[384,1152]{1,0:T(8,128)(2,1)S(1)} %bitcast.5), channel_id=1, source_target_pairs={{0,16},{16,0},{1,17},{17,1},{2,18},{18,2},{3,19},{19,3},{4,20},{20... | collective-permute-start | bytes 2654216 | tf_op jit(solution)/shard_map/ppermute | solution.py:154
  39.6 5.8 %collective-permute-done.1.mine_ref = bf16[384,1152]{1,0:T(8,128)(2,1)S(1)} collective-permute-done((bf16[384,1152]{1,0:T(8,128)(2,1)S(1)}, bf16[384,1152]{1,0:T(8,128)(2,1)S(1)}, u32[]{:S(2)}, u32[]{:S(2)}) %collective-permute-start.1) | collective-permute-done | bytes 884768 | tf_op jit(solution)/shard_map/ppermute | solution.py:144
  45.4 5.7 %collective-permute-start.2 = (bf16[384,1152]{1,0:T(8,128)(2,1)S(1)}, bf16[384,1152]{1,0:T(8,128)(2,1)S(1)}, u32[]{:S(2)}, u32[]{:S(2)}) collective-permute-start(bf16[384,1152]{1,0:T(8,128)(2,1)S(1)} %collective-permute-done.1.mine_ref), channel_id=1, source_target_pairs={{0,16},{16,0},{1,17},{17,1},{2,18},{18,2},{3,19},{19,3},{4,20},{20... | collective-permute-start | bytes 2654216 | tf_op jit(solution)/shard_map/ppermute | solution.py:155
  52.4 0.1 pad_maximum_fusion.1.refs_1_.numbers_ref
  52.5 0.0 collective-permute-done.3.refs_3_.near_ref
  52.5 0.7 collective-permute-done.2.other_ref.far_ref
  53.2 3.1 %far_rows.1 = f32[16,8,3584]{2,1,0:T(8,128)S(1)} custom-call(f32[2]{0:T(128)S(1)} %pad_maximum_fusion.1.refs_1_.numbers_ref, bf16[384,1152]{1,0:T(8,128)(2,1)S(1)} %collective-permute-done.1.mine_ref, bf16[384,1152]{1,0:T(8,128)(2,1)S(1)} %collective-permute-done.3.refs_3_.near_ref, bf16[384,1152]{1,0:T(8,128)(2,1)S(1)} %collective-permute-done.2.other_ref.far_ref), custom_call_target="tpu_custom_call" | custom-call | flops 1358954496 | bytes 3538944 | tf_op jit(solution)/shard_map/far_rows/pallas_call | solution.py:171
  56.2 1.0 %convert_element_type.12 = f16[16,8,3584]{2,1,0:T(8,128)(2,1)} convert(f32[16,8,3584]{2,1,0:T(8,128)S(1)} %far_rows.1) | non-fusion elementwise | flops 458752 | bytes 2752512 | tf_op jit(solution)/shard_map/convert_element_type | solution.py:198
  57.3 4.4 %collective-permute-start.4 = (f16[16,8,3584]{2,1,0:T(8,128)(2,1)}, f16[16,8,3584]{2,1,0:T(8,128)(2,1)}, u32[]{:S(2)}, u32[]{:S(2)}) collective-permute-start(f16[16,8,3584]{2,1,0:T(8,128)(2,1)} %convert_element_type.12), channel_id=1, source_target_pairs={{0,32},{16,112},{32,0},{48,80},{64,96},{80,48},{96,64},{112,16},{1... | collective-permute-start | bytes 2752520 | tf_op jit(solution)/shard_map/ppermute | solution.py:144
  61.7 0.1 broadcast_select_fusion.6.refs_0_
  61.7 2.4 %near_near.1.before_ref = f32[384,1152]{1,0:T(8,128)S(1)} custom-call(s32[2]{0:T(128)S(1)} %broadcast_select_fusion.6.refs_0_, f32[2]{0:T(128)S(1)} %pad_maximum_fusion.1.refs_1_.numbers_ref, bf16[384,1152]{1,0:T(8,128)(2,1)S(1)} %bitcast.6, bf16[384,1152]{1,0:T(8,128)(2,1)S(1)} %collective-permute-done.3.refs_3_.near_ref), custom_call_target="tpu_custom_call" | custom-call | flops 679477248 | bytes 3538944 | tf_op jit(solution)/shard_map/near_near/pallas_call | solution.py:171
  64.1 1.9 %near_far.1.before_ref = f32[384,1152]{1,0:T(8,128)S(1)} custom-call(f32[2]{0:T(128)S(1)} %pad_maximum_fusion.1.refs_1_.numbers_ref, bf16[384,1152]{1,0:T(8,128)(2,1)S(1)} %bitcast.7, bf16[384,1152]{1,0:T(8,128)(2,1)S(1)} %collective-permute-done.2.other_ref.far_ref, f32[384,1152]{1,0:T(8,128)S(1)} %near_near.1.before_ref), custom_call_target="tpu_custom_call" | custom-call | flops 679477248 | bytes 3538944 | tf_op jit(solution)/shard_map/near_far/pallas_call | solution.py:171
  66.0 7.0 %collective-permute-done.4 = f16[16,8,3584]{2,1,0:T(8,128)(2,1)} collective-permute-done((f16[16,8,3584]{2,1,0:T(8,128)(2,1)}, f16[16,8,3584]{2,1,0:T(8,128)(2,1)}, u32[]{:S(2)}, u32[]{:S(2)}) %collective-permute-start.4) | collective-permute-done | bytes 917536 | tf_op jit(solution)/shard_map/ppermute | solution.py:144
  72.9 1.4 %convert_element_type.13.arrived_ref = f32[16,8,3584]{2,1,0:T(8,128)S(1)} convert(f16[16,8,3584]{2,1,0:T(8,128)(2,1)} %collective-permute-done.4) | non-fusion elementwise | flops 458752 | bytes 2752512 | tf_op jit(solution)/shard_map/convert_element_type | solution.py:198
  74.3 1.2 %add_x.1 = f32[16,8,3584]{2,1,0:T(8,128)S(1)} custom-call(f32[384,1152]{1,0:T(8,128)S(1)} %near_far.1.before_ref, f32[16,8,3584]{2,1,0:T(8,128)S(1)} %convert_element_type.13.arrived_ref), custom_call_target="tpu_custom_call" | custom-call | bytes 3538944 | tf_op jit(solution)/shard_map/add_x/pallas_call | solution.py:171
  75.5 0.1 convert_element_type.14
  75.6 23.0 %all_to_all.11 = f16[16,8,3584]{2,1,0:T(8,128)(2,1)S(1)} all-to-all(f16[16,8,3584]{2,1,0:T(8,128)(2,1)S(1)} %convert_element_type.14), channel_id=1, replica_groups={{0,1,128,129,256,257,384,385},{2,3,130,131,258,259,386,387},{4,5,132,13..., dimensions={0} | all-to-all | bytes 1835008 | tf_op jit(solution)/shard_map/all_to_all | solution.py:139
  98.6 0.2 convert_element_type.15.packed_ref
  98.8 0.2 sum_parts.1
  99.0 2.1 %collective-permute-start.5 = (f32[24,1152]{1,0:T(8,128)S(1)}, f32[24,1152]{1,0:T(8,128)S(1)}, u32[]{:S(2)}, u32[]{:S(2)}) collective-permute-start(f32[24,1152]{1,0:T(8,128)S(1)} %get-tuple-element.5), channel_id=1, source_target_pairs={{0,16},{16,0},{1,17},{17,1},{2,18},{18,2},{3,19},{19,3},{4,20},{20... | collective-permute-start | bytes 331784 | tf_op jit(solution)/shard_map/ppermute | solution.py:208
  101.1 1.1 %collective-permute-done.5 = f32[24,1152]{1,0:T(8,128)S(1)} collective-permute-done((f32[24,1152]{1,0:T(8,128)S(1)}, f32[24,1152]{1,0:T(8,128)S(1)}, u32[]{:S(2)}, u32[]{:S(2)}) %collective-permute-start.5) | collective-permute-done | bytes 110624 | tf_op jit(solution)/shard_map/ppermute | solution.py:208
  102.2 0.7 broadcast_select_fusion
  (1 shorter events, 0.0 us)
Async XLA Ops:
  1.5 9.7 %collective-permute-start = (bf16[24,1152]{1,0:T(8,128)(2,1)S(1)}, bf16[24,1152]{1,0:T(8,128)(2,1)S(1)}, u32[]{:S(2)}, u32[]{:S(2)}) collective-permute-start(bf16[24,1152]{1,0:T(8,128)(2,1)S(1)} %broadcast_select_fusion.4), channel_id=1, source_target_pairs={{0,16},{16,0},{1,17},{17,1},{2,18},{18,2},{3,19},{19,3},{4,20},{20... | collective-permute-start | bytes 165896 | tf_op jit(solution)/shard_map/ppermute | solution.py:147
  30.5 15.0 %collective-permute-start.1 = (bf16[384,1152]{1,0:T(8,128)(2,1)S(1)}, bf16[384,1152]{1,0:T(8,128)(2,1)S(1)}, u32[]{:S(2)}, u32[]{:S(2)}) collective-permute-start(bf16[384,1152]{1,0:T(8,128)(2,1)S(1)} %bitcast.4), channel_id=1, source_target_pairs={{0,32},{16,112},{32,0},{48,80},{64,96},{80,48},{96,64},{112,16},{1... | collective-permute-start | bytes 2654216 | tf_op jit(solution)/shard_map/ppermute | solution.py:144
  34.0 18.5 %collective-permute-start.3 = (bf16[384,1152]{1,0:T(8,128)(2,1)S(1)}, bf16[384,1152]{1,0:T(8,128)(2,1)S(1)}, u32[]{:S(2)}, u32[]{:S(2)}) collective-permute-start(bf16[384,1152]{1,0:T(8,128)(2,1)S(1)} %bitcast.5), channel_id=1, source_target_pairs={{0,16},{16,0},{1,17},{17,1},{2,18},{18,2},{3,19},{19,3},{4,20},{20... | collective-permute-start | bytes 2654216 | tf_op jit(solution)/shard_map/ppermute | solution.py:154
  45.4 7.7 %collective-permute-start.2 = (bf16[384,1152]{1,0:T(8,128)(2,1)S(1)}, bf16[384,1152]{1,0:T(8,128)(2,1)S(1)}, u32[]{:S(2)}, u32[]{:S(2)}) collective-permute-start(bf16[384,1152]{1,0:T(8,128)(2,1)S(1)} %collective-permute-done.1.mine_ref), channel_id=1, source_target_pairs={{0,16},{16,0},{1,17},{17,1},{2,18},{18,2},{3,19},{19,3},{4,20},{20... | collective-permute-start | bytes 2654216 | tf_op jit(solution)/shard_map/ppermute | solution.py:155
  57.3 15.7 %collective-permute-start.4 = (f16[16,8,3584]{2,1,0:T(8,128)(2,1)}, f16[16,8,3584]{2,1,0:T(8,128)(2,1)}, u32[]{:S(2)}, u32[]{:S(2)}) collective-permute-start(f16[16,8,3584]{2,1,0:T(8,128)(2,1)} %convert_element_type.12), channel_id=1, source_target_pairs={{0,32},{16,112},{32,0},{48,80},{64,96},{80,48},{96,64},{112,16},{1... | collective-permute-start | bytes 2752520 | tf_op jit(solution)/shard_map/ppermute | solution.py:144
  99.0 3.2 %collective-permute-start.5 = (f32[24,1152]{1,0:T(8,128)S(1)}, f32[24,1152]{1,0:T(8,128)S(1)}, u32[]{:S(2)}, u32[]{:S(2)}) collective-permute-start(f32[24,1152]{1,0:T(8,128)S(1)} %get-tuple-element.5), channel_id=1, source_target_pairs={{0,16},{16,0},{1,17},{17,1},{2,18},{18,2},{3,19},{19,3},{4,20},{20... | collective-permute-start | bytes 331784 | tf_op jit(solution)/shard_map/ppermute | solution.py:208

commit v6 on v4

--- a/solution.py
+++ b/solution.py
@@ -6,27 +6,29 @@
 from jax.experimental.pallas import tpu as pltpu
 from jax.sharding import Mesh, PartitionSpec as P
 
-MESH_AXES = ("z_hi", "x_hi", "x_lo", "core", "y", "z_lo")
-IMAGE_AXES = ("x_lo", "z_hi", "z_lo")
-TEXT_AXES = ("x_hi", "y")
+MESH_AXES = ("z_hi", "x", "core", "y", "z_lo")
+LOG2_E = 1.4426950408889634
 LANES = 128
 FOLD = 8
 
 
 def finer_mesh(mesh):
-    return Mesh(mesh.devices.reshape(4, 2, 2, 2, 8, 2), MESH_AXES)
+    return Mesh(mesh.devices.reshape(4, 4, 2, 8, 2), MESH_AXES)
 
 
 def exchange_groups(sizes):
     places = np.arange(np.prod(sizes)).reshape(sizes)
+    x_count, y_count = sizes[1], sizes[3]
     groups = []
-    for core, axes in enumerate((IMAGE_AXES, TEXT_AXES)):
-        part = np.take(places, core, axis=MESH_AXES.index("core"))
-        names = [name for name in MESH_AXES if name != "core"]
-        fixed = [name for name in names if name not in axes]
-        order = [names.index(name) for name in (*fixed, *axes)]
-        length = np.prod([sizes[MESH_AXES.index(name)] for name in axes])
-        groups += part.transpose(order).reshape(-1, length).tolist()
+    for x in range(0, x_count, 2):
+        pair = [x, x + 1]
+        for y in range(y_count):
+            groups.append(places[:, pair, 0, y, :].transpose(1, 0, 2).reshape(-1).tolist())
+    for x in range(1, x_count, 2):
+        pair = [x, (x + 1) % x_count]
+        for z_hi in range(sizes[0]):
+            for z_lo in range(sizes[4]):
+                groups.append(places[z_hi, pair, 1, :, z_lo].reshape(-1).tolist())
     return groups
 
 
@@ -34,10 +36,10 @@
     products = lax.dot_general(
         mine, other, (((1,), (1,)), ((), ())), preferred_element_type=jnp.float32
     )
-    logits = scale_value * products + bias_value
+    exponent = products * (-LOG2_E * scale_value) + (-LOG2_E * bias_value)
     if same is None:
-        return (scale_value / (1.0 + jnp.exp(-logits))).astype(jnp.bfloat16)
-    magnitude = scale_value / (1.0 + jnp.exp(jnp.where(same, logits, -logits)))
+        return (scale_value / (1.0 + jnp.exp2(exponent))).astype(jnp.bfloat16)
+    magnitude = scale_value / (1.0 + jnp.exp2(jnp.where(same, -exponent, exponent)))
     return jnp.where(same, -magnitude, magnitude).astype(jnp.bfloat16)
 
 
@@ -115,7 +117,10 @@
     other = lax.ppermute(mine, "core", swap)
 
     numbers = jnp.concatenate([logit_scale, logit_bias])
-    image_place, text_place = lax.axis_index(IMAGE_AXES), lax.axis_index(TEXT_AXES)
+    x, y = lax.axis_index("x"), lax.axis_index("y")
+    z_count = sizes[0] * sizes[4]
+    image_place = x % 2 * z_count + lax.axis_index(("z_hi", "z_lo"))
+    text_place = (x + 1) % 2 * sizes[3] + y
     place = jnp.where(
         image_core, jnp.stack([image_place, text_place]), jnp.stack([text_place, image_place])
     )

time: 94.2 us -> 92.4 us (0.981)
  blocking collectives: 64.3 us -> 60.3 us
  starting transfers between devices: 14.5 us -> 16.8 us
    all_to_all x2, blocking collectives: 64.3 us -> 60.3 us  [exchange(): lax.all_to_all(array, MESH_AXES, 0, 0, axis_index_groups=groups, tiled=True)]
    ppermute x1, starting transfers between devices: 3.84 us -> 6.06 us  [local(): other = lax.ppermute(mine, 'core', swap)]
where the time goes in v6:
time: 92.4 us; the launch traced here: 92.1 us
  blocking collectives  60.3 us (65%)
  starting transfers between devices  16.8 us (18%)
  Pallas kernels  5.66 us (6%)
  waiting for transfers between devices  3.98 us (4%)
  other arithmetic  3.16 us (3%)
  between operations  2.03 us (2%)
    all_to_all x2, blocking collectives, exchange(): lax.all_to_all(array, MESH_AXES, 0, 0, axis_index_groups=groups, tiled=True)  60.3 us
    ppermute x1, starting transfers between devices, local(): lax.ppermute(jnp.where(image_core, text_embed, image_embed), 'core', swap)  8.79 us
    ppermute x1, starting transfers between devices, local(): other = lax.ppermute(mine, 'core', swap)  6.06 us
    pallas_call x1, Pallas kernels, local(): pl.pallas_call(lambda *refs: block_kernel(2 * row_count, *refs), out_shap...  5.31 us
    ppermute x1, starting transfers between devices, local(): sibling = lax.ppermute(sent, 'core', swap)  1.92 us
  transfers between devices with their start and end apart: 3, of which 3 were waited for; matrix products, arithmetic and copies ran while one was open for 0% of the time, Pallas kernels for 0%

profile of v6, /device:TPU:1, one launch (start us, length us, event | category | flops | bytes accessed | tf_op | source)
XLA Modules:
  0.0 92.1 jit_solution(1312070919716568700)
XLA Ops:
  0.6 0.8 broadcast_select_fusion.4
  1.5 8.8 %collective-permute-start = (bf16[24,1152]{1,0:T(8,128)(2,1)S(1)}, bf16[24,1152]{1,0:T(8,128)(2,1)S(1)}, u32[]{:S(2)}, u32[]{:S(2)}) collective-permute-start(bf16[24,1152]{1,0:T(8,128)(2,1)S(1)} %broadcast_select_fusion.4), channel_id=1, source_target_pairs={{0,16},{16,0},{1,17},{17,1},{2,18},{18,2},{3,19},{19,3},{4,20},{20... | collective-permute-start | bytes 165896 | tf_op jit(solution)/shard_map/ppermute | solution.py:111
  10.3 0.9 collective-permute-done
  11.1 0.8 broadcast_select_fusion.3
  12.0 0.1 broadcast_in_dim.10
  12.1 27.3 %all_to_all.10 = bf16[16,48,1152]{2,1,0:T(8,128)(2,1)S(1)} all-to-all(bf16[16,48,1152]{2,1,0:T(8,128)(2,1)S(1)} %broadcast_in_dim.10), channel_id=1, replica_groups={{0,1,128,129,256,257,384,385,32,33,160,161,288,289,416,417},{2,3,130,13..., dimensions={0} | all-to-all | bytes 3538944 | tf_op jit(solution)/shard_map/all_to_all | solution.py:106
  39.5 6.1 %collective-permute-start.1 = (bf16[768,1152]{1,0:T(8,128)(2,1)S(1)}, bf16[768,1152]{1,0:T(8,128)(2,1)S(1)}, u32[]{:S(2)}, u32[]{:S(2)}) collective-permute-start(bf16[768,1152]{1,0:T(8,128)(2,1)S(1)} %bitcast.4), channel_id=1, source_target_pairs={{0,16},{16,0},{1,17},{17,1},{2,18},{18,2},{3,19},{19,3},{4,20},{20... | collective-permute-start | bytes 5308424 | tf_op jit(solution)/shard_map/ppermute | solution.py:117
  46.8 0.1 pad_maximum_fusion.1.refs_1_
  46.9 0.1 broadcast_select_fusion.6.refs_0_
  47.0 1.8 %collective-permute-done.1.refs_3_ = bf16[768,1152]{1,0:T(8,128)(2,1)S(1)} collective-permute-done((bf16[768,1152]{1,0:T(8,128)(2,1)S(1)}, bf16[768,1152]{1,0:T(8,128)(2,1)S(1)}, u32[]{:S(2)}, u32[]{:S(2)}) %collective-permute-start.1) | collective-permute-done | bytes 1769504 | tf_op jit(solution)/shard_map/ppermute | solution.py:117
  48.8 5.3 %block.1 = f32[32,8,3584]{2,1,0:T(8,128)S(1)} custom-call(s32[2]{0:T(128)S(1)} %broadcast_select_fusion.6.refs_0_, f32[2]{0:T(128)S(1)} %pad_maximum_fusion.1.refs_1_, bf16[768,1152]{1,0:T(8,128)(2,1)S(1)} %bitcast.5, bf16[768,1152]{1,0:T(8,128)(2,1)S(1)} %collective-permute-done.1.refs_3_), custom_call_target="tpu_custom_call" | custom-call | flops 2717908992 | bytes 7077888 | tf_op jit(solution)/shard_map/block/pallas_call | solution.py:132
  54.1 0.2 convert_element_type.6
  54.3 33.0 %all_to_all.11 = f16[32,8,3584]{2,1,0:T(8,128)(2,1)S(1)} all-to-all(f16[32,8,3584]{2,1,0:T(8,128)(2,1)S(1)} %convert_element_type.6), channel_id=1, replica_groups={{0,1,128,129,256,257,384,385,32,33,160,161,288,289,416,417},{2,3,130,13..., dimensions={0} | all-to-all | bytes 3670016 | tf_op jit(solution)/shard_map/all_to_all | solution.py:106
  87.3 0.4 convert_element_type.7.packed_ref
  87.8 0.4 sum_parts.1
  88.1 1.9 %collective-permute-start.2 = (f32[24,1152]{1,0:T(8,128)S(1)}, f32[24,1152]{1,0:T(8,128)S(1)}, u32[]{:S(2)}, u32[]{:S(2)}) collective-permute-start(f32[24,1152]{1,0:T(8,128)S(1)} %get-tuple-element.5), channel_id=1, source_target_pairs={{0,16},{16,0},{1,17},{17,1},{2,18},{18,2},{3,19},{19,3},{4,20},{20... | collective-permute-start | bytes 331784 | tf_op jit(solution)/shard_map/ppermute | solution.py:161
  90.1 1.3 %collective-permute-done.2 = f32[24,1152]{1,0:T(8,128)S(1)} collective-permute-done((f32[24,1152]{1,0:T(8,128)S(1)}, f32[24,1152]{1,0:T(8,128)S(1)}, u32[]{:S(2)}, u32[]{:S(2)}) %collective-permute-start.2) | collective-permute-done | bytes 110624 | tf_op jit(solution)/shard_map/ppermute | solution.py:161
  91.4 0.7 broadcast_select_fusion
  (1 shorter events, 0.0 us)
Async XLA Ops:
  1.5 9.7 %collective-permute-start = (bf16[24,1152]{1,0:T(8,128)(2,1)S(1)}, bf16[24,1152]{1,0:T(8,128)(2,1)S(1)}, u32[]{:S(2)}, u32[]{:S(2)}) collective-permute-start(bf16[24,1152]{1,0:T(8,128)(2,1)S(1)} %broadcast_select_fusion.4), channel_id=1, source_target_pairs={{0,16},{16,0},{1,17},{17,1},{2,18},{18,2},{3,19},{19,3},{4,20},{20... | collective-permute-start | bytes 165896 | tf_op jit(solution)/shard_map/ppermute | solution.py:111
  39.5 9.4 %collective-permute-start.1 = (bf16[768,1152]{1,0:T(8,128)(2,1)S(1)}, bf16[768,1152]{1,0:T(8,128)(2,1)S(1)}, u32[]{:S(2)}, u32[]{:S(2)}) collective-permute-start(bf16[768,1152]{1,0:T(8,128)(2,1)S(1)} %bitcast.4), channel_id=1, source_target_pairs={{0,16},{16,0},{1,17},{17,1},{2,18},{18,2},{3,19},{19,3},{4,20},{20... | collective-permute-start | bytes 5308424 | tf_op jit(solution)/shard_map/ppermute | solution.py:117
  88.1 3.2 %collective-permute-start.2 = (f32[24,1152]{1,0:T(8,128)S(1)}, f32[24,1152]{1,0:T(8,128)S(1)}, u32[]{:S(2)}, u32[]{:S(2)}) collective-permute-start(f32[24,1152]{1,0:T(8,128)S(1)} %get-tuple-element.5), channel_id=1, source_target_pairs={{0,16},{16,0},{1,17},{17,1},{2,18},{18,2},{3,19},{19,3},{4,20},{20... | collective-permute-start | bytes 331784 | tf_op jit(solution)/shard_map/ppermute | solution.py:161

commit v7 on v6

--- a/solution.py
+++ b/solution.py
@@ -32,15 +32,42 @@
     return groups
 
 
-def weights_of(mine, other, scale_value, bias_value, same=None):
+def x_pairs(count):
+    pairs = []
+    for x in range(count):
+        for core in range(2):
+            step = 1 if (x + core) % 2 == 0 else -1
+            pairs.append((2 * x + core, 2 * ((x + step) % count) + core))
+    return pairs
+
+
+def ring(sizes, step):
+    places = np.arange(np.prod(sizes)).reshape(sizes)
+    along_z = places[:, :, 0].transpose(0, 3, 1, 2).reshape(-1, sizes[1] * sizes[3])
+    along_y = places[:, :, 1].transpose(2, 0, 1, 3)
+    pairs = []
+    for array in (along_z, along_y):
+        pairs += zip(array.reshape(-1).tolist(), np.roll(array, -step, 0).reshape(-1).tolist())
+    return pairs
+
+
+def weights_of(mine, other, scale_value, bias_value, paired=0):
     products = lax.dot_general(
         mine, other, (((1,), (1,)), ((), ())), preferred_element_type=jnp.float32
     )
     exponent = products * (-LOG2_E * scale_value) + (-LOG2_E * bias_value)
-    if same is None:
+    if not paired:
         return (scale_value / (1.0 + jnp.exp2(exponent))).astype(jnp.bfloat16)
-    magnitude = scale_value / (1.0 + jnp.exp2(jnp.where(same, -exponent, exponent)))
-    return jnp.where(same, -magnitude, magnitude).astype(jnp.bfloat16)
+    count = min(LANES, exponent.shape[1])
+    first = exponent[:, :count]
+    row = lax.broadcasted_iota(jnp.int32, first.shape, 0)
+    same = (row == lax.broadcasted_iota(jnp.int32, first.shape, 1)) & (row < paired)
+    magnitude = scale_value / (1.0 + jnp.exp2(jnp.where(same, -first, first)))
+    weight = jnp.where(same, -magnitude, magnitude)
+    if count < exponent.shape[1]:
+        rest = scale_value / (1.0 + jnp.exp2(exponent[:, count:]))
+        weight = jnp.concatenate([weight, rest], axis=1)
+    return weight.astype(jnp.bfloat16)
 
 
 def pack_into(packed_ref, block, values):
@@ -57,27 +84,45 @@
     packed_ref[block, :, rows // FOLD * width :] = tail
 
 
-def block_kernel(chip_rows, place_ref, numbers_ref, mine_ref, other_ref, packed_ref, total_ref):
-    rows = mine_ref.shape[0]
+def block_kernel(
+    offsets,
+    chip_rows,
+    place_ref,
+    numbers_ref,
+    mine_first_ref,
+    mine_last_ref,
+    other_first_ref,
+    other_last_ref,
+    packed_ref,
+    other_ref,
+    total_ref,
+):
     scale_value, bias_value = numbers_ref[0], numbers_ref[1]
+    split, rows = mine_first_ref.shape[0], other_ref.shape[0]
+    other_ref[pl.ds(0, split), :] = other_first_ref[...]
+    other_ref[pl.ds(split, rows - split), :] = other_last_ref[...]
     other = other_ref[...]
-    step = rows // 3
-    for start in range(0, rows, step):
-        part = pl.ds(start, step)
-        weight = weights_of(mine_ref[part, :], other, scale_value, bias_value)
-        total_ref[part, :] = jnp.dot(weight, other, preferred_element_type=jnp.float32)
-
-    shape = (chip_rows, other.shape[0])
-    band = pl.ds(pl.multiple_of(place_ref[0] * chip_rows, 16), chip_rows)
-    row = lax.broadcasted_iota(jnp.int32, shape, 0)
-    column = lax.broadcasted_iota(jnp.int32, shape, 1) - place_ref[1] * chip_rows
-    weight = weights_of(mine_ref[band, :], other, scale_value, bias_value, row == column)
-    total_ref[band, :] = jnp.dot(weight, other, preferred_element_type=jnp.float32)
-
-    blocks = packed_ref.shape[0]
-    block_rows = rows // blocks
-    for block in range(blocks):
-        pack_into(packed_ref, block, total_ref[pl.ds(block * block_rows, block_rows), :])
+    half = split // 2
+    for start, mine, paired in (
+        (0, mine_first_ref[pl.ds(0, half), :], chip_rows),
+        (half, mine_first_ref[pl.ds(half, half), :], 0),
+        (split, mine_last_ref[...], 0),
+    ):
+        weight = weights_of(mine, other, scale_value, bias_value, paired)
+        total_ref[pl.ds(start, mine.shape[0]), :] = jnp.dot(
+            weight, other, preferred_element_type=jnp.float32
+        )
+
+    places = packed_ref.shape[0] // 2
+    length = places // 2
+    block_rows = chip_rows // 2
+    for at, (pair, offset) in enumerate(offsets):
+        across = lax.rem(place_ref[0] + pair, 2)
+        along = lax.rem(place_ref[1] + (offset + length), length)
+        for core in range(2):
+            block = 2 * (across * length + along) + core
+            part = pl.ds((2 * at + core) * block_rows, block_rows)
+            pack_into(packed_ref, block, total_ref[part, :])
 
 
 def sum_kernel(core_ref, packed_ref, own_ref, sent_ref):
@@ -112,29 +157,44 @@
     chip = jnp.concatenate(
         [jnp.where(image_core, kept, arrived), jnp.where(image_core, arrived, kept)], axis=0
     )
-    mine = exchange(jnp.broadcast_to(chip[None], (places, *chip.shape)))
-    mine = mine.reshape(-1, feature_count)
-    other = lax.ppermute(mine, "core", swap)
+    beside = lax.ppermute(chip, ("x", "core"), x_pairs(sizes[1]))
+    column = jnp.concatenate([chip, beside], axis=0)
+    length = places // 2
+    up = down = column
+    pieces, offsets = [column], [(0, 0), (1, 0)]
+    for k in range(1, length // 2):
+        up = lax.ppermute(up, MESH_AXES, ring(sizes, 1))
+        down = lax.ppermute(down, MESH_AXES, ring(sizes, -1))
+        pieces += [up, down]
+        offsets += [(0, -k), (1, -k), (0, k), (1, k)]
+    chip_rows = 2 * row_count
+    pieces.append(lax.ppermute(up[:chip_rows], MESH_AXES, ring(sizes, 1)))
+    pieces.append(lax.ppermute(down[chip_rows:], MESH_AXES, ring(sizes, -1)))
+    offsets += [(0, length // 2), (1, length // 2)]
+    cut = max(1, len(pieces) - 4)
+    mine_first = jnp.concatenate(pieces[:cut], axis=0)
+    mine_last = jnp.concatenate(pieces[cut:], axis=0)
+    other_first = lax.ppermute(mine_first, "core", swap)
+    other_last = lax.ppermute(mine_last, "core", swap)
 
     numbers = jnp.concatenate([logit_scale, logit_bias])
-    x, y = lax.axis_index("x"), lax.axis_index("y")
-    z_count = sizes[0] * sizes[4]
-    image_place = x % 2 * z_count + lax.axis_index(("z_hi", "z_lo"))
-    text_place = (x + 1) % 2 * sizes[3] + y
-    place = jnp.where(
-        image_core, jnp.stack([image_place, text_place]), jnp.stack([text_place, image_place])
-    )
+    across = (lax.axis_index("x") + core) % 2
+    along = jnp.where(image_core, lax.axis_index(("z_hi", "z_lo")), lax.axis_index("y"))
+    place = jnp.stack([across, along])
     smem = pl.BlockSpec(memory_space=pltpu.SMEM)
     vmem = pl.BlockSpec(memory_space=pltpu.VMEM)
     params = pltpu.CompilerParams(vmem_limit_bytes=24 * 2**20)
-    rows = mine.shape[0]
+    rows = chip_rows * places
     width = row_count // FOLD * feature_count + LANES
     packed = pl.pallas_call(
-        lambda *refs: block_kernel(2 * row_count, *refs),
+        lambda *refs: block_kernel(offsets, chip_rows, *refs),
         out_shape=jax.ShapeDtypeStruct((2 * places, FOLD, width), jnp.float32),
-        in_specs=[smem, smem, vmem, vmem],
+        in_specs=[smem, smem, vmem, vmem, vmem, vmem],
         out_specs=vmem,
-        scratch_shapes=[pltpu.VMEM((rows, feature_count), jnp.float32)],
+        scratch_shapes=[
+            pltpu.VMEM((rows, feature_count), jnp.bfloat16),
+            pltpu.VMEM((rows, feature_count), jnp.float32),
+        ],
         compiler_params=params,
         cost_estimate=pl.CostEstimate(
             flops=4 * rows * rows * feature_count,
@@ -142,7 +202,7 @@
             transcendentals=rows * rows,
         ),
         name="block",
-    )(place, numbers, mine, other)
+    )(place, numbers, mine_first, mine_last, other_first, other_last)
     sums = exchange(packed.astype(jnp.float16)).astype(jnp.float32)
     result = jax.ShapeDtypeStruct((row_count, feature_count), jnp.float32)
     own, sent = pl.pallas_call(

time: 92.4 us -> 108 us (1.17)
  starting transfers between devices: 16.8 us -> 46.8 us
  blocking collectives: 60.3 us -> 33.1 us
  waiting for transfers between devices: 3.98 us -> 15.5 us
    ppermute x1 -> x11, starting transfers between devices: 6.06 us -> 36.1 us  [the longest x3 8.78 us: local(): down = lax.ppermute(down, MESH_AXES, ring(sizes, -1))]
    all_to_all x2 -> x1, blocking collectives: 60.3 us -> 33.1 us  [exchange(): lax.all_to_all(array, MESH_AXES, 0, 0, axis_index_groups=groups, tiled=True)]
    ppermute x1 -> x11, waiting for transfers between devices: 1.83 us -> 13.3 us  [the longest x1 5.01 us: local(): pieces.append(lax.ppermute(up[:chip_rows], MESH_AXES, ring(sizes, 1)))]
    unnamed x0 -> x2, other arithmetic: none -> 1.71 us
  transfers between devices with their start and end apart: 3 -> 13, of which waited for: 3 -> 7; matrix products, arithmetic and copies ran while one was open for 0% -> 0% of each run, Pallas kernels for 0% -> 0%
where the time goes in v7:
time: 108 us; the launch traced here: 107 us
  starting transfers between devices  46.8 us (43%)
  blocking collectives  33.1 us (31%)
  waiting for transfers between devices  15.5 us (14%)
  Pallas kernels  5.12 us (5%)
  other arithmetic  4.05 us (4%)
  between operations  2.2 us (2%)
    all_to_all x1, blocking collectives, exchange(): lax.all_to_all(array, MESH_AXES, 0, 0, axis_index_groups=groups, tiled=True)  33.1 us
    ppermute x1, starting transfers between devices, local(): lax.ppermute(jnp.where(image_core, text_embed, image_embed), 'core', swap)  8.79 us
    ppermute x3, starting transfers between devices, local(): down = lax.ppermute(down, MESH_AXES, ring(sizes, -1))  8.78 us
    ppermute x1, starting transfers between devices, local(): other_first = lax.ppermute(mine_first, 'core', swap)  7.85 us
    ppermute x3, starting transfers between devices, local(): up = lax.ppermute(up, MESH_AXES, ring(sizes, 1))  7.73 us
    ppermute x1, starting transfers between devices, local(): pieces.append(lax.ppermute(down[chip_rows:], MESH_AXES, ring(sizes, -1)))  5.1 us
    ppermute x1, waiting for transfers between devices, local(): pieces.append(lax.ppermute(up[:chip_rows], MESH_AXES, ring(sizes, 1)))  5.01 us
    ppermute x1, waiting for transfers between devices, local(): beside = lax.ppermute(chip, ('x', 'core'), x_pairs(sizes[1]))  4.77 us
  transfers between devices with their start and end apart: 13, of which 7 were waited for; matrix products, arithmetic and copies ran while one was open for 0% of the time, Pallas kernels for 0%

profile of v7, /device:TPU:1, one launch (start us, length us, event | category | flops | bytes accessed | tf_op | source)
XLA Modules:
  0.0 106.9 jit_solution(10269245309307663596)
XLA Ops:
  0.6 0.8 broadcast_select_fusion.4
  1.5 8.8 %collective-permute-start = (bf16[24,1152]{1,0:T(8,128)(2,1)S(1)}, bf16[24,1152]{1,0:T(8,128)(2,1)S(1)}, u32[]{:S(2)}, u32[]{:S(2)}) collective-permute-start(bf16[24,1152]{1,0:T(8,128)(2,1)S(1)} %broadcast_select_fusion.4), channel_id=1, source_target_pairs={{0,16},{16,0},{1,17},{17,1},{2,18},{18,2},{3,19},{19,3},{4,20},{20... | collective-permute-start | bytes 165896 | tf_op jit(solution)/shard_map/ppermute | solution.py:156
  10.3 0.9 collective-permute-done
  11.1 0.8 constant_dynamic-update-slice_fusion.6
  12.0 0.9 constant_dynamic-update-slice_fusion.5
  12.9 1.9 %collective-permute-start.1 = (bf16[48,1152]{1,0:T(8,128)(2,1)S(1)}, bf16[48,1152]{1,0:T(8,128)(2,1)S(1)}, u32[]{:S(2)}, u32[]{:S(2)}) collective-permute-start(bf16[48,1152]{1,0:T(8,128)(2,1)S(1)} %pad_maximum_fusion.1), channel_id=1, source_target_pairs={{0,32},{16,112},{32,0},{48,80},{64,96},{80,48},{96,64},{112,16},{1... | collective-permute-start | bytes 331784 | tf_op jit(solution)/shard_map/ppermute | solution.py:160
  14.8 4.8 %collective-permute-done.1 = bf16[48,1152]{1,0:T(8,128)(2,1)S(1)} collective-permute-done((bf16[48,1152]{1,0:T(8,128)(2,1)S(1)}, bf16[48,1152]{1,0:T(8,128)(2,1)S(1)}, u32[]{:S(2)}, u32[]{:S(2)}) %collective-permute-start.1) | collective-permute-done | bytes 110624 | tf_op jit(solution)/shard_map/ppermute | solution.py:160
  19.6 1.9 %collective-permute-start.3 = (bf16[96,1152]{1,0:T(8,128)(2,1)S(1)}, bf16[96,1152]{1,0:T(8,128)(2,1)S(1)}, u32[]{:S(2)}, u32[]{:S(2)}) collective-permute-start(bf16[96,1152]{1,0:T(8,128)(2,1)S(1)} %pad_maximum_fusion), channel_id=1, source_target_pairs={{0,385},{2,387},{4,389},{6,391},{8,393},{10,395},{12,397},{14,399}... | collective-permute-start | bytes 663560 | tf_op jit(solution)/shard_map/ppermute | solution.py:167
  21.5 3.4 %collective-permute-start.2 = (bf16[96,1152]{1,0:T(8,128)(2,1)S(1)}, bf16[96,1152]{1,0:T(8,128)(2,1)S(1)}, u32[]{:S(2)}, u32[]{:S(2)}) collective-permute-start(bf16[96,1152]{1,0:T(8,128)(2,1)S(1)} %pad_maximum_fusion), channel_id=1, source_target_pairs={{0,1},{2,3},{4,5},{6,7},{8,9},{10,11},{12,13},{14,15},{32,33},{34,... | collective-permute-start | bytes 663560 | tf_op jit(solution)/shard_map/ppermute | solution.py:166
  24.9 1.7 %collective-permute-done.3 = bf16[96,1152]{1,0:T(8,128)(2,1)S(1)} collective-permute-done((bf16[96,1152]{1,0:T(8,128)(2,1)S(1)}, bf16[96,1152]{1,0:T(8,128)(2,1)S(1)}, u32[]{:S(2)}, u32[]{:S(2)}) %collective-permute-start.3) | collective-permute-done | bytes 221216 | tf_op jit(solution)/shard_map/ppermute | solution.py:167
  26.6 2.8 %collective-permute-start.5 = (bf16[96,1152]{1,0:T(8,128)(2,1)S(1)}, bf16[96,1152]{1,0:T(8,128)(2,1)S(1)}, u32[]{:S(2)}, u32[]{:S(2)}) collective-permute-start(bf16[96,1152]{1,0:T(8,128)(2,1)S(1)} %collective-permute-done.3), channel_id=1, source_target_pairs={{0,385},{2,387},{4,389},{6,391},{8,393},{10,395},{12,397},{14,399}... | collective-permute-start | bytes 663560 | tf_op jit(solution)/shard_map/ppermute | solution.py:167
  29.4 0.0 collective-permute-done.2
  29.4 2.4 %collective-permute-start.4 = (bf16[96,1152]{1,0:T(8,128)(2,1)S(1)}, bf16[96,1152]{1,0:T(8,128)(2,1)S(1)}, u32[]{:S(2)}, u32[]{:S(2)}) collective-permute-start(bf16[96,1152]{1,0:T(8,128)(2,1)S(1)} %collective-permute-done.2), channel_id=1, source_target_pairs={{0,1},{2,3},{4,5},{6,7},{8,9},{10,11},{12,13},{14,15},{32,33},{34,... | collective-permute-start | bytes 663560 | tf_op jit(solution)/shard_map/ppermute | solution.py:166
  31.9 1.6 %collective-permute-done.5 = bf16[96,1152]{1,0:T(8,128)(2,1)S(1)} collective-permute-done((bf16[96,1152]{1,0:T(8,128)(2,1)S(1)}, bf16[96,1152]{1,0:T(8,128)(2,1)S(1)}, u32[]{:S(2)}, u32[]{:S(2)}) %collective-permute-start.5) | collective-permute-done | bytes 221216 | tf_op jit(solution)/shard_map/ppermute | solution.py:167
  33.5 4.0 %collective-permute-start.7 = (bf16[96,1152]{1,0:T(8,128)(2,1)S(1)}, bf16[96,1152]{1,0:T(8,128)(2,1)S(1)}, u32[]{:S(2)}, u32[]{:S(2)}) collective-permute-start(bf16[96,1152]{1,0:T(8,128)(2,1)S(1)} %collective-permute-done.5), channel_id=1, source_target_pairs={{0,385},{2,387},{4,389},{6,391},{8,393},{10,395},{12,397},{14,399}... | collective-permute-start | bytes 663560 | tf_op jit(solution)/shard_map/ppermute | solution.py:167
  37.6 1.9 %collective-permute-start.6 = (bf16[96,1152]{1,0:T(8,128)(2,1)S(1)}, bf16[96,1152]{1,0:T(8,128)(2,1)S(1)}, u32[]{:S(2)}, u32[]{:S(2)}) collective-permute-start(bf16[96,1152]{1,0:T(8,128)(2,1)S(1)} %collective-permute-done.4), channel_id=1, source_target_pairs={{0,1},{2,3},{4,5},{6,7},{8,9},{10,11},{12,13},{14,15},{32,33},{34,... | collective-permute-start | bytes 663560 | tf_op jit(solution)/shard_map/ppermute | solution.py:166
  39.6 7.9 %collective-permute-start.10 = (bf16[480,1152]{1,0:T(8,128)(2,1)S(1)}, bf16[480,1152]{1,0:T(8,128)(2,1)S(1)}, u32[]{:S(2)}, u32[]{:S(2)}) collective-permute-start(bf16[480,1152]{1,0:T(8,128)(2,1)S(1)} %constant_dynamic-update-slice_fusion.refs_2_), channel_id=1, source_target_pairs={{0,16},{16,0},{1,17},{17,1},{2,18},{18,2},{3,19},{19,3},{4,20},{20... | collective-permute-start | bytes 3317768 | tf_op jit(solution)/shard_map/ppermute | solution.py:177
  47.5 5.1 %collective-permute-start.9 = (bf16[48,1152]{1,0:T(8,128)(2,1)S(1)}, bf16[48,1152]{1,0:T(8,128)(2,1)S(1)}, u32[]{:S(2)}, u32[]{:S(2)}) collective-permute-start(bf16[48,1152]{1,0:T(8,128)(2,1)S(1)} %slice.9), channel_id=1, source_target_pairs={{0,385},{2,387},{4,389},{6,391},{8,393},{10,395},{12,397},{14,399}... | collective-permute-start | bytes 331784 | tf_op jit(solution)/shard_map/ppermute | solution.py:172
  52.6 1.9 %collective-permute-start.8 = (bf16[48,1152]{1,0:T(8,128)(2,1)S(1)}, bf16[48,1152]{1,0:T(8,128)(2,1)S(1)}, u32[]{:S(2)}, u32[]{:S(2)}) collective-permute-start(bf16[48,1152]{1,0:T(8,128)(2,1)S(1)} %slice.8), channel_id=1, source_target_pairs={{0,1},{2,3},{4,5},{6,7},{8,9},{10,11},{12,13},{14,15},{32,33},{34,... | collective-permute-start | bytes 331784 | tf_op jit(solution)/shard_map/ppermute | solution.py:171
  54.6 5.0 %collective-permute-done.8 = bf16[48,1152]{1,0:T(8,128)(2,1)S(1)} collective-permute-done((bf16[48,1152]{1,0:T(8,128)(2,1)S(1)}, bf16[48,1152]{1,0:T(8,128)(2,1)S(1)}, u32[]{:S(2)}, u32[]{:S(2)}) %collective-permute-start.8) | collective-permute-done | bytes 110624 | tf_op jit(solution)/shard_map/ppermute | solution.py:171
  59.6 2.8 %collective-permute-start.11 = (bf16[288,1152]{1,0:T(8,128)(2,1)S(1)}, bf16[288,1152]{1,0:T(8,128)(2,1)S(1)}, u32[]{:S(2)}, u32[]{:S(2)}) collective-permute-start(bf16[288,1152]{1,0:T(8,128)(2,1)S(1)} %constant_dynamic-update-slice_fusion.7.refs_3_), channel_id=1, source_target_pairs={{0,16},{16,0},{1,17},{17,1},{2,18},{18,2},{3,19},{19,3},{4,20},{20... | collective-permute-start | bytes 1990664 | tf_op jit(solution)/shard_map/ppermute | solution.py:178
  63.8 0.1 pad_maximum_fusion.2.refs_1_
  63.9 0.1 pad_add_fusion.refs_0_
  63.9 0.2 collective-permute-done.11.refs_5_
  64.2 4.8 %block.1 = f32[32,8,3584]{2,1,0:T(8,128)S(1)} custom-call(s32[2]{0:T(128)S(1)} %pad_add_fusion.refs_0_, f32[2]{0:T(128)S(1)} %pad_maximum_fusion.2.refs_1_, bf16[480,1152]{1,0:T(8,128)(2,1)S(1)} %constant_dynamic-update-slice_fusion.refs_2_, bf16[288,1152]{1,0:T(8,128)(2,1)S(1)} %constant_dynamic-update-slice_fusion.7.refs_3_, ...), custom_call_target="tpu_custom_call" | custom-call | flops 2717908992 | bytes 7077888 | tf_op jit(solution)/shard_map/block/pallas_call | solution.py:189
  68.9 0.2 convert_element_type.6
  69.1 33.1 %all_to_all.5 = f16[32,8,3584]{2,1,0:T(8,128)(2,1)S(1)} all-to-all(f16[32,8,3584]{2,1,0:T(8,128)(2,1)S(1)} %convert_element_type.6), channel_id=1, replica_groups={{0,1,128,129,256,257,384,385,32,33,160,161,288,289,416,417},{2,3,130,13..., dimensions={0} | all-to-all | bytes 3670016 | tf_op jit(solution)/shard_map/all_to_all | solution.py:151
  102.2 0.4 convert_element_type.7.packed_ref
  102.7 0.4 sum_parts.1
  103.0 1.9 %collective-permute-start.12 = (f32[24,1152]{1,0:T(8,128)S(1)}, f32[24,1152]{1,0:T(8,128)S(1)}, u32[]{:S(2)}, u32[]{:S(2)}) collective-permute-start(f32[24,1152]{1,0:T(8,128)S(1)} %get-tuple-element.5), channel_id=1, source_target_pairs={{0,16},{16,0},{1,17},{17,1},{2,18},{18,2},{3,19},{19,3},{4,20},{20... | collective-permute-start | bytes 331784 | tf_op jit(solution)/shard_map/ppermute | solution.py:221
  105.0 1.3 %collective-permute-done.12 = f32[24,1152]{1,0:T(8,128)S(1)} collective-permute-done((f32[24,1152]{1,0:T(8,128)S(1)}, f32[24,1152]{1,0:T(8,128)S(1)}, u32[]{:S(2)}, u32[]{:S(2)}) %collective-permute-start.12) | collective-permute-done | bytes 110624 | tf_op jit(solution)/shard_map/ppermute | solution.py:221
  106.2 0.7 broadcast_select_fusion
  (18 shorter events, 0.3 us)
Async XLA Ops:
  1.5 9.7 %collective-permute-start = (bf16[24,1152]{1,0:T(8,128)(2,1)S(1)}, bf16[24,1152]{1,0:T(8,128)(2,1)S(1)}, u32[]{:S(2)}, u32[]{:S(2)}) collective-permute-start(bf16[24,1152]{1,0:T(8,128)(2,1)S(1)} %broadcast_select_fusion.4), channel_id=1, source_target_pairs={{0,16},{16,0},{1,17},{17,1},{2,18},{18,2},{3,19},{19,3},{4,20},{20... | collective-permute-start | bytes 165896 | tf_op jit(solution)/shard_map/ppermute | solution.py:156
  12.9 6.7 %collective-permute-start.1 = (bf16[48,1152]{1,0:T(8,128)(2,1)S(1)}, bf16[48,1152]{1,0:T(8,128)(2,1)S(1)}, u32[]{:S(2)}, u32[]{:S(2)}) collective-permute-start(bf16[48,1152]{1,0:T(8,128)(2,1)S(1)} %pad_maximum_fusion.1), channel_id=1, source_target_pairs={{0,32},{16,112},{32,0},{48,80},{64,96},{80,48},{96,64},{112,16},{1... | collective-permute-start | bytes 331784 | tf_op jit(solution)/shard_map/ppermute | solution.py:160
  19.6 7.0 %collective-permute-start.3 = (bf16[96,1152]{1,0:T(8,128)(2,1)S(1)}, bf16[96,1152]{1,0:T(8,128)(2,1)S(1)}, u32[]{:S(2)}, u32[]{:S(2)}) collective-permute-start(bf16[96,1152]{1,0:T(8,128)(2,1)S(1)} %pad_maximum_fusion), channel_id=1, source_target_pairs={{0,385},{2,387},{4,389},{6,391},{8,393},{10,395},{12,397},{14,399}... | collective-permute-start | bytes 663560 | tf_op jit(solution)/shard_map/ppermute | solution.py:167
  21.5 7.9 %collective-permute-start.2 = (bf16[96,1152]{1,0:T(8,128)(2,1)S(1)}, bf16[96,1152]{1,0:T(8,128)(2,1)S(1)}, u32[]{:S(2)}, u32[]{:S(2)}) collective-permute-start(bf16[96,1152]{1,0:T(8,128)(2,1)S(1)} %pad_maximum_fusion), channel_id=1, source_target_pairs={{0,1},{2,3},{4,5},{6,7},{8,9},{10,11},{12,13},{14,15},{32,33},{34,... | collective-permute-start | bytes 663560 | tf_op jit(solution)/shard_map/ppermute | solution.py:166
  26.6 7.0 %collective-permute-start.5 = (bf16[96,1152]{1,0:T(8,128)(2,1)S(1)}, bf16[96,1152]{1,0:T(8,128)(2,1)S(1)}, u32[]{:S(2)}, u32[]{:S(2)}) collective-permute-start(bf16[96,1152]{1,0:T(8,128)(2,1)S(1)} %collective-permute-done.3), channel_id=1, source_target_pairs={{0,385},{2,387},{4,389},{6,391},{8,393},{10,395},{12,397},{14,399}... | collective-permute-start | bytes 663560 | tf_op jit(solution)/shard_map/ppermute | solution.py:167
  29.4 8.2 %collective-permute-start.4 = (bf16[96,1152]{1,0:T(8,128)(2,1)S(1)}, bf16[96,1152]{1,0:T(8,128)(2,1)S(1)}, u32[]{:S(2)}, u32[]{:S(2)}) collective-permute-start(bf16[96,1152]{1,0:T(8,128)(2,1)S(1)} %collective-permute-done.2), channel_id=1, source_target_pairs={{0,1},{2,3},{4,5},{6,7},{8,9},{10,11},{12,13},{14,15},{32,33},{34,... | collective-permute-start | bytes 663560 | tf_op jit(solution)/shard_map/ppermute | solution.py:166
  33.5 13.9 %collective-permute-start.7 = (bf16[96,1152]{1,0:T(8,128)(2,1)S(1)}, bf16[96,1152]{1,0:T(8,128)(2,1)S(1)}, u32[]{:S(2)}, u32[]{:S(2)}) collective-permute-start(bf16[96,1152]{1,0:T(8,128)(2,1)S(1)} %collective-permute-done.5), channel_id=1, source_target_pairs={{0,385},{2,387},{4,389},{6,391},{8,393},{10,395},{12,397},{14,399}... | collective-permute-start | bytes 663560 | tf_op jit(solution)/shard_map/ppermute | solution.py:167
  37.6 15.0 %collective-permute-start.6 = (bf16[96,1152]{1,0:T(8,128)(2,1)S(1)}, bf16[96,1152]{1,0:T(8,128)(2,1)S(1)}, u32[]{:S(2)}, u32[]{:S(2)}) collective-permute-start(bf16[96,1152]{1,0:T(8,128)(2,1)S(1)} %collective-permute-done.4), channel_id=1, source_target_pairs={{0,1},{2,3},{4,5},{6,7},{8,9},{10,11},{12,13},{14,15},{32,33},{34,... | collective-permute-start | bytes 663560 | tf_op jit(solution)/shard_map/ppermute | solution.py:166
  39.6 24.6 %collective-permute-start.10 = (bf16[480,1152]{1,0:T(8,128)(2,1)S(1)}, bf16[480,1152]{1,0:T(8,128)(2,1)S(1)}, u32[]{:S(2)}, u32[]{:S(2)}) collective-permute-start(bf16[480,1152]{1,0:T(8,128)(2,1)S(1)} %constant_dynamic-update-slice_fusion.refs_2_), channel_id=1, source_target_pairs={{0,16},{16,0},{1,17},{17,1},{2,18},{18,2},{3,19},{19,3},{4,20},{20... | collective-permute-start | bytes 3317768 | tf_op jit(solution)/shard_map/ppermute | solution.py:177
  47.5 12.2 %collective-permute-start.9 = (bf16[48,1152]{1,0:T(8,128)(2,1)S(1)}, bf16[48,1152]{1,0:T(8,128)(2,1)S(1)}, u32[]{:S(2)}, u32[]{:S(2)}) collective-permute-start(bf16[48,1152]{1,0:T(8,128)(2,1)S(1)} %slice.9), channel_id=1, source_target_pairs={{0,385},{2,387},{4,389},{6,391},{8,393},{10,395},{12,397},{14,399}... | collective-permute-start | bytes 331784 | tf_op jit(solution)/shard_map/ppermute | solution.py:172
  52.6 7.0 %collective-permute-start.8 = (bf16[48,1152]{1,0:T(8,128)(2,1)S(1)}, bf16[48,1152]{1,0:T(8,128)(2,1)S(1)}, u32[]{:S(2)}, u32[]{:S(2)}) collective-permute-start(bf16[48,1152]{1,0:T(8,128)(2,1)S(1)} %slice.8), channel_id=1, source_target_pairs={{0,1},{2,3},{4,5},{6,7},{8,9},{10,11},{12,13},{14,15},{32,33},{34,... | collective-permute-start | bytes 331784 | tf_op jit(solution)/shard_map/ppermute | solution.py:171
  59.6 4.5 %collective-permute-start.11 = (bf16[288,1152]{1,0:T(8,128)(2,1)S(1)}, bf16[288,1152]{1,0:T(8,128)(2,1)S(1)}, u32[]{:S(2)}, u32[]{:S(2)}) collective-permute-start(bf16[288,1152]{1,0:T(8,128)(2,1)S(1)} %constant_dynamic-update-slice_fusion.7.refs_3_), channel_id=1, source_target_pairs={{0,16},{16,0},{1,17},{17,1},{2,18},{18,2},{3,19},{19,3},{4,20},{20... | collective-permute-start | bytes 1990664 | tf_op jit(solution)/shard_map/ppermute | solution.py:178
  103.0 3.2 %collective-permute-start.12 = (f32[24,1152]{1,0:T(8,128)S(1)}, f32[24,1152]{1,0:T(8,128)S(1)}, u32[]{:S(2)}, u32[]{:S(2)}) collective-permute-start(f32[24,1152]{1,0:T(8,128)S(1)} %get-tuple-element.5), channel_id=1, source_target_pairs={{0,16},{16,0},{1,17},{17,1},{2,18},{18,2},{3,19},{19,3},{4,20},{20... | collective-permute-start | bytes 331784 | tf_op jit(solution)/shard_map/ppermute | solution.py:221

commit v8 on v6

--- a/solution.py
+++ b/solution.py
@@ -32,13 +32,15 @@
     return groups
 
 
-def weights_of(mine, other, scale_value, bias_value, same=None):
-    products = lax.dot_general(
+def products_of(mine, other):
+    return lax.dot_general(
         mine, other, (((1,), (1,)), ((), ())), preferred_element_type=jnp.float32
     )
+
+
+def weights_of(products, scale_value, bias_value, pair):
+    same = lax.broadcasted_iota(jnp.int32, products.shape, 1) == pair
     exponent = products * (-LOG2_E * scale_value) + (-LOG2_E * bias_value)
-    if same is None:
-        return (scale_value / (1.0 + jnp.exp2(exponent))).astype(jnp.bfloat16)
     magnitude = scale_value / (1.0 + jnp.exp2(jnp.where(same, -exponent, exponent)))
     return jnp.where(same, -magnitude, magnitude).astype(jnp.bfloat16)
 
@@ -57,40 +59,42 @@
     packed_ref[block, :, rows // FOLD * width :] = tail
 
 
-def block_kernel(chip_rows, place_ref, numbers_ref, mine_ref, other_ref, packed_ref, total_ref):
+def block_kernel(place_ref, numbers_ref, mine_ref, other_ref, packed_ref, total_ref):
     rows = mine_ref.shape[0]
     scale_value, bias_value = numbers_ref[0], numbers_ref[1]
+    places = packed_ref.shape[0]
+    chip_rows = rows // places
     other = other_ref[...]
-    step = rows // 3
-    for start in range(0, rows, step):
-        part = pl.ds(start, step)
-        weight = weights_of(mine_ref[part, :], other, scale_value, bias_value)
-        total_ref[part, :] = jnp.dot(weight, other, preferred_element_type=jnp.float32)
-
-    shape = (chip_rows, other.shape[0])
-    band = pl.ds(pl.multiple_of(place_ref[0] * chip_rows, 16), chip_rows)
-    row = lax.broadcasted_iota(jnp.int32, shape, 0)
-    column = lax.broadcasted_iota(jnp.int32, shape, 1) - place_ref[1] * chip_rows
-    weight = weights_of(mine_ref[band, :], other, scale_value, bias_value, row == column)
-    total_ref[band, :] = jnp.dot(weight, other, preferred_element_type=jnp.float32)
-
-    blocks = packed_ref.shape[0]
-    block_rows = rows // blocks
-    for block in range(blocks):
-        pack_into(packed_ref, block, total_ref[pl.ds(block * block_rows, block_rows), :])
+    step = rows // 2
+    halves = (0, step)
+    products = [products_of(mine_ref[pl.ds(start, step), :], other) for start in halves]
+    for start, product in zip(halves, products):
+        row = lax.broadcasted_iota(jnp.int32, (step, 1), 0) + start - place_ref[0] * chip_rows
+        own = (row >= 0) & (row < chip_rows)
+        pair = jnp.where(own, row + place_ref[1] * chip_rows, -1)
+        weight = weights_of(product, scale_value, bias_value, pair)
+        total_ref[pl.ds(start, step), :] = jnp.dot(
+            weight, other, preferred_element_type=jnp.float32
+        )
+    for place in range(places):
+        pack_into(packed_ref, place, total_ref[pl.ds(place * chip_rows, chip_rows), :])
 
 
 def sum_kernel(core_ref, packed_ref, own_ref, sent_ref):
     rows, width = own_ref.shape
     folds = rows // FOLD
-    for out_ref, core in ((own_ref, core_ref[0]), (sent_ref, 1 - core_ref[0])):
-        for k in range(folds):
-            total = jnp.zeros((FOLD, width), jnp.float32)
-            for place in range(packed_ref.shape[0] // 2):
-                block = 2 * place + core
-                factor = jnp.exp2(packed_ref[block, :, folds * width :] - 13.0)[:, k : k + 1]
-                total = total + packed_ref[block, :, k * width : (k + 1) * width] * factor
-            out_ref[pl.ds(k * FOLD, FOLD), :] = total
+    totals = []
+    for k in range(2 * folds):
+        total = jnp.zeros((FOLD, width), jnp.float32)
+        for place in range(packed_ref.shape[0]):
+            factor = jnp.exp2(packed_ref[place, :, 2 * folds * width :] - 13.0)[:, k : k + 1]
+            total = total + packed_ref[place, :, k * width : (k + 1) * width] * factor
+        totals.append(total)
+    first = core_ref[0] == 0
+    for k in range(folds):
+        part = pl.ds(k * FOLD, FOLD)
+        own_ref[part, :] = jnp.where(first, totals[k], totals[folds + k])
+        sent_ref[part, :] = jnp.where(first, totals[folds + k], totals[k])
 
 
 def local(image_embed, text_embed, logit_scale, logit_bias):
@@ -128,10 +132,10 @@
     vmem = pl.BlockSpec(memory_space=pltpu.VMEM)
     params = pltpu.CompilerParams(vmem_limit_bytes=24 * 2**20)
     rows = mine.shape[0]
-    width = row_count // FOLD * feature_count + LANES
+    width = 2 * row_count // FOLD * feature_count + LANES
     packed = pl.pallas_call(
-        lambda *refs: block_kernel(2 * row_count, *refs),
-        out_shape=jax.ShapeDtypeStruct((2 * places, FOLD, width), jnp.float32),
+        block_kernel,
+        out_shape=jax.ShapeDtypeStruct((places, FOLD, width), jnp.float32),
         in_specs=[smem, smem, vmem, vmem],
         out_specs=vmem,
         scratch_shapes=[pltpu.VMEM((rows, feature_count), jnp.float32)],

time: 92.4 us -> 90.8 us (0.983)
  Pallas kernels: 5.66 us -> 4.5 us
    pallas_call x1, Pallas kernels: 5.31 us -> 4.18 us  [local(): pl.pallas_call(block_kernel, out_shape=jax.ShapeDtypeStruct((places, FOLD...]
where the time goes in v8:
time: 90.8 us; the launch traced here: 90.4 us
  blocking collectives  60.1 us (66%)
  starting transfers between devices  16.8 us (19%)
  Pallas kernels  4.5 us (5%)
  waiting for transfers between devices  3.98 us (4%)
  other arithmetic  2.95 us (3%)
  between operations  2.03 us (2%)
    all_to_all x2, blocking collectives, exchange(): lax.all_to_all(array, MESH_AXES, 0, 0, axis_index_groups=groups, tiled=True)  60.1 us
    ppermute x1, starting transfers between devices, local(): lax.ppermute(jnp.where(image_core, text_embed, image_embed), 'core', swap)  8.79 us
    ppermute x1, starting transfers between devices, local(): other = lax.ppermute(mine, 'core', swap)  6.06 us
    pallas_call x1, Pallas kernels, local(): pl.pallas_call(block_kernel, out_shape=jax.ShapeDtypeStruct((places, FOLD...  4.18 us
    ppermute x1, starting transfers between devices, local(): sibling = lax.ppermute(sent, 'core', swap)  1.92 us
    ppermute x1, waiting for transfers between devices, local(): other = lax.ppermute(mine, 'core', swap)  1.83 us
  transfers between devices with their start and end apart: 3, of which 3 were waited for; matrix products, arithmetic and copies ran while one was open for 0% of the time, Pallas kernels for 0%

profile of v8, /device:TPU:1, one launch (start us, length us, event | category | flops | bytes accessed | tf_op | source)
XLA Modules:
  0.0 90.4 jit_solution(14515262689080363844)
XLA Ops:
  0.6 0.8 broadcast_select_fusion.4
  1.5 8.8 %collective-permute-start = (bf16[24,1152]{1,0:T(8,128)(2,1)S(1)}, bf16[24,1152]{1,0:T(8,128)(2,1)S(1)}, u32[]{:S(2)}, u32[]{:S(2)}) collective-permute-start(bf16[24,1152]{1,0:T(8,128)(2,1)S(1)} %broadcast_select_fusion.4), channel_id=1, source_target_pairs={{0,16},{16,0},{1,17},{17,1},{2,18},{18,2},{3,19},{19,3},{4,20},{20... | collective-permute-start | bytes 165896 | tf_op jit(solution)/shard_map/ppermute | solution.py:115
  10.3 0.9 collective-permute-done
  11.1 0.8 broadcast_select_fusion.3
  12.0 0.1 broadcast_in_dim.10
  12.1 27.3 %all_to_all.10 = bf16[16,48,1152]{2,1,0:T(8,128)(2,1)S(1)} all-to-all(bf16[16,48,1152]{2,1,0:T(8,128)(2,1)S(1)} %broadcast_in_dim.10), channel_id=1, replica_groups={{0,1,128,129,256,257,384,385,32,33,160,161,288,289,416,417},{2,3,130,13..., dimensions={0} | all-to-all | bytes 3538944 | tf_op jit(solution)/shard_map/all_to_all | solution.py:110
  39.5 6.1 %collective-permute-start.1 = (bf16[768,1152]{1,0:T(8,128)(2,1)S(1)}, bf16[768,1152]{1,0:T(8,128)(2,1)S(1)}, u32[]{:S(2)}, u32[]{:S(2)}) collective-permute-start(bf16[768,1152]{1,0:T(8,128)(2,1)S(1)} %bitcast.4), channel_id=1, source_target_pairs={{0,16},{16,0},{1,17},{17,1},{2,18},{18,2},{3,19},{19,3},{4,20},{20... | collective-permute-start | bytes 5308424 | tf_op jit(solution)/shard_map/ppermute | solution.py:121
  46.8 0.1 pad_maximum_fusion.1.numbers_ref
  46.9 0.1 broadcast_select_fusion.6.place_ref
  47.0 1.8 %collective-permute-done.1.other_ref = bf16[768,1152]{1,0:T(8,128)(2,1)S(1)} collective-permute-done((bf16[768,1152]{1,0:T(8,128)(2,1)S(1)}, bf16[768,1152]{1,0:T(8,128)(2,1)S(1)}, u32[]{:S(2)}, u32[]{:S(2)}) %collective-permute-start.1) | collective-permute-done | bytes 1769504 | tf_op jit(solution)/shard_map/ppermute | solution.py:121
  48.8 4.2 %block.1 = f32[16,8,7040]{2,1,0:T(8,128)S(1)} custom-call(s32[2]{0:T(128)S(1)} %broadcast_select_fusion.6.place_ref, f32[2]{0:T(128)S(1)} %pad_maximum_fusion.1.numbers_ref, bf16[768,1152]{1,0:T(8,128)(2,1)S(1)} %bitcast.5, bf16[768,1152]{1,0:T(8,128)(2,1)S(1)} %collective-permute-done.1.other_ref), custom_call_target="tpu_custom_call" | custom-call | flops 2717908992 | bytes 7077888 | tf_op jit(solution)/shard_map/block/pallas_call | solution.py:136
  53.0 0.2 convert_element_type.6
  53.2 32.7 %all_to_all.11 = f16[16,8,7040]{2,1,0:T(8,128)(2,1)S(1)} all-to-all(f16[16,8,7040]{2,1,0:T(8,128)(2,1)S(1)} %convert_element_type.6), channel_id=1, replica_groups={{0,1,128,129,256,257,384,385,32,33,160,161,288,289,416,417},{2,3,130,13..., dimensions={0} | all-to-all | bytes 3604480 | tf_op jit(solution)/shard_map/all_to_all | solution.py:110
  85.9 0.2 convert_element_type.7.packed_ref
  86.2 0.3 sum_parts.1
  86.5 1.9 %collective-permute-start.2 = (f32[24,1152]{1,0:T(8,128)S(1)}, f32[24,1152]{1,0:T(8,128)S(1)}, u32[]{:S(2)}, u32[]{:S(2)}) collective-permute-start(f32[24,1152]{1,0:T(8,128)S(1)} %get-tuple-element.5), channel_id=1, source_target_pairs={{0,16},{16,0},{1,17},{17,1},{2,18},{18,2},{3,19},{19,3},{4,20},{20... | collective-permute-start | bytes 331784 | tf_op jit(solution)/shard_map/ppermute | solution.py:165
  88.4 1.3 %collective-permute-done.2 = f32[24,1152]{1,0:T(8,128)S(1)} collective-permute-done((f32[24,1152]{1,0:T(8,128)S(1)}, f32[24,1152]{1,0:T(8,128)S(1)}, u32[]{:S(2)}, u32[]{:S(2)}) %collective-permute-start.2) | collective-permute-done | bytes 110624 | tf_op jit(solution)/shard_map/ppermute | solution.py:165
  89.7 0.7 broadcast_select_fusion
  (1 shorter events, 0.0 us)
Async XLA Ops:
  1.5 9.7 %collective-permute-start = (bf16[24,1152]{1,0:T(8,128)(2,1)S(1)}, bf16[24,1152]{1,0:T(8,128)(2,1)S(1)}, u32[]{:S(2)}, u32[]{:S(2)}) collective-permute-start(bf16[24,1152]{1,0:T(8,128)(2,1)S(1)} %broadcast_select_fusion.4), channel_id=1, source_target_pairs={{0,16},{16,0},{1,17},{17,1},{2,18},{18,2},{3,19},{19,3},{4,20},{20... | collective-permute-start | bytes 165896 | tf_op jit(solution)/shard_map/ppermute | solution.py:115
  39.5 9.4 %collective-permute-start.1 = (bf16[768,1152]{1,0:T(8,128)(2,1)S(1)}, bf16[768,1152]{1,0:T(8,128)(2,1)S(1)}, u32[]{:S(2)}, u32[]{:S(2)}) collective-permute-start(bf16[768,1152]{1,0:T(8,128)(2,1)S(1)} %bitcast.4), channel_id=1, source_target_pairs={{0,16},{16,0},{1,17},{17,1},{2,18},{18,2},{3,19},{19,3},{4,20},{20... | collective-permute-start | bytes 5308424 | tf_op jit(solution)/shard_map/ppermute | solution.py:121
  86.5 3.2 %collective-permute-start.2 = (f32[24,1152]{1,0:T(8,128)S(1)}, f32[24,1152]{1,0:T(8,128)S(1)}, u32[]{:S(2)}, u32[]{:S(2)}) collective-permute-start(f32[24,1152]{1,0:T(8,128)S(1)} %get-tuple-element.5), channel_id=1, source_target_pairs={{0,16},{16,0},{1,17},{17,1},{2,18},{18,2},{3,19},{19,3},{4,20},{20... | collective-permute-start | bytes 331784 | tf_op jit(solution)/shard_map/ppermute | solution.py:165

commit v9 on v8

--- a/solution.py
+++ b/solution.py
@@ -16,19 +16,23 @@
     return Mesh(mesh.devices.reshape(4, 4, 2, 8, 2), MESH_AXES)
 
 
+def reversed_bits(value, count):
+    bits = count.bit_length() - 1
+    return sum(((value >> i) & 1) << (bits - 1 - i) for i in range(bits))
+
+
 def exchange_groups(sizes):
     places = np.arange(np.prod(sizes)).reshape(sizes)
-    x_count, y_count = sizes[1], sizes[3]
+    x_count = sizes[1]
+    along_z = places[:, :, 0].transpose(0, 3, 1, 2).reshape(-1, x_count, sizes[3])
+    along_y = places[:, :, 1].transpose(2, 1, 0, 3).reshape(sizes[3], x_count, -1)
     groups = []
-    for x in range(0, x_count, 2):
-        pair = [x, x + 1]
-        for y in range(y_count):
-            groups.append(places[:, pair, 0, y, :].transpose(1, 0, 2).reshape(-1).tolist())
-    for x in range(1, x_count, 2):
-        pair = [x, (x + 1) % x_count]
-        for z_hi in range(sizes[0]):
-            for z_lo in range(sizes[4]):
-                groups.append(places[z_hi, pair, 1, :, z_lo].reshape(-1).tolist())
+    for first, array in ((0, along_z), (1, along_y)):
+        length = array.shape[0]
+        array = array[[reversed_bits(i, length) for i in range(length)]]
+        for x in range(first, x_count, 2):
+            for other in range(array.shape[2]):
+                groups.append(array[:, [x, (x + 1) % x_count], other].reshape(-1).tolist())
     return groups
 
 
@@ -123,8 +127,9 @@
     numbers = jnp.concatenate([logit_scale, logit_bias])
     x, y = lax.axis_index("x"), lax.axis_index("y")
     z_count = sizes[0] * sizes[4]
-    image_place = x % 2 * z_count + lax.axis_index(("z_hi", "z_lo"))
-    text_place = (x + 1) % 2 * sizes[3] + y
+    z = lax.axis_index(("z_hi", "z_lo"))
+    image_place = reversed_bits(z, z_count) * 2 + x % 2
+    text_place = reversed_bits(y, sizes[3]) * 2 + (x + 1) % 2
     place = jnp.where(
         image_core, jnp.stack([image_place, text_place]), jnp.stack([text_place, image_place])
     )

time: 90.8 us -> 94.4 us (1.040)
  blocking collectives: 60.1 us -> 63.2 us
    all_to_all x2, blocking collectives: 60.1 us -> 63.2 us  [exchange(): lax.all_to_all(array, MESH_AXES, 0, 0, axis_index_groups=groups, tiled=True)]
where the time goes in v9:
time: 94.4 us; the launch traced here: 94 us
  blocking collectives  63.2 us (67%)
  starting transfers between devices  17.2 us (18%)
  Pallas kernels  4.5 us (5%)
  waiting for transfers between devices  3.97 us (4%)
  other arithmetic  2.95 us (3%)
  between operations  2.04 us (2%)
    all_to_all x2, blocking collectives, exchange(): lax.all_to_all(array, MESH_AXES, 0, 0, axis_index_groups=groups, tiled=True)  63.2 us
    ppermute x1, starting transfers between devices, local(): lax.ppermute(jnp.where(image_core, text_embed, image_embed), 'core', swap)  8.79 us
    ppermute x1, starting transfers between devices, local(): other = lax.ppermute(mine, 'core', swap)  6.5 us
    pallas_call x1, Pallas kernels, local(): pl.pallas_call(block_kernel, out_shape=jax.ShapeDtypeStruct((places, FOLD...  4.18 us
    ppermute x1, starting transfers between devices, local(): sibling = lax.ppermute(sent, 'core', swap)  1.92 us
  transfers between devices with their start and end apart: 3, of which 3 were waited for; matrix products, arithmetic and copies ran while one was open for 0% of the time, Pallas kernels for 0%

profile of v9, /device:TPU:1, one launch (start us, length us, event | category | flops | bytes accessed | tf_op | source)
XLA Modules:
  0.0 94.0 jit_solution(15161115887141469407)
XLA Ops:
  0.6 0.8 broadcast_select_fusion.4
  1.5 8.8 %collective-permute-start = (bf16[24,1152]{1,0:T(8,128)(2,1)S(1)}, bf16[24,1152]{1,0:T(8,128)(2,1)S(1)}, u32[]{:S(2)}, u32[]{:S(2)}) collective-permute-start(bf16[24,1152]{1,0:T(8,128)(2,1)S(1)} %broadcast_select_fusion.4), channel_id=1, source_target_pairs={{0,16},{16,0},{1,17},{17,1},{2,18},{18,2},{3,19},{19,3},{4,20},{20... | collective-permute-start | bytes 165896 | tf_op jit(solution)/shard_map/ppermute | solution.py:119
  10.3 0.9 collective-permute-done
  11.1 0.8 broadcast_select_fusion.3
  12.0 0.1 broadcast_in_dim.10
  12.1 28.8 %all_to_all.10 = bf16[16,48,1152]{2,1,0:T(8,128)(2,1)S(1)} all-to-all(bf16[16,48,1152]{2,1,0:T(8,128)(2,1)S(1)} %broadcast_in_dim.10), channel_id=1, replica_groups={{0,32,256,288,128,160,384,416,1,33,257,289,129,161,385,417},{2,34,258,2..., dimensions={0} | all-to-all | bytes 3538944 | tf_op jit(solution)/shard_map/all_to_all | solution.py:114
  41.0 6.5 %collective-permute-start.1 = (bf16[768,1152]{1,0:T(8,128)(2,1)S(1)}, bf16[768,1152]{1,0:T(8,128)(2,1)S(1)}, u32[]{:S(2)}, u32[]{:S(2)}) collective-permute-start(bf16[768,1152]{1,0:T(8,128)(2,1)S(1)} %bitcast.4), channel_id=1, source_target_pairs={{0,16},{16,0},{1,17},{17,1},{2,18},{18,2},{3,19},{19,3},{4,20},{20... | collective-permute-start | bytes 5308424 | tf_op jit(solution)/shard_map/ppermute | solution.py:125
  48.8 0.1 pad_maximum_fusion.1.numbers_ref
  48.9 0.1 broadcast_select_fusion.6.place_ref
  48.9 1.8 %collective-permute-done.1.other_ref = bf16[768,1152]{1,0:T(8,128)(2,1)S(1)} collective-permute-done((bf16[768,1152]{1,0:T(8,128)(2,1)S(1)}, bf16[768,1152]{1,0:T(8,128)(2,1)S(1)}, u32[]{:S(2)}, u32[]{:S(2)}) %collective-permute-start.1) | collective-permute-done | bytes 1769504 | tf_op jit(solution)/shard_map/ppermute | solution.py:125
  50.8 4.2 %block.1 = f32[16,8,7040]{2,1,0:T(8,128)S(1)} custom-call(s32[2]{0:T(128)S(1)} %broadcast_select_fusion.6.place_ref, f32[2]{0:T(128)S(1)} %pad_maximum_fusion.1.numbers_ref, bf16[768,1152]{1,0:T(8,128)(2,1)S(1)} %bitcast.5, bf16[768,1152]{1,0:T(8,128)(2,1)S(1)} %collective-permute-done.1.other_ref), custom_call_target="tpu_custom_call" | custom-call | flops 2717908992 | bytes 7077888 | tf_op jit(solution)/shard_map/block/pallas_call | solution.py:141
  54.9 0.2 convert_element_type.6
  55.1 34.4 %all_to_all.11 = f16[16,8,7040]{2,1,0:T(8,128)(2,1)S(1)} all-to-all(f16[16,8,7040]{2,1,0:T(8,128)(2,1)S(1)} %convert_element_type.6), channel_id=1, replica_groups={{0,32,256,288,128,160,384,416,1,33,257,289,129,161,385,417},{2,34,258,2..., dimensions={0} | all-to-all | bytes 3604480 | tf_op jit(solution)/shard_map/all_to_all | solution.py:114
  89.5 0.2 convert_element_type.7.packed_ref
  89.8 0.3 sum_parts.1
  90.1 1.9 %collective-permute-start.2 = (f32[24,1152]{1,0:T(8,128)S(1)}, f32[24,1152]{1,0:T(8,128)S(1)}, u32[]{:S(2)}, u32[]{:S(2)}) collective-permute-start(f32[24,1152]{1,0:T(8,128)S(1)} %get-tuple-element.5), channel_id=1, source_target_pairs={{0,16},{16,0},{1,17},{17,1},{2,18},{18,2},{3,19},{19,3},{4,20},{20... | collective-permute-start | bytes 331784 | tf_op jit(solution)/shard_map/ppermute | solution.py:170
  92.0 1.3 %collective-permute-done.2 = f32[24,1152]{1,0:T(8,128)S(1)} collective-permute-done((f32[24,1152]{1,0:T(8,128)S(1)}, f32[24,1152]{1,0:T(8,128)S(1)}, u32[]{:S(2)}, u32[]{:S(2)}) %collective-permute-start.2) | collective-permute-done | bytes 110624 | tf_op jit(solution)/shard_map/ppermute | solution.py:170
  93.3 0.7 broadcast_select_fusion
  (1 shorter events, 0.0 us)
Async XLA Ops:
  1.5 9.7 %collective-permute-start = (bf16[24,1152]{1,0:T(8,128)(2,1)S(1)}, bf16[24,1152]{1,0:T(8,128)(2,1)S(1)}, u32[]{:S(2)}, u32[]{:S(2)}) collective-permute-start(bf16[24,1152]{1,0:T(8,128)(2,1)S(1)} %broadcast_select_fusion.4), channel_id=1, source_target_pairs={{0,16},{16,0},{1,17},{17,1},{2,18},{18,2},{3,19},{19,3},{4,20},{20... | collective-permute-start | bytes 165896 | tf_op jit(solution)/shard_map/ppermute | solution.py:119
  41.0 9.8 %collective-permute-start.1 = (bf16[768,1152]{1,0:T(8,128)(2,1)S(1)}, bf16[768,1152]{1,0:T(8,128)(2,1)S(1)}, u32[]{:S(2)}, u32[]{:S(2)}) collective-permute-start(bf16[768,1152]{1,0:T(8,128)(2,1)S(1)} %bitcast.4), channel_id=1, source_target_pairs={{0,16},{16,0},{1,17},{17,1},{2,18},{18,2},{3,19},{19,3},{4,20},{20... | collective-permute-start | bytes 5308424 | tf_op jit(solution)/shard_map/ppermute | solution.py:125
  90.1 3.2 %collective-permute-start.2 = (f32[24,1152]{1,0:T(8,128)S(1)}, f32[24,1152]{1,0:T(8,128)S(1)}, u32[]{:S(2)}, u32[]{:S(2)}) collective-permute-start(f32[24,1152]{1,0:T(8,128)S(1)} %get-tuple-element.5), channel_id=1, source_target_pairs={{0,16},{16,0},{1,17},{17,1},{2,18},{18,2},{3,19},{19,3},{4,20},{20... | collective-permute-start | bytes 331784 | tf_op jit(solution)/shard_map/ppermute | solution.py:170

commit v10 on v9

--- a/solution.py
+++ b/solution.py
@@ -10,15 +10,11 @@
 LOG2_E = 1.4426950408889634
 LANES = 128
 FOLD = 8
+STRIDE = 3
 
 
 def finer_mesh(mesh):
     return Mesh(mesh.devices.reshape(4, 4, 2, 8, 2), MESH_AXES)
-
-
-def reversed_bits(value, count):
-    bits = count.bit_length() - 1
-    return sum(((value >> i) & 1) << (bits - 1 - i) for i in range(bits))
 
 
 def exchange_groups(sizes):
@@ -29,10 +25,10 @@
     groups = []
     for first, array in ((0, along_z), (1, along_y)):
         length = array.shape[0]
-        array = array[[reversed_bits(i, length) for i in range(length)]]
+        array = array[[STRIDE * i % length for i in range(length)]]
         for x in range(first, x_count, 2):
             for other in range(array.shape[2]):
-                groups.append(array[:, [x, (x + 1) % x_count], other].reshape(-1).tolist())
+                groups.append(array[:, [x, (x + 1) % x_count], other].T.reshape(-1).tolist())
     return groups
 
 
@@ -128,8 +124,8 @@
     x, y = lax.axis_index("x"), lax.axis_index("y")
     z_count = sizes[0] * sizes[4]
     z = lax.axis_index(("z_hi", "z_lo"))
-    image_place = reversed_bits(z, z_count) * 2 + x % 2
-    text_place = reversed_bits(y, sizes[3]) * 2 + (x + 1) % 2
+    image_place = x % 2 * z_count + STRIDE * z % z_count
+    text_place = (x + 1) % 2 * sizes[3] + STRIDE * y % sizes[3]
     place = jnp.where(
         image_core, jnp.stack([image_place, text_place]), jnp.stack([text_place, image_place])
     )

time: 94.4 us -> 91.3 us (0.967)
  blocking collectives: 63.2 us -> 61 us
    all_to_all x2, blocking collectives: 63.2 us -> 61 us  [exchange(): lax.all_to_all(array, MESH_AXES, 0, 0, axis_index_groups=groups, tiled=True)]
where the time goes in v10:
time: 91.3 us; the launch traced here: 91 us
  blocking collectives  61 us (67%)
  starting transfers between devices  16.4 us (18%)
  Pallas kernels  4.5 us (5%)
  waiting for transfers between devices  3.96 us (4%)
  other arithmetic  2.95 us (3%)
  between operations  2.04 us (2%)
    all_to_all x2, blocking collectives, exchange(): lax.all_to_all(array, MESH_AXES, 0, 0, axis_index_groups=groups, tiled=True)  61 us
    ppermute x1, starting transfers between devices, local(): lax.ppermute(jnp.where(image_core, text_embed, image_embed), 'core', swap)  8.79 us
    ppermute x1, starting transfers between devices, local(): other = lax.ppermute(mine, 'core', swap)  5.72 us
    pallas_call x1, Pallas kernels, local(): pl.pallas_call(block_kernel, out_shape=jax.ShapeDtypeStruct((places, FOLD...  4.18 us
    ppermute x1, starting transfers between devices, local(): sibling = lax.ppermute(sent, 'core', swap)  1.92 us
  transfers between devices with their start and end apart: 3, of which 3 were waited for; matrix products, arithmetic and copies ran while one was open for 0% of the time, Pallas kernels for 0%

profile of v10, /device:TPU:1, one launch (start us, length us, event | category | flops | bytes accessed | tf_op | source)
XLA Modules:
  0.0 91.0 jit_solution(5410262591793882013)
XLA Ops:
  0.6 0.8 broadcast_select_fusion.4
  1.5 8.8 %collective-permute-start = (bf16[24,1152]{1,0:T(8,128)(2,1)S(1)}, bf16[24,1152]{1,0:T(8,128)(2,1)S(1)}, u32[]{:S(2)}, u32[]{:S(2)}) collective-permute-start(bf16[24,1152]{1,0:T(8,128)(2,1)S(1)} %broadcast_select_fusion.4), channel_id=1, source_target_pairs={{0,16},{16,0},{1,17},{17,1},{2,18},{18,2},{3,19},{19,3},{4,20},{20... | collective-permute-start | bytes 165896 | tf_op jit(solution)/shard_map/ppermute | solution.py:115
  10.3 0.9 collective-permute-done
  11.1 0.8 broadcast_select_fusion.3
  12.0 0.1 broadcast_in_dim.10
  12.1 27.8 %all_to_all.10 = bf16[16,48,1152]{2,1,0:T(8,128)(2,1)S(1)} all-to-all(bf16[16,48,1152]{2,1,0:T(8,128)(2,1)S(1)} %broadcast_in_dim.10), channel_id=1, replica_groups={{0,129,384,1,256,385,128,257,32,161,416,33,288,417,160,289},{2,131,386,..., dimensions={0} | all-to-all | bytes 3538944 | tf_op jit(solution)/shard_map/all_to_all | solution.py:110
  39.9 5.7 %collective-permute-start.1 = (bf16[768,1152]{1,0:T(8,128)(2,1)S(1)}, bf16[768,1152]{1,0:T(8,128)(2,1)S(1)}, u32[]{:S(2)}, u32[]{:S(2)}) collective-permute-start(bf16[768,1152]{1,0:T(8,128)(2,1)S(1)} %bitcast.4), channel_id=1, source_target_pairs={{0,16},{16,0},{1,17},{17,1},{2,18},{18,2},{3,19},{19,3},{4,20},{20... | collective-permute-start | bytes 5308424 | tf_op jit(solution)/shard_map/ppermute | solution.py:121
  47.0 0.1 pad_maximum_fusion.1.numbers_ref
  47.0 0.1 broadcast_select_fusion.6.place_ref
  47.1 1.8 %collective-permute-done.1.other_ref = bf16[768,1152]{1,0:T(8,128)(2,1)S(1)} collective-permute-done((bf16[768,1152]{1,0:T(8,128)(2,1)S(1)}, bf16[768,1152]{1,0:T(8,128)(2,1)S(1)}, u32[]{:S(2)}, u32[]{:S(2)}) %collective-permute-start.1) | collective-permute-done | bytes 1769504 | tf_op jit(solution)/shard_map/ppermute | solution.py:121
  48.9 4.2 %block.1 = f32[16,8,7040]{2,1,0:T(8,128)S(1)} custom-call(s32[2]{0:T(128)S(1)} %broadcast_select_fusion.6.place_ref, f32[2]{0:T(128)S(1)} %pad_maximum_fusion.1.numbers_ref, bf16[768,1152]{1,0:T(8,128)(2,1)S(1)} %bitcast.5, bf16[768,1152]{1,0:T(8,128)(2,1)S(1)} %collective-permute-done.1.other_ref), custom_call_target="tpu_custom_call" | custom-call | flops 2717908992 | bytes 7077888 | tf_op jit(solution)/shard_map/block/pallas_call | solution.py:137
  53.1 0.2 convert_element_type.6
  53.3 33.2 %all_to_all.11 = f16[16,8,7040]{2,1,0:T(8,128)(2,1)S(1)} all-to-all(f16[16,8,7040]{2,1,0:T(8,128)(2,1)S(1)} %convert_element_type.6), channel_id=1, replica_groups={{0,129,384,1,256,385,128,257,32,161,416,33,288,417,160,289},{2,131,386,..., dimensions={0} | all-to-all | bytes 3604480 | tf_op jit(solution)/shard_map/all_to_all | solution.py:110
  86.5 0.2 convert_element_type.7.packed_ref
  86.7 0.3 sum_parts.1
  87.0 1.9 %collective-permute-start.2 = (f32[24,1152]{1,0:T(8,128)S(1)}, f32[24,1152]{1,0:T(8,128)S(1)}, u32[]{:S(2)}, u32[]{:S(2)}) collective-permute-start(f32[24,1152]{1,0:T(8,128)S(1)} %get-tuple-element.5), channel_id=1, source_target_pairs={{0,16},{16,0},{1,17},{17,1},{2,18},{18,2},{3,19},{19,3},{4,20},{20... | collective-permute-start | bytes 331784 | tf_op jit(solution)/shard_map/ppermute | solution.py:166
  89.0 1.3 %collective-permute-done.2 = f32[24,1152]{1,0:T(8,128)S(1)} collective-permute-done((f32[24,1152]{1,0:T(8,128)S(1)}, f32[24,1152]{1,0:T(8,128)S(1)}, u32[]{:S(2)}, u32[]{:S(2)}) %collective-permute-start.2) | collective-permute-done | bytes 110624 | tf_op jit(solution)/shard_map/ppermute | solution.py:166
  90.3 0.7 broadcast_select_fusion
  (1 shorter events, 0.0 us)
Async XLA Ops:
  1.5 9.7 %collective-permute-start = (bf16[24,1152]{1,0:T(8,128)(2,1)S(1)}, bf16[24,1152]{1,0:T(8,128)(2,1)S(1)}, u32[]{:S(2)}, u32[]{:S(2)}) collective-permute-start(bf16[24,1152]{1,0:T(8,128)(2,1)S(1)} %broadcast_select_fusion.4), channel_id=1, source_target_pairs={{0,16},{16,0},{1,17},{17,1},{2,18},{18,2},{3,19},{19,3},{4,20},{20... | collective-permute-start | bytes 165896 | tf_op jit(solution)/shard_map/ppermute | solution.py:115
  39.9 9.0 %collective-permute-start.1 = (bf16[768,1152]{1,0:T(8,128)(2,1)S(1)}, bf16[768,1152]{1,0:T(8,128)(2,1)S(1)}, u32[]{:S(2)}, u32[]{:S(2)}) collective-permute-start(bf16[768,1152]{1,0:T(8,128)(2,1)S(1)} %bitcast.4), channel_id=1, source_target_pairs={{0,16},{16,0},{1,17},{17,1},{2,18},{18,2},{3,19},{19,3},{4,20},{20... | collective-permute-start | bytes 5308424 | tf_op jit(solution)/shard_map/ppermute | solution.py:121
  87.0 3.2 %collective-permute-start.2 = (f32[24,1152]{1,0:T(8,128)S(1)}, f32[24,1152]{1,0:T(8,128)S(1)}, u32[]{:S(2)}, u32[]{:S(2)}) collective-permute-start(f32[24,1152]{1,0:T(8,128)S(1)} %get-tuple-element.5), channel_id=1, source_target_pairs={{0,16},{16,0},{1,17},{17,1},{2,18},{18,2},{3,19},{19,3},{4,20},{20... | collective-permute-start | bytes 331784 | tf_op jit(solution)/shard_map/ppermute | solution.py:166

commit v11 on v8

--- a/solution.py
+++ b/solution.py
@@ -111,8 +111,13 @@
             array, MESH_AXES, 0, 0, axis_index_groups=groups, tiled=True
         )
 
-    kept = jnp.where(image_core, image_embed, text_embed)
-    arrived = lax.ppermute(jnp.where(image_core, text_embed, image_embed), "core", swap)
+    kept, sent = lax.optimization_barrier(
+        (
+            jnp.where(image_core, image_embed, text_embed),
+            jnp.where(image_core, text_embed, image_embed),
+        )
+    )
+    arrived = lax.ppermute(sent, "core", swap)
     chip = jnp.concatenate(
         [jnp.where(image_core, kept, arrived), jnp.where(image_core, arrived, kept)], axis=0
     )

time: 90.8 us -> 89.9 us (0.990)
  no operation moved by 1% of the time
where the time goes in v11:
time: 89.9 us; the launch traced here: 89.6 us
  blocking collectives  60.1 us (67%)
  starting transfers between devices  16.8 us (19%)
  Pallas kernels  4.5 us (5%)
  waiting for transfers between devices  3.98 us (4%)
  other arithmetic  2.14 us (2%)
  between operations  2.03 us (2%)
    all_to_all x2, blocking collectives, exchange(): lax.all_to_all(array, MESH_AXES, 0, 0, axis_index_groups=groups, tiled=True)  60.1 us
    ppermute x1, starting transfers between devices, local(): arrived = lax.ppermute(sent, 'core', swap)  8.79 us
    ppermute x1, starting transfers between devices, local(): other = lax.ppermute(mine, 'core', swap)  6.06 us
    pallas_call x1, Pallas kernels, local(): pl.pallas_call(block_kernel, out_shape=jax.ShapeDtypeStruct((places, FOLD...  4.18 us
    ppermute x1, starting transfers between devices, local(): sibling = lax.ppermute(sent, 'core', swap)  1.92 us
    ppermute x1, waiting for transfers between devices, local(): other = lax.ppermute(mine, 'core', swap)  1.83 us
  transfers between devices with their start and end apart: 3, of which 3 were waited for; matrix products, arithmetic and copies ran while one was open for 0% of the time, Pallas kernels for 0%

profile of v11, /device:TPU:1, one launch (start us, length us, event | category | flops | bytes accessed | tf_op | source)
XLA Modules:
  0.0 89.6 jit_solution(16802199004673982525)
XLA Ops:
  0.6 0.9 broadcast_select_fusion.4
  1.5 8.8 %collective-permute-start = (bf16[24,1152]{1,0:T(8,128)(2,1)S(1)}, bf16[24,1152]{1,0:T(8,128)(2,1)S(1)}, u32[]{:S(2)}, u32[]{:S(2)}) collective-permute-start(bf16[24,1152]{1,0:T(8,128)(2,1)S(1)} %get-tuple-element.7), channel_id=1, source_target_pairs={{0,16},{16,0},{1,17},{17,1},{2,18},{18,2},{3,19},{19,3},{4,20},{20... | collective-permute-start | bytes 165896 | tf_op jit(solution)/shard_map/ppermute | solution.py:120
  10.3 0.9 collective-permute-done
  11.2 0.1 broadcast_in_dim.10
  11.3 27.3 %all_to_all.10 = bf16[16,48,1152]{2,1,0:T(8,128)(2,1)S(1)} all-to-all(bf16[16,48,1152]{2,1,0:T(8,128)(2,1)S(1)} %broadcast_in_dim.10), channel_id=1, replica_groups={{0,1,128,129,256,257,384,385,32,33,160,161,288,289,416,417},{2,3,130,13..., dimensions={0} | all-to-all | bytes 3538944 | tf_op jit(solution)/shard_map/all_to_all | solution.py:110
  38.7 6.1 %collective-permute-start.1 = (bf16[768,1152]{1,0:T(8,128)(2,1)S(1)}, bf16[768,1152]{1,0:T(8,128)(2,1)S(1)}, u32[]{:S(2)}, u32[]{:S(2)}) collective-permute-start(bf16[768,1152]{1,0:T(8,128)(2,1)S(1)} %bitcast.4), channel_id=1, source_target_pairs={{0,16},{16,0},{1,17},{17,1},{2,18},{18,2},{3,19},{19,3},{4,20},{20... | collective-permute-start | bytes 5308424 | tf_op jit(solution)/shard_map/ppermute | solution.py:126
  46.1 0.1 pad_maximum_fusion.1.numbers_ref
  46.1 0.1 broadcast_select_fusion.6.place_ref
  46.2 1.8 %collective-permute-done.1.other_ref = bf16[768,1152]{1,0:T(8,128)(2,1)S(1)} collective-permute-done((bf16[768,1152]{1,0:T(8,128)(2,1)S(1)}, bf16[768,1152]{1,0:T(8,128)(2,1)S(1)}, u32[]{:S(2)}, u32[]{:S(2)}) %collective-permute-start.1) | collective-permute-done | bytes 1769504 | tf_op jit(solution)/shard_map/ppermute | solution.py:126
  48.0 4.2 %block.1 = f32[16,8,7040]{2,1,0:T(8,128)S(1)} custom-call(s32[2]{0:T(128)S(1)} %broadcast_select_fusion.6.place_ref, f32[2]{0:T(128)S(1)} %pad_maximum_fusion.1.numbers_ref, bf16[768,1152]{1,0:T(8,128)(2,1)S(1)} %bitcast.5, bf16[768,1152]{1,0:T(8,128)(2,1)S(1)} %collective-permute-done.1.other_ref), custom_call_target="tpu_custom_call" | custom-call | flops 2717908992 | bytes 7077888 | tf_op jit(solution)/shard_map/block/pallas_call | solution.py:141
  52.2 0.2 convert_element_type.6
  52.4 32.7 %all_to_all.11 = f16[16,8,7040]{2,1,0:T(8,128)(2,1)S(1)} all-to-all(f16[16,8,7040]{2,1,0:T(8,128)(2,1)S(1)} %convert_element_type.6), channel_id=1, replica_groups={{0,1,128,129,256,257,384,385,32,33,160,161,288,289,416,417},{2,3,130,13..., dimensions={0} | all-to-all | bytes 3604480 | tf_op jit(solution)/shard_map/all_to_all | solution.py:110
  85.1 0.2 convert_element_type.7.packed_ref
  85.4 0.3 sum_parts.1
  85.7 1.9 %collective-permute-start.2 = (f32[24,1152]{1,0:T(8,128)S(1)}, f32[24,1152]{1,0:T(8,128)S(1)}, u32[]{:S(2)}, u32[]{:S(2)}) collective-permute-start(f32[24,1152]{1,0:T(8,128)S(1)} %get-tuple-element.9), channel_id=1, source_target_pairs={{0,16},{16,0},{1,17},{17,1},{2,18},{18,2},{3,19},{19,3},{4,20},{20... | collective-permute-start | bytes 331784 | tf_op jit(solution)/shard_map/ppermute | solution.py:170
  87.6 1.3 %collective-permute-done.2 = f32[24,1152]{1,0:T(8,128)S(1)} collective-permute-done((f32[24,1152]{1,0:T(8,128)S(1)}, f32[24,1152]{1,0:T(8,128)S(1)}, u32[]{:S(2)}, u32[]{:S(2)}) %collective-permute-start.2) | collective-permute-done | bytes 110624 | tf_op jit(solution)/shard_map/ppermute | solution.py:170
  88.9 0.7 broadcast_select_fusion
  (2 shorter events, 0.0 us)
Async XLA Ops:
  1.5 9.7 %collective-permute-start = (bf16[24,1152]{1,0:T(8,128)(2,1)S(1)}, bf16[24,1152]{1,0:T(8,128)(2,1)S(1)}, u32[]{:S(2)}, u32[]{:S(2)}) collective-permute-start(bf16[24,1152]{1,0:T(8,128)(2,1)S(1)} %get-tuple-element.7), channel_id=1, source_target_pairs={{0,16},{16,0},{1,17},{17,1},{2,18},{18,2},{3,19},{19,3},{4,20},{20... | collective-permute-start | bytes 165896 | tf_op jit(solution)/shard_map/ppermute | solution.py:120
  38.7 9.4 %collective-permute-start.1 = (bf16[768,1152]{1,0:T(8,128)(2,1)S(1)}, bf16[768,1152]{1,0:T(8,128)(2,1)S(1)}, u32[]{:S(2)}, u32[]{:S(2)}) collective-permute-start(bf16[768,1152]{1,0:T(8,128)(2,1)S(1)} %bitcast.4), channel_id=1, source_target_pairs={{0,16},{16,0},{1,17},{17,1},{2,18},{18,2},{3,19},{19,3},{4,20},{20... | collective-permute-start | bytes 5308424 | tf_op jit(solution)/shard_map/ppermute | solution.py:126
  85.7 3.2 %collective-permute-start.2 = (f32[24,1152]{1,0:T(8,128)S(1)}, f32[24,1152]{1,0:T(8,128)S(1)}, u32[]{:S(2)}, u32[]{:S(2)}) collective-permute-start(f32[24,1152]{1,0:T(8,128)S(1)} %get-tuple-element.9), channel_id=1, source_target_pairs={{0,16},{16,0},{1,17},{17,1},{2,18},{18,2},{3,19},{19,3},{4,20},{20... | collective-permute-start | bytes 331784 | tf_op jit(solution)/shard_map/ppermute | solution.py:170

commit v12 on v11

--- a/solution.py
+++ b/solution.py
@@ -59,7 +59,7 @@
     packed_ref[block, :, rows // FOLD * width :] = tail
 
 
-def block_kernel(place_ref, numbers_ref, mine_ref, other_ref, packed_ref, total_ref):
+def block_kernel(place_ref, numbers_ref, mine_ref, other_ref, packed_ref):
     rows = mine_ref.shape[0]
     scale_value, bias_value = numbers_ref[0], numbers_ref[1]
     places = packed_ref.shape[0]
@@ -73,11 +73,9 @@
         own = (row >= 0) & (row < chip_rows)
         pair = jnp.where(own, row + place_ref[1] * chip_rows, -1)
         weight = weights_of(product, scale_value, bias_value, pair)
-        total_ref[pl.ds(start, step), :] = jnp.dot(
-            weight, other, preferred_element_type=jnp.float32
-        )
-    for place in range(places):
-        pack_into(packed_ref, place, total_ref[pl.ds(place * chip_rows, chip_rows), :])
+        total = jnp.dot(weight, other, preferred_element_type=jnp.float32)
+        for at in range(0, step, chip_rows):
+            pack_into(packed_ref, (start + at) // chip_rows, total[at : at + chip_rows, :])
 
 
 def sum_kernel(core_ref, packed_ref, own_ref, sent_ref):
@@ -143,7 +141,6 @@
         out_shape=jax.ShapeDtypeStruct((places, FOLD, width), jnp.float32),
         in_specs=[smem, smem, vmem, vmem],
         out_specs=vmem,
-        scratch_shapes=[pltpu.VMEM((rows, feature_count), jnp.float32)],
         compiler_params=params,
         cost_estimate=pl.CostEstimate(
             flops=4 * rows * rows * feature_count,

time: 89.9 us -> 89.9 us (level)
  no operation moved by 1% of the time
where the time goes in v12:
time: 89.9 us; the launch traced here: 89.6 us
  blocking collectives  60.1 us (67%)
  starting transfers between devices  16.8 us (19%)
  Pallas kernels  4.5 us (5%)
  waiting for transfers between devices  3.98 us (4%)
  other arithmetic  2.14 us (2%)
  between operations  2.03 us (2%)
    all_to_all x2, blocking collectives, exchange(): lax.all_to_all(array, MESH_AXES, 0, 0, axis_index_groups=groups, tiled=True)  60.1 us
    ppermute x1, starting transfers between devices, local(): arrived = lax.ppermute(sent, 'core', swap)  8.79 us
    ppermute x1, starting transfers between devices, local(): other = lax.ppermute(mine, 'core', swap)  6.06 us
    pallas_call x1, Pallas kernels, local(): pl.pallas_call(block_kernel, out_shape=jax.ShapeDtypeStruct((places, FOLD...  4.18 us
    ppermute x1, starting transfers between devices, local(): sibling = lax.ppermute(sent, 'core', swap)  1.92 us
    ppermute x1, waiting for transfers between devices, local(): other = lax.ppermute(mine, 'core', swap)  1.83 us
  transfers between devices with their start and end apart: 3, of which 3 were waited for; matrix products, arithmetic and copies ran while one was open for 0% of the time, Pallas kernels for 0%

profile of v12, /device:TPU:1, one launch (start us, length us, event | category | flops | bytes accessed | tf_op | source)
XLA Modules:
  0.0 89.6 jit_solution(2242068067101730440)
XLA Ops:
  0.6 0.9 broadcast_select_fusion.4
  1.5 8.8 %collective-permute-start = (bf16[24,1152]{1,0:T(8,128)(2,1)S(1)}, bf16[24,1152]{1,0:T(8,128)(2,1)S(1)}, u32[]{:S(2)}, u32[]{:S(2)}) collective-permute-start(bf16[24,1152]{1,0:T(8,128)(2,1)S(1)} %get-tuple-element.7), channel_id=1, source_target_pairs={{0,16},{16,0},{1,17},{17,1},{2,18},{18,2},{3,19},{19,3},{4,20},{20... | collective-permute-start | bytes 165896 | tf_op jit(solution)/shard_map/ppermute | solution.py:118
  10.3 0.9 collective-permute-done
  11.2 0.1 broadcast_in_dim.10
  11.3 27.3 %all_to_all.10 = bf16[16,48,1152]{2,1,0:T(8,128)(2,1)S(1)} all-to-all(bf16[16,48,1152]{2,1,0:T(8,128)(2,1)S(1)} %broadcast_in_dim.10), channel_id=1, replica_groups={{0,1,128,129,256,257,384,385,32,33,160,161,288,289,416,417},{2,3,130,13..., dimensions={0} | all-to-all | bytes 3538944 | tf_op jit(solution)/shard_map/all_to_all | solution.py:108
  38.7 6.1 %collective-permute-start.1 = (bf16[768,1152]{1,0:T(8,128)(2,1)S(1)}, bf16[768,1152]{1,0:T(8,128)(2,1)S(1)}, u32[]{:S(2)}, u32[]{:S(2)}) collective-permute-start(bf16[768,1152]{1,0:T(8,128)(2,1)S(1)} %bitcast.4), channel_id=1, source_target_pairs={{0,16},{16,0},{1,17},{17,1},{2,18},{18,2},{3,19},{19,3},{4,20},{20... | collective-permute-start | bytes 5308424 | tf_op jit(solution)/shard_map/ppermute | solution.py:124
  46.1 0.1 pad_maximum_fusion.1.numbers_ref
  46.1 0.1 broadcast_select_fusion.6.place_ref
  46.2 1.8 %collective-permute-done.1.other_ref = bf16[768,1152]{1,0:T(8,128)(2,1)S(1)} collective-permute-done((bf16[768,1152]{1,0:T(8,128)(2,1)S(1)}, bf16[768,1152]{1,0:T(8,128)(2,1)S(1)}, u32[]{:S(2)}, u32[]{:S(2)}) %collective-permute-start.1) | collective-permute-done | bytes 1769504 | tf_op jit(solution)/shard_map/ppermute | solution.py:124
  48.0 4.2 %block.1 = f32[16,8,7040]{2,1,0:T(8,128)S(1)} custom-call(s32[2]{0:T(128)S(1)} %broadcast_select_fusion.6.place_ref, f32[2]{0:T(128)S(1)} %pad_maximum_fusion.1.numbers_ref, bf16[768,1152]{1,0:T(8,128)(2,1)S(1)} %bitcast.5, bf16[768,1152]{1,0:T(8,128)(2,1)S(1)} %collective-permute-done.1.other_ref), custom_call_target="tpu_custom_call" | custom-call | flops 2717908992 | bytes 7077888 | tf_op jit(solution)/shard_map/block/pallas_call | solution.py:139
  52.2 0.2 convert_element_type.6
  52.4 32.7 %all_to_all.11 = f16[16,8,7040]{2,1,0:T(8,128)(2,1)S(1)} all-to-all(f16[16,8,7040]{2,1,0:T(8,128)(2,1)S(1)} %convert_element_type.6), channel_id=1, replica_groups={{0,1,128,129,256,257,384,385,32,33,160,161,288,289,416,417},{2,3,130,13..., dimensions={0} | all-to-all | bytes 3604480 | tf_op jit(solution)/shard_map/all_to_all | solution.py:108
  85.1 0.2 convert_element_type.7.packed_ref
  85.4 0.3 sum_parts.1
  85.7 1.9 %collective-permute-start.2 = (f32[24,1152]{1,0:T(8,128)S(1)}, f32[24,1152]{1,0:T(8,128)S(1)}, u32[]{:S(2)}, u32[]{:S(2)}) collective-permute-start(f32[24,1152]{1,0:T(8,128)S(1)} %get-tuple-element.9), channel_id=1, source_target_pairs={{0,16},{16,0},{1,17},{17,1},{2,18},{18,2},{3,19},{19,3},{4,20},{20... | collective-permute-start | bytes 331784 | tf_op jit(solution)/shard_map/ppermute | solution.py:167
  87.6 1.3 %collective-permute-done.2 = f32[24,1152]{1,0:T(8,128)S(1)} collective-permute-done((f32[24,1152]{1,0:T(8,128)S(1)}, f32[24,1152]{1,0:T(8,128)S(1)}, u32[]{:S(2)}, u32[]{:S(2)}) %collective-permute-start.2) | collective-permute-done | bytes 110624 | tf_op jit(solution)/shard_map/ppermute | solution.py:167
  88.9 0.7 broadcast_select_fusion
  (2 shorter events, 0.0 us)
Async XLA Ops:
  1.5 9.7 %collective-permute-start = (bf16[24,1152]{1,0:T(8,128)(2,1)S(1)}, bf16[24,1152]{1,0:T(8,128)(2,1)S(1)}, u32[]{:S(2)}, u32[]{:S(2)}) collective-permute-start(bf16[24,1152]{1,0:T(8,128)(2,1)S(1)} %get-tuple-element.7), channel_id=1, source_target_pairs={{0,16},{16,0},{1,17},{17,1},{2,18},{18,2},{3,19},{19,3},{4,20},{20... | collective-permute-start | bytes 165896 | tf_op jit(solution)/shard_map/ppermute | solution.py:118
  38.7 9.4 %collective-permute-start.1 = (bf16[768,1152]{1,0:T(8,128)(2,1)S(1)}, bf16[768,1152]{1,0:T(8,128)(2,1)S(1)}, u32[]{:S(2)}, u32[]{:S(2)}) collective-permute-start(bf16[768,1152]{1,0:T(8,128)(2,1)S(1)} %bitcast.4), channel_id=1, source_target_pairs={{0,16},{16,0},{1,17},{17,1},{2,18},{18,2},{3,19},{19,3},{4,20},{20... | collective-permute-start | bytes 5308424 | tf_op jit(solution)/shard_map/ppermute | solution.py:124
  85.7 3.2 %collective-permute-start.2 = (f32[24,1152]{1,0:T(8,128)S(1)}, f32[24,1152]{1,0:T(8,128)S(1)}, u32[]{:S(2)}, u32[]{:S(2)}) collective-permute-start(f32[24,1152]{1,0:T(8,128)S(1)} %get-tuple-element.9), channel_id=1, source_target_pairs={{0,16},{16,0},{1,17},{17,1},{2,18},{18,2},{3,19},{19,3},{4,20},{20... | collective-permute-start | bytes 331784 | tf_op jit(solution)/shard_map/ppermute | solution.py:167

commit v13 on v11

--- a/solution.py
+++ b/solution.py
@@ -23,12 +23,12 @@
     for x in range(0, x_count, 2):
         pair = [x, x + 1]
         for y in range(y_count):
-            groups.append(places[:, pair, 0, y, :].transpose(1, 0, 2).reshape(-1).tolist())
+            groups.append(places[:, pair, 0, y, :].transpose(0, 2, 1).reshape(-1).tolist())
     for x in range(1, x_count, 2):
         pair = [x, (x + 1) % x_count]
         for z_hi in range(sizes[0]):
             for z_lo in range(sizes[4]):
-                groups.append(places[z_hi, pair, 1, :, z_lo].reshape(-1).tolist())
+                groups.append(places[z_hi, pair, 1, :, z_lo].T.reshape(-1).tolist())
     return groups
 
 
@@ -127,9 +127,8 @@
 
     numbers = jnp.concatenate([logit_scale, logit_bias])
     x, y = lax.axis_index("x"), lax.axis_index("y")
-    z_count = sizes[0] * sizes[4]
-    image_place = x % 2 * z_count + lax.axis_index(("z_hi", "z_lo"))
-    text_place = (x + 1) % 2 * sizes[3] + y
+    image_place = lax.axis_index(("z_hi", "z_lo")) * 2 + x % 2
+    text_place = y * 2 + (x + 1) % 2
     place = jnp.where(
         image_core, jnp.stack([image_place, text_place]), jnp.stack([text_place, image_place])
     )

time: 89.9 us -> 93 us (1.034)
  blocking collectives: 60.1 us -> 62.7 us
    all_to_all x2, blocking collectives: 60.1 us -> 62.7 us  [exchange(): lax.all_to_all(array, MESH_AXES, 0, 0, axis_index_groups=groups, tiled=True)]
where the time goes in v13:
time: 93 us; the launch traced here: 92.7 us
  blocking collectives  62.7 us (67%)
  starting transfers between devices  17.2 us (18%)
  Pallas kernels  4.5 us (5%)
  waiting for transfers between devices  3.98 us (4%)
  other arithmetic  2.14 us (2%)
  between operations  2.03 us (2%)
    all_to_all x2, blocking collectives, exchange(): lax.all_to_all(array, MESH_AXES, 0, 0, axis_index_groups=groups, tiled=True)  62.7 us
    ppermute x1, starting transfers between devices, local(): arrived = lax.ppermute(sent, 'core', swap)  8.79 us
    ppermute x1, starting transfers between devices, local(): other = lax.ppermute(mine, 'core', swap)  6.5 us
    pallas_call x1, Pallas kernels, local(): pl.pallas_call(block_kernel, out_shape=jax.ShapeDtypeStruct((places, FOLD...  4.19 us
    ppermute x1, starting transfers between devices, local(): sibling = lax.ppermute(sent, 'core', swap)  1.92 us
  transfers between devices with their start and end apart: 3, of which 3 were waited for; matrix products, arithmetic and copies ran while one was open for 0% of the time, Pallas kernels for 0%

profile of v13, /device:TPU:1, one launch (start us, length us, event | category | flops | bytes accessed | tf_op | source)
XLA Modules:
  0.0 92.7 jit_solution(8328825773863239918)
XLA Ops:
  0.6 0.9 broadcast_select_fusion.4
  1.5 8.8 %collective-permute-start = (bf16[24,1152]{1,0:T(8,128)(2,1)S(1)}, bf16[24,1152]{1,0:T(8,128)(2,1)S(1)}, u32[]{:S(2)}, u32[]{:S(2)}) collective-permute-start(bf16[24,1152]{1,0:T(8,128)(2,1)S(1)} %get-tuple-element.7), channel_id=1, source_target_pairs={{0,16},{16,0},{1,17},{17,1},{2,18},{18,2},{3,19},{19,3},{4,20},{20... | collective-permute-start | bytes 165896 | tf_op jit(solution)/shard_map/ppermute | solution.py:120
  10.3 0.9 collective-permute-done
  11.2 0.1 broadcast_in_dim.10
  11.3 28.6 %all_to_all.10 = bf16[16,48,1152]{2,1,0:T(8,128)(2,1)S(1)} all-to-all(bf16[16,48,1152]{2,1,0:T(8,128)(2,1)S(1)} %broadcast_in_dim.10), channel_id=1, replica_groups={{0,32,1,33,128,160,129,161,256,288,257,289,384,416,385,417},{2,34,3,35,..., dimensions={0} | all-to-all | bytes 3538944 | tf_op jit(solution)/shard_map/all_to_all | solution.py:110
  39.9 6.5 %collective-permute-start.1 = (bf16[768,1152]{1,0:T(8,128)(2,1)S(1)}, bf16[768,1152]{1,0:T(8,128)(2,1)S(1)}, u32[]{:S(2)}, u32[]{:S(2)}) collective-permute-start(bf16[768,1152]{1,0:T(8,128)(2,1)S(1)} %bitcast.4), channel_id=1, source_target_pairs={{0,16},{16,0},{1,17},{17,1},{2,18},{18,2},{3,19},{19,3},{4,20},{20... | collective-permute-start | bytes 5308424 | tf_op jit(solution)/shard_map/ppermute | solution.py:126
  47.7 0.1 pad_maximum_fusion.1.numbers_ref
  47.8 0.1 broadcast_select_fusion.6.place_ref
  47.9 1.8 %collective-permute-done.1.other_ref = bf16[768,1152]{1,0:T(8,128)(2,1)S(1)} collective-permute-done((bf16[768,1152]{1,0:T(8,128)(2,1)S(1)}, bf16[768,1152]{1,0:T(8,128)(2,1)S(1)}, u32[]{:S(2)}, u32[]{:S(2)}) %collective-permute-start.1) | collective-permute-done | bytes 1769504 | tf_op jit(solution)/shard_map/ppermute | solution.py:126
  49.7 4.2 %block.1 = f32[16,8,7040]{2,1,0:T(8,128)S(1)} custom-call(s32[2]{0:T(128)S(1)} %broadcast_select_fusion.6.place_ref, f32[2]{0:T(128)S(1)} %pad_maximum_fusion.1.numbers_ref, bf16[768,1152]{1,0:T(8,128)(2,1)S(1)} %bitcast.5, bf16[768,1152]{1,0:T(8,128)(2,1)S(1)} %collective-permute-done.1.other_ref), custom_call_target="tpu_custom_call" | custom-call | flops 2717908992 | bytes 7077888 | tf_op jit(solution)/shard_map/block/pallas_call | solution.py:140
  53.9 0.2 convert_element_type.6
  54.1 34.1 %all_to_all.11 = f16[16,8,7040]{2,1,0:T(8,128)(2,1)S(1)} all-to-all(f16[16,8,7040]{2,1,0:T(8,128)(2,1)S(1)} %convert_element_type.6), channel_id=1, replica_groups={{0,32,1,33,128,160,129,161,256,288,257,289,384,416,385,417},{2,34,3,35,..., dimensions={0} | all-to-all | bytes 3604480 | tf_op jit(solution)/shard_map/all_to_all | solution.py:110
  88.2 0.2 convert_element_type.7.packed_ref
  88.4 0.3 sum_parts.1
  88.8 1.9 %collective-permute-start.2 = (f32[24,1152]{1,0:T(8,128)S(1)}, f32[24,1152]{1,0:T(8,128)S(1)}, u32[]{:S(2)}, u32[]{:S(2)}) collective-permute-start(f32[24,1152]{1,0:T(8,128)S(1)} %get-tuple-element.9), channel_id=1, source_target_pairs={{0,16},{16,0},{1,17},{17,1},{2,18},{18,2},{3,19},{19,3},{4,20},{20... | collective-permute-start | bytes 331784 | tf_op jit(solution)/shard_map/ppermute | solution.py:169
  90.7 1.3 %collective-permute-done.2 = f32[24,1152]{1,0:T(8,128)S(1)} collective-permute-done((f32[24,1152]{1,0:T(8,128)S(1)}, f32[24,1152]{1,0:T(8,128)S(1)}, u32[]{:S(2)}, u32[]{:S(2)}) %collective-permute-start.2) | collective-permute-done | bytes 110624 | tf_op jit(solution)/shard_map/ppermute | solution.py:169
  92.0 0.7 broadcast_select_fusion
  (2 shorter events, 0.0 us)
Async XLA Ops:
  1.5 9.7 %collective-permute-start = (bf16[24,1152]{1,0:T(8,128)(2,1)S(1)}, bf16[24,1152]{1,0:T(8,128)(2,1)S(1)}, u32[]{:S(2)}, u32[]{:S(2)}) collective-permute-start(bf16[24,1152]{1,0:T(8,128)(2,1)S(1)} %get-tuple-element.7), channel_id=1, source_target_pairs={{0,16},{16,0},{1,17},{17,1},{2,18},{18,2},{3,19},{19,3},{4,20},{20... | collective-permute-start | bytes 165896 | tf_op jit(solution)/shard_map/ppermute | solution.py:120
  39.9 9.8 %collective-permute-start.1 = (bf16[768,1152]{1,0:T(8,128)(2,1)S(1)}, bf16[768,1152]{1,0:T(8,128)(2,1)S(1)}, u32[]{:S(2)}, u32[]{:S(2)}) collective-permute-start(bf16[768,1152]{1,0:T(8,128)(2,1)S(1)} %bitcast.4), channel_id=1, source_target_pairs={{0,16},{16,0},{1,17},{17,1},{2,18},{18,2},{3,19},{19,3},{4,20},{20... | collective-permute-start | bytes 5308424 | tf_op jit(solution)/shard_map/ppermute | solution.py:126
  88.8 3.2 %collective-permute-start.2 = (f32[24,1152]{1,0:T(8,128)S(1)}, f32[24,1152]{1,0:T(8,128)S(1)}, u32[]{:S(2)}, u32[]{:S(2)}) collective-permute-start(f32[24,1152]{1,0:T(8,128)S(1)} %get-tuple-element.9), channel_id=1, source_target_pairs={{0,16},{16,0},{1,17},{17,1},{2,18},{18,2},{3,19},{19,3},{4,20},{20... | collective-permute-start | bytes 331784 | tf_op jit(solution)/shard_map/ppermute | solution.py:169
